TPU v7x, 32 devices: a whole 2x2x4 slice. The times are simulated.
32 devices in a mesh: rep: 8 (over y, x, core), shard: 4 (over z).
Axes of the slice: x: 2, y: 2, z: 4, core: 2. Of those that a mesh axis runs over, the one named last changes fastest.
Arguments:
- hidden_in: bfloat16 [16, 512, 1024], P('rep', 'shard'), may hold values from -6 to 6
- segments: int32 [16, 512], P('rep'), may hold values from 0 to 3, as said below
- norm_gains: bfloat16 [2, 2, 1024], P(None, None, 'shard'), may hold values from 0.5 to 1.5
- norm_biases: bfloat16 [2, 2, 1024], P(None, None, 'shard'), may hold values from -3 to 3
- qkv_weight: bfloat16 [2, 1024, 3072], P(None, 'shard'), may hold values from -0.1875 to 0.1875
- qkv_bias: bfloat16 [2, 3072], P(None, 'shard'), may hold values from -3 to 3
- out_weight: bfloat16 [2, 1024, 1024], P(None, 'shard'), may hold values from -0.75 to 0.75
- out_bias: bfloat16 [2, 1024], P(None, 'shard'), may hold values from -3 to 3
- up_weight: bfloat16 [2, 1024, 4096], P(None, 'shard'), may hold values from -0.1875 to 0.1875
- up_bias: bfloat16 [2, 4096], P(None, 'shard'), may hold values from -3 to 3
- down_weight: bfloat16 [2, 4096, 1024], P(None, 'shard'), may hold values from -0.09375 to 0.09375
- down_bias: bfloat16 [2, 1024], P(None, 'shard'), may hold values from -3 to 3
- out_grad: bfloat16 [16, 512, 1024], P('rep', 'shard'), may hold values from -6 to 6
Outputs:
- block_out: bfloat16 [16, 512, 1024], P('rep', 'shard')
- in_grad: float32 [16, 512, 1024], P('rep', 'shard')
- norm_gains_grad: float32 [2, 2, 1024], P(None, None, 'shard')
- norm_biases_grad: float32 [2, 2, 1024], P(None, None, 'shard')
- qkv_weight_grad: float32 [2, 1024, 3072], P(None, 'shard')
- qkv_bias_grad: float32 [2, 3072], P(None, 'shard')
- out_weight_grad: float32 [2, 1024, 1024], P(None, 'shard')
- out_bias_grad: float32 [2, 1024], P(None, 'shard')
- up_weight_grad: float32 [2, 1024, 4096], P(None, 'shard')
- up_bias_grad: float32 [2, 4096], P(None, 'shard')
- down_weight_grad: float32 [2, 4096, 1024], P(None, 'shard')
- down_bias_grad: float32 [2, 1024], P(None, 'shard')
Inputs may be any that keep to these rules, and one draw needn't show every extreme that they name: `segments`: in every row the segment numbers start at 0, never fall and rise by at most one from one token to the next.
All inputs are finite; a program needn't handle non-finite values.
Results may differ from a plain program's by a relative error of at most 0.02.
Values may be sent and summed in bfloat16 or wider, within the bound.
No kernel may reach another device: no remote copies, remote signals or barrier semaphores. Data moves between devices by JAX's collectives and lax.ppermute only.
A program may use at most 320 MiB of HBM per device.

v0:
```python
import math

import jax
import jax.numpy as jnp
from jax import lax
from jax.sharding import PartitionSpec as P

H = 16
ROT = 16
LAYERS = 2


epsilon = 1e-05


def layer_norm(stream, gain_vec, shift_vec):
    average = jnp.mean(stream, -1, keepdims=True)
    centred = stream - average
    spread = jnp.mean(centred * centred, -1, keepdims=True)
    return centred * lax.rsqrt(spread + epsilon) * gain_vec + shift_vec


def rotary_tables(positions):
    half_rot = ROT // 2
    inverse = jnp.power(10000.0, -2.0 * jnp.arange(half_rot, dtype=jnp.float32) / ROT)
    angles = positions.astype(jnp.float32)[..., None] * inverse
    return (jnp.cos(angles)[..., None, :], jnp.sin(angles)[..., None, :])


def rotate(vectors, cosine_tab, sine_tab):
    half_rot = ROT // 2
    first_part = vectors[..., :half_rot]
    second = vectors[..., half_rot:ROT]
    return jnp.concatenate(
        [
            first_part * cosine_tab - second * sine_tab,
            second * cosine_tab + first_part * sine_tab,
            vectors[..., ROT:],
        ],
        -1,
    )


def visible(context, key_count):
    segments, seg_local, q_index, score_scale = context
    k_index = jnp.arange(key_count, dtype=jnp.int32)
    return (k_index[None, None, :] <= q_index[None, :, None]) & (
        segments[:, None, :] == seg_local[:, :, None]
    )


def attend(query_low, key_low, value_low, context):
    score_scale = context[3]
    row_count, span_len, head_count, head_dim = query_low.shape

    def fold(running, pieces, offset):
        run_max, run_sum, weighted = running
        key_part, value_part = pieces
        visible_mask = visible(context, key_part.shape[1])[:, None]
        scores = (
            jnp.einsum("rqhd,rkhd->rhqk", query_low, key_part, preferred_element_type=jnp.float32)
            * score_scale
        )
        scores = jnp.where(visible_mask, scores, -1e30)
        new_max = jnp.maximum(run_max, jnp.max(scores, -1))
        attn_weights = jnp.where(visible_mask, jnp.exp(scores - new_max[..., None]), 0.0)
        run_sum = jnp.sum(attn_weights, -1)
        weighted = jnp.einsum(
            "rhqk,rkhd->rhqd",
            attn_weights.astype(jnp.bfloat16),
            value_part,
            preferred_element_type=jnp.float32,
        )
        return (new_max, run_sum, weighted)

    start_max = jnp.full((row_count, head_count, span_len), -1e30, jnp.float32)
    start_sum = jnp.zeros((row_count, head_count, span_len), jnp.float32)
    start_acc = jnp.zeros((row_count, head_count, span_len, head_dim), jnp.float32)
    run_max, run_sum, weighted = fold(
        (start_max, start_sum, start_acc),
        (
            lax.all_gather(key_low, "shard", axis=1, tiled=True),
            lax.all_gather(value_low, "shard", axis=1, tiled=True),
        ),
        jnp.int32(0),
    )
    mixed = (weighted / run_sum[..., None]).transpose(0, 2, 1, 3)
    return (mixed, run_max + jnp.log(run_sum))


def attend_back(query_low, key_low, value_low, d_mixed, log_sum, delta, context):
    score_scale = context[3]
    row_count, span_len, head_count, head_dim = query_low.shape
    seq_len = context[0].shape[1]

    def fold(running, pieces, offset):
        key_part, value_part = pieces
        visible_mask = visible(context, key_part.shape[1])[:, None]
        scores = (
            jnp.einsum("rqhd,rkhd->rhqk", query_low, key_part, preferred_element_type=jnp.float32)
            * score_scale
        )
        attn_weights = jnp.exp(jnp.where(visible_mask, scores - log_sum[..., None], -1e30))
        d_weights = jnp.einsum(
            "rqhd,rkhd->rhqk", d_mixed, value_part, preferred_element_type=jnp.float32
        )
        d_scores = (attn_weights * (d_weights - delta[..., None])).astype(jnp.bfloat16)
        d_query = (
            jnp.einsum("rhqk,rkhd->rqhd", d_scores, key_part, preferred_element_type=jnp.float32)
            * score_scale
        )
        key_term = (
            jnp.einsum("rhqk,rqhd->rkhd", d_scores, query_low, preferred_element_type=jnp.float32)
            * score_scale
        )
        value_term = jnp.einsum(
            "rhqk,rqhd->rkhd",
            attn_weights.astype(jnp.bfloat16),
            d_mixed,
            preferred_element_type=jnp.float32,
        )
        return (d_query, key_term, value_term)

    start_query = jnp.zeros((row_count, span_len, head_count, head_dim), jnp.float32)
    start_keys = jnp.zeros((row_count, seq_len, head_count, head_dim), jnp.float32)
    d_query, d_keys, d_values = fold(
        (start_query, start_keys, start_keys),
        (
            lax.all_gather(key_low, "shard", axis=1, tiled=True),
            lax.all_gather(value_low, "shard", axis=1, tiled=True),
        ),
        jnp.int32(0),
    )
    d_keys, d_values = (
        lax.psum_scatter(
            d_keys.astype(jnp.bfloat16), "shard", scatter_dimension=1, tiled=True
        ).astype(jnp.float32),
        lax.psum_scatter(
            d_values.astype(jnp.bfloat16), "shard", scatter_dimension=1, tiled=True
        ).astype(jnp.float32),
    )
    return (d_query, d_keys, d_values)


def fetch_forward(layer_idx, params):
    (
        qkv_weight,
        qkv_bias,
        out_weight,
        out_bias,
        up_weight,
        up_bias,
        down_weight,
        down_bias,
        norm_gains,
        norm_biases,
    ) = params
    return (
        lax.all_gather(qkv_weight[layer_idx], "shard", axis=0, tiled=True),
        lax.all_gather(qkv_bias[layer_idx], "shard", axis=0, tiled=True),
        lax.all_gather(out_weight[layer_idx], "shard", axis=0, tiled=True),
        lax.all_gather(out_bias[layer_idx], "shard", axis=0, tiled=True),
        lax.all_gather(up_weight[layer_idx], "shard", axis=0, tiled=True),
        lax.all_gather(up_bias[layer_idx], "shard", axis=0, tiled=True),
        lax.all_gather(down_weight[layer_idx], "shard", axis=0, tiled=True),
        lax.all_gather(down_bias[layer_idx], "shard", axis=0, tiled=True),
        lax.all_gather(norm_gains[layer_idx], "shard", axis=1, tiled=True),
        lax.all_gather(norm_biases[layer_idx], "shard", axis=1, tiled=True),
    )


def fetch_backward(layer_idx, params):
    (
        qkv_weight,
        qkv_bias,
        out_weight,
        out_bias,
        up_weight,
        up_bias,
        down_weight,
        down_bias,
        norm_gains,
        norm_biases,
    ) = params
    return (
        lax.all_gather(qkv_weight[layer_idx], "shard", axis=0, tiled=True),
        lax.all_gather(qkv_bias[layer_idx], "shard", axis=0, tiled=True),
        lax.all_gather(out_weight[layer_idx], "shard", axis=0, tiled=True),
        lax.all_gather(out_bias[layer_idx], "shard", axis=0, tiled=True),
        lax.all_gather(up_weight[layer_idx], "shard", axis=0, tiled=True),
        lax.all_gather(up_bias[layer_idx], "shard", axis=0, tiled=True),
        lax.all_gather(down_weight[layer_idx], "shard", axis=0, tiled=True),
        lax.all_gather(down_bias[layer_idx], "shard", axis=0, tiled=True),
        lax.all_gather(norm_gains[layer_idx], "shard", axis=1, tiled=True),
        lax.all_gather(norm_biases[layer_idx], "shard", axis=1, tiled=True),
    )


def forward_layer(stream, gathered, cosine_tab, sine_tab, context, shape_rows):
    w_qkv, b_qkv, w_out, b_out, w_up, b_up, w_down, b_down, gains, shifts = gathered
    row_count, span_len = shape_rows
    model_width = stream.shape[1]
    gains_f = gains.astype(jnp.float32)
    shifts_f = shifts.astype(jnp.float32)
    attn_low = layer_norm(stream, gains_f[0], shifts_f[0]).astype(jnp.bfloat16)
    mlp_low = layer_norm(stream, gains_f[1], shifts_f[1]).astype(jnp.bfloat16)
    projected = jnp.dot(attn_low, w_qkv, preferred_element_type=jnp.float32) + b_qkv.astype(
        jnp.float32
    )
    projected = projected.reshape(row_count, span_len, 3, H, model_width // H)
    query_low = rotate(projected[:, :, 0], cosine_tab, sine_tab).astype(jnp.bfloat16)
    key_low = rotate(projected[:, :, 1], cosine_tab, sine_tab).astype(jnp.bfloat16)
    value_low = projected[:, :, 2].astype(jnp.bfloat16)
    mixed, log_sum = attend(query_low, key_low, value_low, context)
    mixed_low = mixed.reshape(row_count * span_len, model_width).astype(jnp.bfloat16)
    attn_out = jnp.dot(mixed_low, w_out, preferred_element_type=jnp.float32) + b_out.astype(
        jnp.float32
    )
    hidden_pre = jnp.dot(mlp_low, w_up, preferred_element_type=jnp.float32) + b_up.astype(
        jnp.float32
    )
    hidden_low = jax.nn.gelu(hidden_pre, approximate=False).astype(jnp.bfloat16)
    mlp_out = jnp.dot(hidden_low, w_down, preferred_element_type=jnp.float32) + b_down.astype(
        jnp.float32
    )
    saved = (
        stream,
        attn_low,
        mlp_low,
        query_low,
        key_low,
        value_low,
        mixed,
        log_sum,
        hidden_pre,
        mixed_low,
        hidden_low,
    )
    return (stream + attn_out + mlp_out, saved)


def backward_layer(grad_res, gathered, saved, cosine_tab, sine_tab, context):
    w_qkv, b_qkv, w_out, b_out, w_up, b_up, w_down, b_down, gains, shifts = gathered
    (
        stream,
        attn_low,
        mlp_low,
        query_low,
        key_low,
        value_low,
        mixed,
        log_sum,
        hidden_pre,
        mixed_low,
        hidden_low,
    ) = saved
    token_count, model_width = grad_res.shape
    gains_f = gains.astype(jnp.float32)
    shifts_f = shifts.astype(jnp.float32)
    grad_low = grad_res.astype(jnp.bfloat16)
    d_out_w = jnp.einsum("td,te->de", mixed_low, grad_low, preferred_element_type=jnp.float32)
    d_branch_b = jnp.sum(grad_low.astype(jnp.float32), 0)
    d_down_w = jnp.einsum("tf,td->fd", hidden_low, grad_low, preferred_element_type=jnp.float32)
    d_hidden = jnp.einsum("td,fd->tf", grad_low, w_down, preferred_element_type=jnp.float32)
    _, gelu_pull = jax.vjp(lambda inputs: jax.nn.gelu(inputs, approximate=False), hidden_pre)
    d_pre = gelu_pull(d_hidden)[0].astype(jnp.bfloat16)
    d_up_w = jnp.einsum("td,tf->df", mlp_low, d_pre, preferred_element_type=jnp.float32)
    d_up_b = jnp.sum(d_pre.astype(jnp.float32), 0)
    d_mlp_in = jnp.einsum("tf,df->td", d_pre, w_up, preferred_element_type=jnp.float32)
    d_mixed = (
        jnp.einsum("td,ed->te", grad_low, w_out, preferred_element_type=jnp.float32)
        .reshape(query_low.shape)
        .astype(jnp.bfloat16)
    )
    delta = jnp.sum(d_mixed.astype(jnp.float32) * mixed, -1).transpose(0, 2, 1)
    d_query, d_keys, d_values = attend_back(
        query_low, key_low, value_low, d_mixed, log_sum, delta, context
    )
    _, rot_pull = jax.vjp(
        lambda vectors: rotate(vectors, cosine_tab, sine_tab), jnp.zeros_like(d_query)
    )
    d_query_pre = rot_pull(d_query)[0]
    d_keys_pre = rot_pull(d_keys)[0]
    d_qkv = (
        jnp.stack([d_query_pre, d_keys_pre, d_values], 2)
        .reshape(token_count, 3 * model_width)
        .astype(jnp.bfloat16)
    )
    d_qkv_w = jnp.einsum("td,te->de", attn_low, d_qkv, preferred_element_type=jnp.float32)
    d_qkv_b = jnp.sum(d_qkv.astype(jnp.float32), 0)
    d_attn_in = jnp.einsum("te,de->td", d_qkv, w_qkv, preferred_element_type=jnp.float32)
    _, norm_first = jax.vjp(layer_norm, stream, gains_f[0], shifts_f[0])
    _, norm_second = jax.vjp(layer_norm, stream, gains_f[1], shifts_f[1])
    d_in_first, d_gain_first, d_shift_first = norm_first(d_attn_in)
    d_in_second, d_gain_second, d_shift_second = norm_second(d_mlp_in)
    d_stream = grad_res + d_in_first + d_in_second
    d_gains = jnp.stack([d_gain_first, d_gain_second])
    d_shifts = jnp.stack([d_shift_first, d_shift_second])
    owned = (
        lax.psum_scatter(
            d_qkv_w.astype(jnp.bfloat16), "shard", scatter_dimension=0, tiled=True
        ).astype(jnp.float32),
        lax.psum_scatter(
            d_qkv_b.astype(jnp.bfloat16), "shard", scatter_dimension=0, tiled=True
        ).astype(jnp.float32),
        lax.psum_scatter(
            d_out_w.astype(jnp.bfloat16), "shard", scatter_dimension=0, tiled=True
        ).astype(jnp.float32),
        lax.psum_scatter(
            d_branch_b.astype(jnp.bfloat16), "shard", scatter_dimension=0, tiled=True
        ).astype(jnp.float32),
        lax.psum_scatter(
            d_up_w.astype(jnp.bfloat16), "shard", scatter_dimension=0, tiled=True
        ).astype(jnp.float32),
        lax.psum_scatter(
            d_up_b.astype(jnp.bfloat16), "shard", scatter_dimension=0, tiled=True
        ).astype(jnp.float32),
        lax.psum_scatter(
            d_down_w.astype(jnp.bfloat16), "shard", scatter_dimension=0, tiled=True
        ).astype(jnp.float32),
        lax.psum_scatter(
            d_gains.astype(jnp.bfloat16), "shard", scatter_dimension=1, tiled=True
        ).astype(jnp.float32),
        lax.psum_scatter(
            d_shifts.astype(jnp.bfloat16), "shard", scatter_dimension=1, tiled=True
        ).astype(jnp.float32),
    )
    return (d_stream, owned)


def on_device(
    hidden_in,
    segments,
    norm_gains,
    norm_biases,
    qkv_weight,
    qkv_bias,
    out_weight,
    out_bias,
    up_weight,
    up_bias,
    down_weight,
    down_bias,
    out_grad,
):
    row_count, span_len, model_width = hidden_in.shape
    token_count = row_count * span_len
    score_scale = 1.0 / math.sqrt(model_width // H)
    first_tok = lax.axis_index("shard") * span_len
    seg_local = lax.dynamic_slice_in_dim(segments, first_tok, span_len, 1)
    earlier = jnp.sum((segments[:, None, :] < seg_local[:, :, None]).astype(jnp.int32), -1)
    q_index = first_tok + jnp.arange(span_len, dtype=jnp.int32)
    positions = q_index[None, :] - earlier
    cosine_tab, sine_tab = rotary_tables(positions)
    context = (segments, seg_local, q_index, score_scale)
    params = (
        qkv_weight,
        qkv_bias,
        out_weight,
        out_bias,
        up_weight,
        up_bias,
        down_weight,
        down_bias,
        norm_gains,
        norm_biases,
    )
    stream = hidden_in.reshape(token_count, model_width).astype(jnp.float32)
    kept_weights = []
    saved_all = []
    for layer_idx in range(LAYERS):
        gathered = fetch_forward(layer_idx, params)
        kept_weights.append(gathered)
        stream, saved = forward_layer(
            stream, gathered, cosine_tab, sine_tab, context, (row_count, span_len)
        )
        saved_all.append(saved)
    block_out = stream.astype(jnp.bfloat16).reshape(row_count, span_len, model_width)
    grad_res = out_grad.reshape(token_count, model_width).astype(jnp.float32)
    owned_all = [None] * LAYERS
    for layer_idx in reversed(range(LAYERS)):
        gathered = fetch_backward(layer_idx, params)
        grad_res, owned = backward_layer(
            grad_res, gathered, saved_all[layer_idx], cosine_tab, sine_tab, context
        )
        owned = (
            lax.psum(owned[0].astype(jnp.bfloat16), "rep").astype(jnp.float32),
            lax.psum(owned[1].astype(jnp.bfloat16), "rep").astype(jnp.float32),
            lax.psum(owned[2].astype(jnp.bfloat16), "rep").astype(jnp.float32),
            lax.psum(owned[3].astype(jnp.bfloat16), "rep").astype(jnp.float32),
            lax.psum(owned[4].astype(jnp.bfloat16), "rep").astype(jnp.float32),
            lax.psum(owned[5].astype(jnp.bfloat16), "rep").astype(jnp.float32),
            lax.psum(owned[6].astype(jnp.bfloat16), "rep").astype(jnp.float32),
            lax.psum(owned[7].astype(jnp.bfloat16), "rep").astype(jnp.float32),
            lax.psum(owned[8].astype(jnp.bfloat16), "rep").astype(jnp.float32),
        )
        owned_all[layer_idx] = owned
    stacked = [jnp.stack([owned[slot] for owned in owned_all]) for slot in range(9)]
    in_grad = grad_res.reshape(row_count, span_len, model_width)
    return (
        block_out,
        in_grad,
        stacked[7],
        stacked[8],
        stacked[0],
        stacked[1],
        stacked[2],
        stacked[3],
        stacked[4],
        stacked[5],
        stacked[6],
        stacked[3],
    )


def solution(mesh):
    in_specs = (
        P("rep", "shard", None),
        P("rep", None),
        P(None, None, "shard"),
        P(None, None, "shard"),
        P(None, "shard", None),
        P(None, "shard"),
        P(None, "shard", None),
        P(None, "shard"),
        P(None, "shard", None),
        P(None, "shard"),
        P(None, "shard", None),
        P(None, "shard"),
        P("rep", "shard", None),
    )
    out_specs = (
        P("rep", "shard", None),
        P("rep", "shard", None),
        P(None, None, "shard"),
        P(None, None, "shard"),
        P(None, "shard", None),
        P(None, "shard"),
        P(None, "shard", None),
        P(None, "shard"),
        P(None, "shard", None),
        P(None, "shard"),
        P(None, "shard", None),
        P(None, "shard"),
    )
    return jax.shard_map(
        on_device, mesh=mesh, in_specs=in_specs, out_specs=out_specs, check_vma=False
    )
```

profile of v0, /device:TPU:0, one launch (start us, length us, event | category | flops | bytes accessed | tf_op | source)
XLA Modules:
  0.0 2567.0 jit_solution(15920273129331718975)
XLA Ops:
  48.5 80.9 %all-gather.39.cloned.1.call-done = bf16[1,1024,3072]{2,1,0:T(8,128)(2,1)} async-done(((bf16[1,256,3072]{2,1,0:T(8,128)(2,1)}), bf16[1,1024,3072]{2,1,0:T(8,128)(2,1)}) %all-gather.39.cloned.1.call-update) | async-done | bytes 6291472 | tf_op jit(solution)/shard_map/all_gather | solution.py:159
  249.3 99.5 %all-gather.45.cloned.1.call-done = bf16[1,1024,4096]{2,1,0:T(8,128)(2,1)} async-done(((bf16[1,256,4096]{2,1,0:T(8,128)(2,1)}), bf16[1,1024,4096]{2,1,0:T(8,128)(2,1)}) %all-gather.45.cloned.1.call-update) | async-done | bytes 8388624 | tf_op jit(solution)/shard_map/all_gather | solution.py:163
  365.1 29.7 %all-gather.41.cloned.1.call-done = bf16[2,512,1,16,64]{1,4,3,0,2:T(8,128)(2,1)} async-done(((bf16[2,128,1,16,64]{1,4,3,0,2:T(8,128)(2,1)}), bf16[2,512,1,16,64]{1,4,3,0,2:T(8,128)(2,1)}) %all-gather.41.cloned.1.call-update) | async-done | bytes 2097168 | tf_op jit(solution)/shard_map/all_gather | solution.py:83
  402.6 142.0 %all-gather.47.cloned.1.call-done = bf16[1,4096,1024]{2,1,0:T(8,128)(2,1)} async-done(((bf16[1,1024,1024]{2,1,0:T(8,128)(2,1)}), bf16[1,4096,1024]{2,1,0:T(8,128)(2,1)}) %all-gather.47.cloned.1.call-update) | async-done | bytes 8388624 | tf_op jit(solution)/shard_map/all_gather | solution.py:165
  551.0 39.3 %all-gather.43.cloned.1.call-done = bf16[1,1024,1024]{2,1,0:T(8,128)(2,1)} async-done(((bf16[1,256,1024]{2,1,0:T(8,128)(2,1)}), bf16[1,1024,1024]{2,1,0:T(8,128)(2,1)}) %all-gather.43.cloned.1.call-update) | async-done | bytes 2097168 | tf_op jit(solution)/shard_map/all_gather | solution.py:161
  593.0 113.5 %all-gather.49.cloned.1.call-done = bf16[1,1024,3072]{2,1,0:T(8,128)(2,1)} async-done(((bf16[1,256,3072]{2,1,0:T(8,128)(2,1)}), bf16[1,1024,3072]{2,1,0:T(8,128)(2,1)}) %all-gather.49.cloned.1.call-update) | async-done | bytes 6291472 | tf_op jit(solution)/shard_map/all_gather | solution.py:159
  756.4 43.6 %all-gather.37.cloned.1.call-done = bf16[2,512,16,64]{1,3,2,0:T(8,128)(2,1)} async-done(((bf16[2,128,16,64]{1,3,2,0:T(8,128)(2,1)}), bf16[2,512,16,64]{1,3,2,0:T(8,128)(2,1)}) %all-gather.37.cloned.1.call-update) | async-done | bytes 2097168 | tf_op jit(solution)/shard_map/all_gather | solution.py:82
  806.7 39.8 %all-gather.51.cloned.1.call-done = bf16[2,512,1,16,64]{1,4,3,0,2:T(8,128)(2,1)} async-done(((bf16[2,128,1,16,64]{1,4,3,0,2:T(8,128)(2,1)}), bf16[2,512,1,16,64]{1,4,3,0,2:T(8,128)(2,1)}) %all-gather.51.cloned.1.call-update) | async-done | bytes 2097168 | tf_op jit(solution)/shard_map/all_gather | solution.py:83
  875.7 18.7 all-gather.19
  916.2 79.9 %all-gather.55.cloned.1.call-done = bf16[1,1024,4096]{2,1,0:T(8,128)(2,1)} async-done(((bf16[1,256,4096]{2,1,0:T(8,128)(2,1)}), bf16[1,1024,4096]{2,1,0:T(8,128)(2,1)}) %all-gather.55.cloned.1.call-update) | async-done | bytes 8388624 | tf_op jit(solution)/shard_map/all_gather | solution.py:163
  1012.8 132.7 %all-gather.57.cloned.1.call-done = bf16[1,4096,1024]{2,1,0:T(8,128)(2,1)} async-done(((bf16[1,1024,1024]{2,1,0:T(8,128)(2,1)}), bf16[1,4096,1024]{2,1,0:T(8,128)(2,1)}) %all-gather.57.cloned.1.call-update) | async-done | bytes 8388624 | tf_op jit(solution)/shard_map/all_gather | solution.py:165
  1164.2 25.6 reduce-scatter.49.cloned.1.call-done
  1197.9 37.4 %reduce-scatter.51.cloned.1.call-done = bf16[128,2048]{1,0:T(8,128)(2,1)} async-done(((bf16[512,2048]{1,0:T(8,128)(2,1)}), bf16[128,2048]{1,0:T(8,128)(2,1)}) %reduce-scatter.51.cloned.1.call-update) | async-done | bytes 524304
  1355.1 19.3 reduce-scatter.55.cloned.1.call-done
  1434.1 31.1 %reduce-scatter.37.cloned.1.call-done = bf16[256,1024]{1,0:T(8,128)(2,1)} async-done(((bf16[1024,1024]{1,0:T(8,128)(2,1)}), bf16[256,1024]{1,0:T(8,128)(2,1)}) %reduce-scatter.37.cloned.1.call-update) | async-done | bytes 524304 | tf_op jit(solution)/shard_map/reduce_scatter | solution.py:306
  1465.3 146.8 %reduce-scatter.43.cloned.1.call-done = bf16[256,4096]{1,0:T(8,128)(2,1)} async-done(((bf16[1024,4096]{1,0:T(8,128)(2,1)}), bf16[256,4096]{1,0:T(8,128)(2,1)}) %reduce-scatter.43.cloned.1.call-update) | async-done | bytes 2097168 | tf_op jit(solution)/shard_map/reduce_scatter | solution.py:312
  1612.0 147.4 %reduce-scatter.47.cloned.1.call-done = bf16[1024,1024]{1,0:T(8,128)(2,1)} async-done(((bf16[4096,1024]{1,0:T(8,128)(2,1)}), bf16[1024,1024]{1,0:T(8,128)(2,1)}) %reduce-scatter.47.cloned.1.call-update) | async-done | bytes 2097168 | tf_op jit(solution)/shard_map/reduce_scatter | solution.py:318
  1759.5 114.4 %reduce-scatter.35.cloned.1.call-done = bf16[256,3072]{1,0:T(8,128)(2,1)} async-done(((bf16[1024,3072]{1,0:T(8,128)(2,1)}), bf16[256,3072]{1,0:T(8,128)(2,1)}) %reduce-scatter.35.cloned.1.call-update) | async-done | bytes 1572880 | tf_op jit(solution)/shard_map/reduce_scatter | solution.py:300
  1873.9 113.6 %reduce-scatter.33.cloned.1.call-done = bf16[256,3072]{1,0:T(8,128)(2,1)} async-done(((bf16[1024,3072]{1,0:T(8,128)(2,1)}), bf16[256,3072]{1,0:T(8,128)(2,1)}) %reduce-scatter.33.cloned.1.call-update) | async-done | bytes 1572880 | tf_op jit(solution)/shard_map/reduce_scatter | solution.py:300
  1987.5 148.0 %reduce-scatter.41.cloned.1.call-done = bf16[256,4096]{1,0:T(8,128)(2,1)} async-done(((bf16[1024,4096]{1,0:T(8,128)(2,1)}), bf16[256,4096]{1,0:T(8,128)(2,1)}) %reduce-scatter.41.cloned.1.call-update) | async-done | bytes 2097168 | tf_op jit(solution)/shard_map/reduce_scatter | solution.py:312
  2135.4 147.4 %reduce-scatter.45.cloned.1.call-done = bf16[1024,1024]{1,0:T(8,128)(2,1)} async-done(((bf16[4096,1024]{1,0:T(8,128)(2,1)}), bf16[1024,1024]{1,0:T(8,128)(2,1)}) %reduce-scatter.45.cloned.1.call-update) | async-done | bytes 2097168 | tf_op jit(solution)/shard_map/reduce_scatter | solution.py:318
  2347.9 18.2 reduce-scatter.61.cloned.1.call-done
  2367.1 23.3 all-reduce.18
  2392.8 151.4 %all-reduce.23.cloned.1.call-done = (bf16[1,256,3072]{2,1,0:T(8,128)(2,1)}, bf16[1,256,3072]{2,1,0:T(8,128)(2,1)}, bf16[1,256,1024]{2,1,0:T(8,128)(2,1)}, bf16[1...) async-done(((bf16[1,256,3072]{2,1,0:T(8,128)(2,1)}, ...) | async-done | bytes 12582928 | tf_op jit(solution)/shard_map/psum | solution.py:387
  (462 shorter events, 605.5 us)
Async XLA Ops:
  11.1 228.8 %all-gather.35.cloned.1.call-start = ((), (), s32[]{:S(2)}) async-start(), calls=%async_computation.16 | async-start | bytes 2621440 | tf_op jit(solution)/shard_map/all_gather | solution.py:82
  153.7 195.1 %all-gather.45.cloned.1.call-start = ((), (), s32[]{:S(2)}) async-start(), calls=%async_computation.29 | async-start | bytes 10485760 | tf_op jit(solution)/shard_map/all_gather | solution.py:163
  158.5 236.2 %all-gather.41.cloned.1.call-start = ((), (), s32[]{:S(2)}) async-start(), calls=%async_computation.27 | async-start | bytes 2621440 | tf_op jit(solution)/shard_map/all_gather | solution.py:83
  162.2 382.5 %all-gather.47.cloned.1.call-start = ((), (), s32[]{:S(2)}) async-start(), calls=%async_computation.30 | async-start | bytes 10485760 | tf_op jit(solution)/shard_map/all_gather | solution.py:165
  167.0 423.2 %all-gather.43.cloned.1.call-start = ((), (), s32[]{:S(2)}) async-start(), calls=%async_computation.28 | async-start | bytes 2621440 | tf_op jit(solution)/shard_map/all_gather | solution.py:161
  168.1 538.4 %all-gather.49.cloned.1.call-start = ((), (), s32[]{:S(2)}) async-start(), calls=%async_computation.31 | async-start | bytes 7864320 | tf_op jit(solution)/shard_map/all_gather | solution.py:159
  168.9 584.0 %all-gather.53.cloned.1.call-start = ((), (), s32[]{:S(2)}) async-start(), calls=%async_computation.33 | async-start | bytes 2621440 | tf_op jit(solution)/shard_map/all_gather | solution.py:161
  169.6 630.4 %all-gather.37.cloned.1.call-start = ((), (), s32[]{:S(2)}) async-start(), calls=%async_computation.17 | async-start | bytes 2621440 | tf_op jit(solution)/shard_map/all_gather | solution.py:82
  735.9 260.2 %all-gather.55.cloned.1.call-start = ((), (), s32[]{:S(2)}) async-start(), calls=%async_computation.34 | async-start | bytes 10485760 | tf_op jit(solution)/shard_map/all_gather | solution.py:163
  736.7 408.8 %all-gather.57.cloned.1.call-start = ((), (), s32[]{:S(2)}) async-start(), calls=%async_computation.35 | async-start | bytes 10485760 | tf_op jit(solution)/shard_map/all_gather | solution.py:165
  737.2 452.6 %reduce-scatter.49.cloned.1.call-start = ((), (), s32[]{:S(2)}) async-start(), calls=%async_computation.36 | async-start | bytes 2621440
  875.6 359.7 %reduce-scatter.51.cloned.1.call-start = ((), (), s32[]{:S(2)}) async-start(), calls=%async_computation.37 | async-start | bytes 2621440
  915.8 429.4 %reduce-scatter.53.cloned.1.call-start = ((), (), s32[]{:S(2)}) async-start(), calls=%async_computation.38 | async-start | bytes 2621440
  1315.4 296.6 %reduce-scatter.43.cloned.1.call-start = ((), (), s32[]{:S(2)}) async-start(), calls=%async_computation.23 | async-start | bytes 10485760 | tf_op jit(solution)/shard_map/reduce_scatter | solution.py:312
  1323.0 436.5 %reduce-scatter.47.cloned.1.call-start = ((), (), s32[]{:S(2)}) async-start(), calls=%async_computation.25 | async-start | bytes 10485760 | tf_op jit(solution)/shard_map/reduce_scatter | solution.py:318
  1330.3 543.5 %reduce-scatter.35.cloned.1.call-start = ((), (), s32[]{:S(2)}) async-start(), calls=%async_computation.19 | async-start | bytes 7864320 | tf_op jit(solution)/shard_map/reduce_scatter | solution.py:300
  1337.1 650.3 %reduce-scatter.33.cloned.1.call-start = ((), (), s32[]{:S(2)}) async-start(), calls=%async_computation.18 | async-start | bytes 7864320 | tf_op jit(solution)/shard_map/reduce_scatter | solution.py:300
  1392.0 743.4 %reduce-scatter.41.cloned.1.call-start = ((), (), s32[]{:S(2)}) async-start(), calls=%async_computation.22 | async-start | bytes 10485760 | tf_op jit(solution)/shard_map/reduce_scatter | solution.py:312
  1409.3 873.6 %reduce-scatter.45.cloned.1.call-start = ((), (), s32[]{:S(2)}) async-start(), calls=%async_computation.24 | async-start | bytes 10485760 | tf_op jit(solution)/shard_map/reduce_scatter | solution.py:318
  1416.7 895.7 %reduce-scatter.63.cloned.1.call-start = ((), (), s32[]{:S(2)}) async-start(), calls=%async_computation.43 | async-start | bytes 327680
  1417.7 907.9 %reduce-scatter.59.cloned.1.call-start = ((), (), s32[]{:S(2)}) async-start(), calls=%async_computation.41 | async-start | bytes 327680
  1418.7 928.3 %reduce-scatter.57.cloned.1.call-start = ((), (), s32[]{:S(2)}) async-start(), calls=%async_computation.40 | async-start | bytes 327680
  1433.1 933.1 %reduce-scatter.61.cloned.1.call-start = ((), (), s32[]{:S(2)}) async-start(), calls=%async_computation.42 | async-start | bytes 327680
  1434.1 1110.2 %all-reduce.23.cloned.1.call-start = ((), (), s32[]{:S(2)}) async-start(), calls=%async_computation.44 | async-start | bytes 25165824 | tf_op jit(solution)/shard_map/psum | solution.py:387
  (100 other events, 6224.4 us)
Sparse Core Ops, SparseCore 0:
  11.2 118.1 all-gather.38
  153.8 44.6 all-gather.34
  200.6 148.1 all-gather.44
  350.2 44.4 all-gather.40
  396.7 147.8 all-gather.46
  546.0 44.1 all-gather.42
  592.4 114.0 all-gather.48
  708.6 44.1 all-gather.52
  755.0 44.9 all-gather.36
  801.9 44.4 all-gather.50
  848.0 148.0 all-gather.54
  997.5 147.8 all-gather.56
  1192.1 43.2 reduce-scatter.50
  1285.7 43.1 reduce-scatter.52
  1331.2 43.1 reduce-scatter.54
  1376.6 43.1 reduce-scatter.38
  1422.0 43.1 reduce-scatter.36
  1468.2 143.7 reduce-scatter.42
  1614.2 145.1 reduce-scatter.46
  1762.3 111.4 reduce-scatter.34
  1876.2 111.2 reduce-scatter.32
  1990.4 144.9 reduce-scatter.40
  2137.6 145.1 reduce-scatter.44
  2370.8 173.3 all-reduce.22
  (5 shorter events, 115.9 us)
where the time goes:
time: 2580 us; the launch traced here: 2570 us
  waiting for transfers between devices  1930 us (75%)
  matrix products  208 us (8%)
  local copies, waits for them, and re-layouts  180 us (7%)
  blocking collectives  178 us (7%)
  other arithmetic  47.7 us (2%)
    reduce_scatter x2, waiting for transfers between devices, backward_layer(): lax.psum_scatter(d_down_w.astype(jnp.bfloat16), 'shard', scatter_dimensio...  295 us
    reduce_scatter x2, waiting for transfers between devices, backward_layer(): lax.psum_scatter(d_up_w.astype(jnp.bfloat16), 'shard', scatter_dimension=...  295 us
    all_gather x2, waiting for transfers between devices, fetch_forward(): lax.all_gather(down_weight[layer_idx], 'shard', axis=0, tiled=True)  275 us
    reduce_scatter x2, waiting for transfers between devices, backward_layer(): lax.psum_scatter(d_qkv_w.astype(jnp.bfloat16), 'shard', scatter_dimension...  228 us
    all_gather x2, waiting for transfers between devices, fetch_forward(): lax.all_gather(qkv_weight[layer_idx], 'shard', axis=0, tiled=True)  194 us
    all_gather x2, waiting for transfers between devices, fetch_forward(): lax.all_gather(up_weight[layer_idx], 'shard', axis=0, tiled=True)  179 us
    psum x1, waiting for transfers between devices, on_device(): lax.psum(owned[0].astype(jnp.bfloat16), 'rep').astype(jnp.float32)  151 us
    unnamed x226, local copies, waits for them, and re-layouts  121 us
  transfers between devices with their start and end apart: 29, of which 24 were waited for; matrix products, arithmetic and copies ran while one was open for 13% of the time, Pallas kernels for 0%

commit v1 on v0

v1 whole, which is shorter than its diff:
```python
import math

import jax
import jax.numpy as jnp
from jax import lax
from jax.experimental import pallas as pl
from jax.experimental.pallas import tpu as pltpu
from jax.sharding import Mesh
from jax.sharding import PartitionSpec as P

H = 16
ROT = 16
LAYERS = 2
EPS = 1e-05
ROOT_HALF = math.sqrt(0.5)
F32 = jnp.float32
BF16 = jnp.bfloat16
AXES = ("outer", "ybit", "xbit", "core")
VMEM_LIMIT = 48 * 1024 * 1024


def swap(x, axis):
    return lax.ppermute(x, axis, [(0, 1), (1, 0)])


def spin(x, k, span):
    return lax.ppermute(x, "shard", [(j, (j + k) % span) for j in range(span)])


def after(x, dep):
    return lax.optimization_barrier((x, dep))[0]


def dot(a, b):
    return jnp.dot(a, b, preferred_element_type=F32)


def dot_t(a, b):
    return lax.dot_general(a, b, (((1,), (1,)), ((), ())), preferred_element_type=F32)


class Place:
    def __init__(self, span):
        self.span = span
        self.z = lax.axis_index("shard")
        self.c = lax.axis_index("core")
        self.bx = lax.axis_index("xbit")
        self.by = lax.axis_index("ybit")
        self.q = 2 * self.by + self.bx
        self.scalars = jnp.stack([self.z, self.q, self.c]).astype(jnp.int32)


def from_relative(blocks, place):
    span = place.span
    order = [blocks[(-m) % span] for m in range(2 * span - 1)]
    return lax.dynamic_slice_in_dim(
        jnp.stack(order), lax.rem(span - place.z, span), span, 0
    )


def by_core(place, own, other, axis):
    return jnp.where(
        place.c == 0,
        jnp.concatenate([own, other], axis),
        jnp.concatenate([other, own], axis),
    )


def copy_call(body, out_shape, copies, operands, place):
    def kernel(scalars, *refs):
        ins, out, sems = refs[: len(operands)], refs[len(operands)], refs[-1]
        started = []
        for slot, (src, dst) in enumerate(body(scalars, ins, out)):
            copy = pltpu.make_async_copy(src, dst, sems.at[slot])
            copy.start()
            started.append(copy)
        for copy in started:
            copy.wait()

    size = 2 * math.prod(out_shape.shape) * out_shape.dtype.itemsize
    return pl.pallas_call(
        kernel,
        out_shape=out_shape,
        in_specs=[pl.BlockSpec(memory_space=pltpu.SMEM)]
        + [pl.BlockSpec(memory_space=pl.ANY)] * len(operands),
        out_specs=pl.BlockSpec(memory_space=pltpu.VMEM),
        scratch_shapes=[pltpu.SemaphoreType.DMA((copies,))],
        compiler_params=pltpu.CompilerParams(vmem_limit_bytes=VMEM_LIMIT),
        cost_estimate=pl.CostEstimate(flops=0, bytes_accessed=size, transcendentals=0),
    )(place.scalars, *operands)


def pick_columns(shard, width, place):
    rows, columns = shard.shape
    count = columns // (2 * width)

    def body(scalars, ins, out):
        core = scalars[2]
        for j in range(count):
            start = pl.multiple_of((2 * j + core) * width, width)
            yield ins[0].at[:, pl.ds(start, width)], out.at[:, pl.ds(j * width, width)]

    shape = jax.ShapeDtypeStruct((rows, count * width), shard.dtype)
    return copy_call(body, shape, count, [shard], place)


def assemble(half, pieces, flips, place):
    span = place.span
    quarter, columns = half.shape[0] // 4, half.shape[1]

    def body(scalars, ins, out):
        z, q = scalars[0], scalars[1]
        yield ins[0], out.at[z]
        for i, flip in enumerate(flips):
            slot = lax.bitwise_xor(q, jnp.int32(flip))
            for k in range(1, span):
                source = lax.rem(z + (span - k), span)
                yield ins[1 + i].at[k - 1], out.at[source, slot]

    shape = jax.ShapeDtypeStruct((span, 4, quarter, columns), half.dtype)
    half = half.reshape(4, quarter, columns)
    out = copy_call(body, shape, 1 + len(flips) * (span - 1), [half, *pieces], place)
    return out.reshape(span * 4 * quarter, columns)


def relative_rows(table, flips, place):
    span = place.span
    quarter = table.shape[0] // (4 * span)
    table = table.reshape(span, 4, quarter, table.shape[1])

    def body(scalars, ins, out):
        z, q = scalars[0], scalars[1]
        for j, flip in enumerate(flips):
            for k in range(span):
                target = lax.rem(z + k, span)
                yield ins[0].at[target, lax.bitwise_xor(q, jnp.int32(flip))], out.at[j, k]

    shape = jax.ShapeDtypeStruct((4, span, quarter, table.shape[3]), table.dtype)
    return copy_call(body, shape, 4 * span, [table], place)


def absolute_quarters(parts, flips, place):
    quarter, columns = parts[0].shape

    def body(scalars, ins, out):
        for i, flip in enumerate(flips):
            yield ins[i], out.at[lax.bitwise_xor(scalars[1], jnp.int32(flip))]

    shape = jax.ShapeDtypeStruct((4, quarter, columns), parts[0].dtype)
    return copy_call(body, shape, 4, list(parts), place).reshape(4 * quarter, columns)


def row_to_chip(x, place):
    span = place.span
    rows, tokens, width = x.shape
    half = width // 2
    mine = lax.dynamic_slice_in_dim(x, place.c * half, half, 2)
    theirs = lax.dynamic_slice_in_dim(x, (1 - place.c) * half, half, 2)
    rows_all = by_core(place, mine, swap(theirs, "core"), 0)
    blocks = []
    for k in range(span):
        block = lax.dynamic_index_in_dim(
            rows_all, lax.rem(place.z + k, span), 0, keepdims=False
        )
        blocks.append(block if k == 0 else spin(block, k, span))
    own = from_relative(blocks, place).reshape(span * tokens, half)
    return by_core(place, own, swap(own, "core"), 1)


def chip_to_rows(y, rows, place):
    span = place.span
    width = y.shape[1]
    tokens = y.shape[0] // span
    half = width // 2
    mine = lax.dynamic_slice_in_dim(y, place.c * half, half, 1)
    mine = mine.reshape(span, tokens, half)
    blocks = []
    for k in range(span):
        block = lax.dynamic_index_in_dim(
            mine, lax.rem(place.z + k, span), 0, keepdims=False
        )
        blocks.append(block if k == 0 else spin(block, k, span))
    stacked = from_relative(blocks, place)
    own = lax.dynamic_slice_in_dim(stacked, place.c * rows, rows, 0)
    theirs = lax.dynamic_slice_in_dim(stacked, (1 - place.c) * rows, rows, 0)
    return by_core(place, own, swap(theirs, "core"), 2)


def axis_order(x_first):
    return ("xbit", 1, "ybit", 2) if x_first else ("ybit", 2, "xbit", 1)


def gather_weight(half, x_first, gate, place):
    span = place.span
    quarter = half.shape[0] // 4
    first, flip_first, second, flip_second = axis_order(x_first)
    mine = lax.dynamic_slice_in_dim(half, place.q * quarter, quarter, 0)
    if gate is not None:
        mine = after(mine, gate)
    near = jnp.stack([spin(mine, k, span) for k in range(1, span)])
    near_first = swap(near, first)
    near_second = swap(near, second)
    far = swap(near_first, second)
    flips = (0, flip_first, flip_second, flip_first ^ flip_second)
    return assemble(half, (near, near_first, near_second, far), flips, place), near


def reduce_weight(left_t, right, x_first, place):
    span = place.span
    first, flip_first, second, flip_second = axis_order(x_first)
    both = flip_first ^ flip_second
    rows = relative_rows(left_t, (0, flip_second, flip_first, both), place)
    quarter, tokens = rows.shape[2:]
    columns = right.shape[1]
    rows = rows.reshape(4 * span * quarter, tokens)
    cut = 2 * span * quarter
    send = dot(rows[cut:], right).astype(BF16)
    keep = dot(rows[:cut], right).astype(BF16)
    got = swap(send, first)
    keep = keep.reshape(2, span, quarter, columns)
    got = got.reshape(2, span, quarter, columns)
    onward = (keep[1].astype(F32) + got[1].astype(F32)).astype(BF16)
    got_second = swap(onward, second)
    total = (
        keep[0].astype(F32) + got[0].astype(F32) + got_second.astype(F32)
    ).astype(BF16)
    summed = total[0].astype(F32)
    for k in range(1, span):
        summed = summed + spin(total[k], k, span).astype(F32)
    summed = summed.astype(BF16)
    if lax.axis_size("outer") > 1:
        summed = lax.psum(summed, "outer")
    near_first = swap(summed, first)
    near_second = swap(summed, second)
    far = swap(near_first, second)
    flips = (0, flip_first, flip_second, both)
    return absolute_quarters((summed, near_first, near_second, far), flips, place)


def gather_small(vectors, place):
    flat = jnp.concatenate([v.reshape(-1) for v in vectors])
    blocks = [flat] + [spin(flat, k, place.span) for k in range(1, place.span)]
    table = from_relative(blocks, place)
    out, start = [], 0
    for v in vectors:
        part = table[:, start : start + v.size].reshape(place.span, *v.shape)
        start += v.size
        part = jnp.moveaxis(part, 0, -2)
        out.append(part.reshape(*v.shape[:-1], -1).astype(F32))
    return out


def blocks_of(length):
    step = 128 if length % 128 == 0 else length
    return [(i * step, step) for i in range(length // step)]


def seen(seg_col, seg_row, start, step):
    stop = start + step
    row = start + lax.broadcasted_iota(jnp.int32, (step, stop), 0)
    col = lax.broadcasted_iota(jnp.int32, (step, stop), 1)
    return (col <= row) & (seg_col[start:stop, :] == seg_row[:, :stop])


def attend_kernel(scale, head, q_ref, k_ref, v_ref, seg_col, seg_row, o_ref, lse_ref):
    length = q_ref.shape[0]
    for start, step in blocks_of(length):
        stop = start + step
        mask = seen(seg_col, seg_row, start, step)
        for h in range(q_ref.shape[1] // head):
            lanes = slice(h * head, (h + 1) * head)
            scores = dot_t(q_ref[start:stop, lanes], k_ref[:stop, lanes]) * scale
            scores = jnp.where(mask, scores, -1e30)
            top = jnp.max(scores, -1, keepdims=True)
            expo = jnp.exp(scores - top)
            total = jnp.sum(expo, -1, keepdims=True)
            probs = (expo * (1.0 / total)).astype(BF16)
            o_ref[start:stop, lanes] = dot(probs, v_ref[:stop, lanes]).astype(BF16)
            lse_ref[h, start:stop, :] = top + jnp.log(total)


def attend_back_kernel(
    scale, head, q_ref, k_ref, v_ref, do_ref, lse_ref, seg_col, seg_row, dq_ref, dk_ref, dv_ref
):
    length = q_ref.shape[0]
    dk_ref[...] = jnp.zeros_like(dk_ref)
    dv_ref[...] = jnp.zeros_like(dv_ref)
    over_rows = (((0,), (0,)), ((), ()))
    for start, step in blocks_of(length):
        stop = start + step
        mask = seen(seg_col, seg_row, start, step)
        for h in range(q_ref.shape[1] // head):
            lanes = slice(h * head, (h + 1) * head)
            query = q_ref[start:stop, lanes]
            keys = k_ref[:stop, lanes]
            grad = do_ref[start:stop, lanes]
            scores = dot_t(query, keys) * scale
            probs = jnp.exp(jnp.where(mask, scores - lse_ref[h, start:stop, :], -1e30))
            d_probs = dot_t(grad, v_ref[:stop, lanes])
            delta = jnp.sum(probs * d_probs, -1, keepdims=True)
            d_scores = (probs * (d_probs - delta)).astype(BF16)
            dq_ref[start:stop, lanes] = dot(d_scores, keys) * scale
            dk_ref[:stop, lanes] += (
                lax.dot_general(d_scores, query, over_rows, preferred_element_type=F32) * scale
            )
            dv_ref[:stop, lanes] += lax.dot_general(
                probs.astype(BF16), grad, over_rows, preferred_element_type=F32
            )


def attention_specs(length, width, head):
    group = max(head, 128)
    wide = pl.BlockSpec((length, group), lambda i: (0, i))
    lse = pl.BlockSpec((group // head, length, 1), lambda i: (i, 0, 0))
    segs = [
        pl.BlockSpec((length, 1), lambda i: (0, 0)),
        pl.BlockSpec((1, length), lambda i: (0, 0)),
    ]
    return wide, lse, segs, (width // group,)


def attend(query, keys, values, seg_col, seg_row, head):
    length, width = query.shape
    wide, lse, segs, grid = attention_specs(length, width, head)
    heads = width // head

    def kernel(*refs):
        attend_kernel(1.0 / math.sqrt(head), head, *refs)

    return pl.pallas_call(
        kernel,
        grid=grid,
        in_specs=[wide, wide, wide, *segs],
        out_specs=[wide, lse],
        out_shape=[
            jax.ShapeDtypeStruct((length, width), BF16),
            jax.ShapeDtypeStruct((heads, length, 1), F32),
        ],
        compiler_params=pltpu.CompilerParams(vmem_limit_bytes=VMEM_LIMIT),
        cost_estimate=pl.CostEstimate(
            flops=4 * length * length * width,
            bytes_accessed=8 * length * width,
            transcendentals=heads * length * length,
        ),
    )(query, keys, values, seg_col, seg_row)


def attend_back(query, keys, values, d_mixed, lse_all, seg_col, seg_row, head):
    length, width = query.shape
    wide, lse, segs, grid = attention_specs(length, width, head)
    heads = width // head

    def kernel(*refs):
        attend_back_kernel(1.0 / math.sqrt(head), head, *refs)

    out = jax.ShapeDtypeStruct((length, width), F32)
    return pl.pallas_call(
        kernel,
        grid=grid,
        in_specs=[wide, wide, wide, wide, lse, *segs],
        out_specs=[wide, wide, wide],
        out_shape=[out, out, out],
        compiler_params=pltpu.CompilerParams(vmem_limit_bytes=VMEM_LIMIT),
        cost_estimate=pl.CostEstimate(
            flops=10 * length * length * width,
            bytes_accessed=20 * length * width,
            transcendentals=heads * length * length,
        ),
    )(query, keys, values, d_mixed, lse_all, seg_col, seg_row)


def rotary_tables(positions, head, heads):
    half = ROT // 2
    inverse = jnp.power(10000.0, -2.0 * jnp.arange(half, dtype=F32) / ROT)
    angles = positions.astype(F32)[:, None] * inverse
    cos, sin = jnp.cos(angles), jnp.sin(angles)
    rest = jnp.zeros((positions.shape[0], head - ROT), F32)
    none = jnp.zeros_like(sin)
    keep = jnp.concatenate([cos, cos, rest + 1.0], 1)
    upper = jnp.concatenate([-sin, none, rest], 1)
    lower = jnp.concatenate([none, sin, rest], 1)
    return [jnp.tile(t, (1, heads)) for t in (keep, upper, lower)]


def rotate(u, tables):
    keep, upper, lower = tables
    half = ROT // 2
    return u * keep + jnp.roll(u, -half, 1) * upper + jnp.roll(u, half, 1) * lower


def rotate_back(d, tables):
    keep, upper, lower = tables
    half = ROT // 2
    return d * keep + jnp.roll(d * upper, half, 1) + jnp.roll(d * lower, -half, 1)


def normalise(x):
    centred = x - jnp.mean(x, -1, keepdims=True)
    spread = jnp.mean(centred * centred, -1, keepdims=True)
    inverse = lax.rsqrt(spread + EPS)
    return centred * inverse, inverse


def forward_layer(x, weights, small, tables, segs, head):
    w_qkv, w_out, w_up, w_down = weights
    gains, shifts, b_qkv, b_out, b_up, b_down = small
    xhat, inverse = normalise(x)
    attn_low = (xhat * gains[0] + shifts[0]).astype(BF16)
    mlp_low = (xhat * gains[1] + shifts[1]).astype(BF16)
    projected = dot(attn_low, w_qkv) + b_qkv
    width = projected.shape[1] // 3
    query = rotate(projected[:, :width], tables).astype(BF16)
    keys = rotate(projected[:, width : 2 * width], tables).astype(BF16)
    values = projected[:, 2 * width :].astype(BF16)
    mixed_low, lse = attend(query, keys, values, *segs, head)
    hidden_pre = dot(mlp_low, w_up) + b_up
    cdf = 0.5 * (1.0 + lax.erf(hidden_pre * ROOT_HALF))
    hidden_low = (hidden_pre * cdf).astype(BF16)
    part = (dot(mixed_low, w_out) + dot(hidden_low, w_down)).astype(BF16)
    other = swap(part, "core")
    y = x + (part.astype(F32) + other.astype(F32) + b_out + b_down)
    return y, (
        xhat,
        inverse,
        attn_low,
        mlp_low,
        query,
        keys,
        values,
        mixed_low,
        lse,
        hidden_pre,
        hidden_low,
    )


def backward_layer(dy, weights, small, saved, tables, segs, head, place, x_first):
    w_qkv, w_out, w_up, w_down = weights
    gains = small[0]
    (
        xhat,
        inverse,
        attn_low,
        mlp_low,
        query,
        keys,
        values,
        mixed_low,
        lse,
        hidden_pre,
        hidden_low,
    ) = saved
    dy_low = dy.astype(BF16)
    d_down = reduce_weight(hidden_low.T, dy_low, x_first, place)
    d_out = reduce_weight(mixed_low.T, dy_low, not x_first, place)
    d_branch_b = jnp.sum(dy_low.astype(F32), 0)
    d_hidden = dot_t(dy_low, w_down)
    cdf = 0.5 * (1.0 + lax.erf(hidden_pre * ROOT_HALF))
    density = jnp.exp(-0.5 * hidden_pre * hidden_pre) * (1.0 / math.sqrt(2.0 * math.pi))
    d_pre = (d_hidden * (cdf + hidden_pre * density)).astype(BF16)
    d_up = reduce_weight(mlp_low.T, d_pre, not x_first, place)
    d_up_b = jnp.sum(d_pre.astype(F32), 0)
    d_mlp = dot_t(d_pre, w_up)
    d_mixed = dot_t(dy_low, w_out).astype(BF16)
    d_query, d_keys, d_values = attend_back(
        query, keys, values, d_mixed, lse, *segs, head
    )
    d_qkv = jnp.concatenate(
        [
            rotate_back(d_query, tables).astype(BF16),
            rotate_back(d_keys, tables).astype(BF16),
            d_values.astype(BF16),
        ],
        1,
    )
    d_qkv_w = reduce_weight(attn_low.T, d_qkv, x_first, place)
    d_qkv_b = jnp.sum(d_qkv.astype(F32), 0)
    d_attn = dot_t(d_qkv, w_qkv)
    d_gains = jnp.stack([jnp.sum(d_attn * xhat, 0), jnp.sum(d_mlp * xhat, 0)])
    d_shifts = jnp.stack([jnp.sum(d_attn, 0), jnp.sum(d_mlp, 0)])
    part = (d_attn * gains[0] + d_mlp * gains[1]).astype(BF16)
    d_xhat = part.astype(F32) + swap(part, "core").astype(F32)
    dx = dy + inverse * (
        d_xhat
        - jnp.mean(d_xhat, -1, keepdims=True)
        - xhat * jnp.mean(d_xhat * xhat, -1, keepdims=True)
    )
    return dx, (d_qkv_w, d_out, d_up, d_down), (d_gains, d_shifts, d_qkv_b, d_branch_b, d_up_b)


def pick_vector(v, width, place):
    return jnp.take(v.reshape(*v.shape[:-1], -1, 2, width), place.c, axis=-2).reshape(
        *v.shape[:-1], -1
    )


def spread_vector(v, width, place):
    blocks = v.reshape(-1, 1, width)
    here = (jnp.arange(2) == place.c)[None, :, None]
    return jnp.where(here, blocks, 0.0).reshape(-1)


def reduce_small(grads, head_cols, ff_cols, place):
    d_gains, d_shifts, d_qkv_b, d_branch_b, d_up_b = grads
    parts = [
        d_gains,
        d_shifts,
        spread_vector(d_qkv_b, head_cols, place),
        jnp.where(place.c == 0, d_branch_b, 0.0),
        spread_vector(d_up_b, ff_cols, place),
    ]
    shapes = [p.shape for p in parts]
    flat = lax.psum(
        jnp.concatenate([p.reshape(-1) for p in parts]), (*AXES, "shard")
    )
    out, start = [], 0
    for shape in shapes:
        size = math.prod(shape)
        part = flat[start : start + size].reshape(shape)
        start += size
        own = shape[-1] // place.span
        out.append(lax.dynamic_slice_in_dim(part, place.z * own, own, len(shape) - 1))
    return out


def join_columns(half, width, place):
    other = swap(half, "core")
    even = jnp.where(place.c == 0, half, other)
    odd = jnp.where(place.c == 0, other, half)
    parts = []
    for j in range(half.shape[1] // width):
        lanes = slice(j * width, (j + 1) * width)
        parts += [even[:, lanes], odd[:, lanes]]
    return jnp.concatenate(parts, 1).astype(F32)


def join_rows(half, place):
    return by_core(place, half, swap(half, "core"), 0).astype(F32)


def on_device(span, *arguments):
    (
        hidden_in,
        segments,
        norm_gains,
        norm_biases,
        qkv_weight,
        qkv_bias,
        out_weight,
        out_bias,
        up_weight,
        up_bias,
        down_weight,
        down_bias,
        out_grad,
    ) = arguments
    place = Place(span)
    rows = hidden_in.shape[0]
    width = hidden_in.shape[2]
    head = width // H
    head_cols = width // (2 * span)
    ff_cols = up_weight.shape[2] // (2 * span)
    assert 2 * rows == span

    x = row_to_chip(hidden_in, place)
    seg_all = by_core(place, segments, swap(segments, "core"), 0)
    seg = lax.dynamic_index_in_dim(seg_all, place.z, 0, keepdims=False)
    seg_col, seg_row = seg[:, None], seg[None, :]
    length = seg.shape[0]
    earlier = jnp.sum((seg_row < seg_col).astype(jnp.int32), -1)
    positions = jnp.arange(length, dtype=jnp.int32) - earlier
    tables = rotary_tables(positions, head, H // 2)
    segs = (seg_col, seg_row)

    small = gather_small(
        [norm_gains, norm_biases, qkv_bias, out_bias, up_bias, down_bias], place
    )
    gains, shifts, b_qkv, b_out, b_up, b_down = small
    b_qkv = pick_vector(b_qkv, head_cols, place)
    b_up = pick_vector(b_up, ff_cols, place)

    def my_rows(w):
        half = w.shape[0] // 2
        return lax.dynamic_slice_in_dim(w, place.c * half, half, 0)

    gate = x
    weights = []
    for layer in range(LAYERS):
        x_first = layer % 2 == 0
        w_qkv, gate = gather_weight(
            pick_columns(qkv_weight[layer], head_cols, place), x_first, gate, place
        )
        w_up, gate = gather_weight(
            pick_columns(up_weight[layer], ff_cols, place), not x_first, gate, place
        )
        w_out, gate = gather_weight(my_rows(out_weight[layer]), x_first, gate, place)
        w_down, gate = gather_weight(
            my_rows(down_weight[layer]), not x_first, gate, place
        )
        weights.append((w_qkv, w_out, w_up, w_down))
    dy = row_to_chip(after(out_grad, gate), place)

    stream = x.astype(F32)
    kept = []
    smalls = []
    for layer in range(LAYERS):
        small = (
            gains[layer],
            shifts[layer],
            b_qkv[layer],
            b_out[layer],
            b_up[layer],
            b_down[layer],
        )
        smalls.append(small)
        stream, saved = forward_layer(stream, weights[layer], small, tables, segs, head)
        kept.append(saved)
    block_out = chip_to_rows(stream.astype(BF16), rows, place)

    dy = dy.astype(F32)
    big = [None] * LAYERS
    little = [None] * LAYERS
    for layer in reversed(range(LAYERS)):
        dy, grads, small_grads = backward_layer(
            dy,
            weights[layer],
            smalls[layer],
            kept[layer],
            tables,
            segs,
            head,
            place,
            layer % 2 == 0,
        )
        d_qkv_w, d_out, d_up, d_down = grads
        big[layer] = (
            join_columns(d_qkv_w, head_cols, place),
            join_rows(d_out, place),
            join_columns(d_up, ff_cols, place),
            join_rows(d_down, place),
        )
        little[layer] = reduce_small(small_grads, head_cols, ff_cols, place)
    in_grad = chip_to_rows(dy.astype(BF16), rows, place).astype(F32)
    d_qkv_w, d_out_w, d_up_w, d_down_w = [
        jnp.stack([grads[i] for grads in big]) for i in range(4)
    ]
    d_gains, d_shifts, d_qkv_b, d_branch_b, d_up_b = [
        jnp.stack([grads[i] for grads in little]) for i in range(5)
    ]
    return (
        block_out,
        in_grad,
        d_gains,
        d_shifts,
        d_qkv_w,
        d_qkv_b,
        d_out_w,
        d_branch_b,
        d_up_w,
        d_up_b,
        d_down_w,
        d_branch_b,
    )


def solution(mesh):
    rep, span = mesh.shape["rep"], mesh.shape["shard"]
    fine = Mesh(mesh.devices.reshape(rep // 8, 2, 2, 2, span), (*AXES, "shard"))
    tokens = P(AXES, "shard", None)
    last = P(None, None, "shard")
    middle = P(None, "shard", None)
    vector = P(None, "shard")
    in_specs = (
        tokens,
        P(AXES, None),
        last,
        last,
        middle,
        vector,
        middle,
        vector,
        middle,
        vector,
        middle,
        vector,
        tokens,
    )
    out_specs = (
        tokens,
        tokens,
        last,
        last,
        middle,
        vector,
        middle,
        vector,
        middle,
        vector,
        middle,
        vector,
    )

    def step(*arguments):
        return on_device(span, *arguments)

    return jax.shard_map(
        step, mesh=fine, in_specs=in_specs, out_specs=out_specs, check_vma=False
    )
```

time: 2580 us -> 1310 us (0.51)
  waiting for transfers between devices: 1930 us -> 676 us
  starting transfers between devices: 2.81 us -> 184 us
  blocking collectives: 178 us -> 0 us
  Pallas kernels: 0 us -> 116 us
  matrix products: 208 us -> 102 us
  local copies, waits for them, and re-layouts: 180 us -> 122 us
  other arithmetic: 47.7 us -> 86.8 us
    reduce_scatter x8 -> x0, waiting for transfers between devices: 849 us -> none  [the longest x2 295 us: backward_layer(): lax.psum_scatter(d_down_w.astype(jnp.bfloat16), 'shard', scatter_dimensio...]
    all_gather x12 -> x0, waiting for transfers between devices: 816 us -> none  [the longest x2 275 us: fetch_forward(): lax.all_gather(down_weight[layer_idx], 'shard', axis=0, tiled=True)]
    ppermute x0 -> x146, waiting for transfers between devices: none -> 561 us  [the longest x83 369 us: swap(): return lax.ppermute(x, axis, [(0, 1), (1, 0)])]
    ppermute x0 -> x146, starting transfers between devices: none -> 184 us  [the longest x63 109 us: spin(): return lax.ppermute(x, 'shard', [(j, (j + k) % span) for j in range(span)])]
    all_gather x12 -> x0, blocking collectives: 139 us -> none  [the longest x2 32.9 us: fetch_forward(): lax.all_gather(qkv_bias[layer_idx], 'shard', axis=0, tiled=True)]
    unnamed x37 -> x1, waiting for transfers between devices: 116 us -> 0.02 us
    pallas_call x0 -> x32, Pallas kernels: none -> 116 us  [the longest x28 57.4 us: copy_call(): pl.pallas_call(kernel, out_shape=out_shape, in_specs=[pl.BlockSpec(memory...]
    dot_general x36 -> x32, matrix products: 208 us -> 102 us  [the longest x24 73.9 us: dot(): return jnp.dot(a, b, preferred_element_type=F32)]
  transfers between devices with their start and end apart: 29 -> 147, of which waited for: 24 -> 64; matrix products, arithmetic and copies ran while one was open for 13% -> 19% of each run, Pallas kernels for 0% -> 7%
where the time goes in v1:
time: 1310 us; the launch traced here: 1300 us
  waiting for transfers between devices  676 us (52%)
  starting transfers between devices  184 us (14%)
  local copies, waits for them, and re-layouts  122 us (9%)
  Pallas kernels  116 us (9%)
  matrix products  102 us (8%)
  other arithmetic  86.8 us (7%)
  between operations  17.8 us (1%)
    ppermute x83, waiting for transfers between devices, swap(): return lax.ppermute(x, axis, [(0, 1), (1, 0)])  369 us
    ppermute x63, waiting for transfers between devices, spin(): return lax.ppermute(x, 'shard', [(j, (j + k) % span) for j in range(span)])  191 us
    psum x1, waiting for transfers between devices, reduce_small(): lax.psum(jnp.concatenate([p.reshape(-1) for p in parts]), (*AXES, 'shard'))  115 us
    ppermute x63, starting transfers between devices, spin(): return lax.ppermute(x, 'shard', [(j, (j + k) % span) for j in range(span)])  109 us
    ppermute x83, starting transfers between devices, swap(): return lax.ppermute(x, axis, [(0, 1), (1, 0)])  74.6 us
    dot_general x24, matrix products, dot(): return jnp.dot(a, b, preferred_element_type=F32)  73.9 us
    pallas_call x28, Pallas kernels, copy_call(): pl.pallas_call(kernel, out_shape=out_shape, in_specs=[pl.BlockSpec(memory...  57.4 us
    unnamed x443, local copies, waits for them, and re-layouts  36.7 us
  transfers between devices with their start and end apart: 147, of which 64 were waited for; matrix products, arithmetic and copies ran while one was open for 19% of the time, Pallas kernels for 7%

profile of v1, /device:TPU:0, one launch (start us, length us, event | category | flops | bytes accessed | tf_op | source)
XLA Modules:
  0.0 1303.3 jit_solution(4254824764017423850)
XLA Ops:
  99.0 9.7 collective-permute-done.9
  117.5 18.5 %collective-permute-done.16 = bf16[64,2048]{1,0:T(8,128)(2,1)} collective-permute-done((bf16[64,2048]{1,0:T(8,128)(2,1)}, bf16[64,2048]{1,0:T(8,128)(2,1)}, u32[]{:S(2)}, u32[]{:S(2)}) %collective-permute-start.16) | collective-permute-done | bytes 262176 | tf_op jit(solution)/shard_map/ppermute | solution.py:27
  156.1 14.5 %collective-permute-done.28 = bf16[128,1024]{1,0:T(8,128)(2,1)} collective-permute-done((bf16[128,1024]{1,0:T(8,128)(2,1)}, bf16[128,1024]{1,0:T(8,128)(2,1)}, u32[]{:S(2)}, u32[]{:S(2)}) %collective-permute-start.28) | collective-permute-done | bytes 262176 | tf_op jit(solution)/shard_map/ppermute | solution.py:27
  180.4 13.2 %collective-permute-done.35 = bf16[64,1536]{1,0:T(8,128)(2,1)} collective-permute-done((bf16[64,1536]{1,0:T(8,128)(2,1)}, bf16[64,1536]{1,0:T(8,128)(2,1)}, u32[]{:S(2)}, u32[]{:S(2)}) %collective-permute-start.35) | collective-permute-done | bytes 196640 | tf_op jit(solution)/shard_map/ppermute | solution.py:27
  205.5 11.9 collective-permute-done.41
  219.9 10.4 collective-permute-done.22.refs_3_
  268.2 12.6 shard_map.222
  303.2 22.2 %collective-permute-done.26.refs_4_ = bf16[3,64,2048]{2,1,0:T(8,128)(2,1)S(1)} collective-permute-done((bf16[3,64,2048]{2,1,0:T(8,128)(2,1)S(1)}, bf16[3,64,2048]{2,1,0:T(8,128)(2,1)S(1)}, u32[]{:S(2)}, u32[]{:S(2)}) %collective-permute-start.26) | collective-permute-done | bytes 786464 | tf_op jit(solution)/shard_map/ppermute | solution.py:23
  356.5 39.4 %collective-permute-done.48.refs_4_ = bf16[3,32,1024]{2,1,0:T(8,128)(2,1)S(1)} collective-permute-done((bf16[3,32,1024]{2,1,0:T(8,128)(2,1)S(1)}, bf16[3,32,1024]{2,1,0:T(8,128)(2,1)S(1)}, u32[]{:S(2)}, u32[]{:S(2)}) %collective-permute-start.48) | collective-permute-done | bytes 196640 | tf_op jit(solution)/shard_map/ppermute | solution.py:23
  422.3 30.9 %collective-permute-done.51.refs_4_ = bf16[3,64,2048]{2,1,0:T(8,128)(2,1)} collective-permute-done((bf16[3,64,2048]{2,1,0:T(8,128)(2,1)}, bf16[3,64,2048]{2,1,0:T(8,128)(2,1)}, u32[]{:S(2)}, u32[]{:S(2)}) %collective-permute-start.51) | collective-permute-done | bytes 786464 | tf_op jit(solution)/shard_map/ppermute | solution.py:23
  457.7 11.9 collective-permute-done.57.refs_4_
  483.0 12.8 shard_map.229
  497.1 16.3 %shard_map.234 = (f32[512,512]{1,0:T(8,128)S(1)}, f32[512,512]{1,0:T(8,128)S(1)}, f32[512,512]{1,0:T(8,128)S(1)}) custom-call(bf16[512,512]{1,0:T(8,128)(2,1)S(1)} %get-tuple-element.96.refs_0_, bf16[512,512]{1,0:T(8,128)(2,1)S(1)} %get-tuple-element.95.refs_1_, bf16[512,512]{1,0:T(8,128)(2,1)S(1)} %slice.1624.refs_2_, ...), custom_call_target="tpu_custom_call" | custom-call | flops 1342177280 | bytes 5242880 | tf_op jit(solution)/shard_map/pallas_call | solution.py:357
  594.3 37.9 %collective-permute-done.107.refs_2_ = bf16[32,1024]{1,0:T(8,128)(2,1)S(1)} collective-permute-done((bf16[32,1024]{1,0:T(8,128)(2,1)S(1)}, bf16[32,1024]{1,0:T(8,128)(2,1)S(1)}, u32[]{:S(2)}, u32[]{:S(2)}) %collective-permute-start.107) | collective-permute-done | bytes 65568 | tf_op jit(solution)/shard_map/ppermute | solution.py:23
  668.1 16.5 %shard_map.235 = (f32[512,512]{1,0:T(8,128)S(1)}, f32[512,512]{1,0:T(8,128)S(1)}, f32[512,512]{1,0:T(8,128)S(1)}) custom-call(bf16[512,512]{1,0:T(8,128)(2,1)S(1)} %copy-done.31, bf16[512,512]{1,0:T(8,128)(2,1)S(1)} %copy-done.29, bf16[512,512]{1,0:T(8,128)(2,1)S(1)} %copy-done.33, bf16[512,512]{1,0:T(8,128)(2,1)S(1)} %convolution_convert_fusion.16.refs_3_, ...), custom_call_target="tpu_custom_call" | custom-call | flops 1342177280 | bytes 5242880 | tf_op jit(solution)/shard_map/pallas_call | solution.py:357
  739.0 115.3 %all-reduce.3.cloned.1.call-done = (f32[12288]{0:T(1024)}, f32[12288]{0:T(1024)}) async-done(((f32[12288]{0:T(1024)}, f32[12288]{0:T(1024)}), (f32[12288]{0:T(1024)}, f32[12288]{0:T(1024)})) %all-reduce.3.cloned.1.call-update) | async-done | bytes 98320 | tf_op jit(solution)/shard_map/psum | solution.py:513
  900.3 27.9 %collective-permute-done.97.refs_1_ = bf16[32,1024]{1,0:T(8,128)(2,1)S(1)} collective-permute-done((bf16[32,1024]{1,0:T(8,128)(2,1)S(1)}, bf16[32,1024]{1,0:T(8,128)(2,1)S(1)}, u32[]{:S(2)}, u32[]{:S(2)}) %collective-permute-start.97) | collective-permute-done | bytes 65568 | tf_op jit(solution)/shard_map/ppermute | solution.py:23
  970.6 109.4 %collective-permute-done.138 = bf16[4,128,1024]{2,1,0:T(8,128)(2,1)S(1)} collective-permute-done((bf16[4,128,1024]{2,1,0:T(8,128)(2,1)S(1)}, bf16[4,128,1024]{2,1,0:T(8,128)(2,1)S(1)}, u32[]{:S(2)}, u32[]{:S(2)}) %collective-permute-start.138) | collective-permute-done | bytes 1048608 | tf_op jit(solution)/shard_map/ppermute | solution.py:23
  1109.7 11.2 collective-permute-done.86
  1125.6 10.9 collective-permute-start.140
  1146.9 11.3 collective-permute-done.89.refs_2_
  1185.5 12.8 collective-permute-done.129
  1218.0 10.7 collective-permute-start.130
  1228.9 11.7 collective-permute-done.122
  (1018 shorter events, 685.6 us)
Async XLA Ops:
  7.2 847.0 %all-reduce.3.cloned.1.call-start = ((), (), s32[]{:S(2)}) async-start(), calls=%async_computation | async-start | bytes 196608 | tf_op jit(solution)/shard_map/psum | solution.py:513
  235.7 66.2 %collective-permute-start.25 = (bf16[3,64,2048]{2,1,0:T(8,128)(2,1)S(1)}, bf16[3,64,2048]{2,1,0:T(8,128)(2,1)S(1)}, u32[]{:S(2)}, u32[]{:S(2)}) collective-permute-start(bf16[3,64,2048]{2,1,0:T(8,128)(2,1)S(1)} %copy-done.12), channel_id=1, source_target_pairs={{0,8},{8,0},{1,9},{9,1},{2,10},{10,2},{3,11},{11,3},{4,12},{12,4},... | collective-permute-start | bytes 2359304 | tf_op jit(solution)/shard_map/ppermute | solution.py:23
  237.3 55.0 %collective-permute-start.24 = (bf16[3,64,2048]{2,1,0:T(8,128)(2,1)S(1)}, bf16[3,64,2048]{2,1,0:T(8,128)(2,1)S(1)}, u32[]{:S(2)}, u32[]{:S(2)}) collective-permute-start(bf16[3,64,2048]{2,1,0:T(8,128)(2,1)S(1)} %copy-done.12), channel_id=1, source_target_pairs={{0,16},{16,0},{1,17},{17,1},{2,18},{18,2},{3,19},{19,3},{4,20},{20... | collective-permute-start | bytes 2359304 | tf_op jit(solution)/shard_map/ppermute | solution.py:23
  251.6 84.9 %collective-permute-start.31 = (bf16[3,128,1024]{2,1,0:T(8,128)(2,1)S(1)}, bf16[3,128,1024]{2,1,0:T(8,128)(2,1)S(1)}, u32[]{:S(2)}, u32[]{:S(2)}) collective-permute-start(bf16[3,128,1024]{2,1,0:T(8,128)(2,1)S(1)} %copy-done.13), channel_id=1, source_target_pairs={{0,8},{8,0},{1,9},{9,1},{2,10},{10,2},{3,11},{11,3},{4,12},{12,4},... | collective-permute-start | bytes 2359304 | tf_op jit(solution)/shard_map/ppermute | solution.py:23
  292.2 62.6 %collective-permute-start.38 = (bf16[3,64,1536]{2,1,0:T(8,128)(2,1)S(1)}, bf16[3,64,1536]{2,1,0:T(8,128)(2,1)S(1)}, u32[]{:S(2)}, u32[]{:S(2)}) collective-permute-start(bf16[3,64,1536]{2,1,0:T(8,128)(2,1)S(1)} %pad_maximum_fusion.7.refs_1_), channel_id=1, source_target_pairs={{0,8},{8,0},{1,9},{9,1},{2,10},{10,2},{3,11},{11,3},{4,12},{12,4},... | collective-permute-start | bytes 1769480 | tf_op jit(solution)/shard_map/ppermute | solution.py:23
  336.4 62.3 %collective-permute-start.49 = (bf16[3,64,2048]{2,1,0:T(8,128)(2,1)}, bf16[3,64,2048]{2,1,0:T(8,128)(2,1)}, u32[]{:S(2)}, u32[]{:S(2)}) collective-permute-start(bf16[3,64,2048]{2,1,0:T(8,128)(2,1)} %pad_maximum_fusion.4.refs_1_), channel_id=1, source_target_pairs={{0,8},{8,0},{1,9},{9,1},{2,10},{10,2},{3,11},{11,3},{4,12},{12,4},... | collective-permute-start | bytes 2359304 | tf_op jit(solution)/shard_map/ppermute | solution.py:23
  396.0 78.3 %collective-permute-start.33 = (bf16[512,1024]{1,0:T(8,128)(2,1)}, bf16[512,1024]{1,0:T(8,128)(2,1)}, u32[]{:S(2)}, u32[]{:S(2)}) collective-permute-start(bf16[512,1024]{1,0:T(8,128)(2,1)} %add_convert_fusion.13), channel_id=1, source_target_pairs={{0,4},{4,0},{1,5},{5,1},{2,6},{6,2},{3,7},{7,3},{8,12},{12,8},{9,1... | collective-permute-start | bytes 3145736 | tf_op jit(solution)/shard_map/ppermute | solution.py:23
  399.8 57.9 %collective-permute-start.56 = (bf16[3,128,1024]{2,1,0:T(8,128)(2,1)}, bf16[3,128,1024]{2,1,0:T(8,128)(2,1)}, u32[]{:S(2)}, u32[]{:S(2)}) collective-permute-start(bf16[3,128,1024]{2,1,0:T(8,128)(2,1)} %pad_maximum_fusion.5.refs_1_), channel_id=1, source_target_pairs={{0,16},{16,0},{1,17},{17,1},{2,18},{18,2},{3,19},{19,3},{4,20},{20... | collective-permute-start | bytes 2359304 | tf_op jit(solution)/shard_map/ppermute | solution.py:23
  401.8 67.8 %collective-permute-start.57 = (bf16[3,128,1024]{2,1,0:T(8,128)(2,1)}, bf16[3,128,1024]{2,1,0:T(8,128)(2,1)}, u32[]{:S(2)}, u32[]{:S(2)}) collective-permute-start(bf16[3,128,1024]{2,1,0:T(8,128)(2,1)} %collective-permute-done.55.refs_2_), channel_id=1, source_target_pairs={{0,16},{16,0},{1,17},{17,1},{2,18},{18,2},{3,19},{19,3},{4,20},{20... | collective-permute-start | bytes 2359304 | tf_op jit(solution)/shard_map/ppermute | solution.py:23
  561.5 72.6 %collective-permute-start.68 = (bf16[512,1024]{1,0:T(8,128)(2,1)}, bf16[512,1024]{1,0:T(8,128)(2,1)}, u32[]{:S(2)}, u32[]{:S(2)}) collective-permute-start(bf16[512,1024]{1,0:T(8,128)(2,1)} %get-tuple-element.264), channel_id=1, source_target_pairs={{0,4},{4,0},{1,5},{5,1},{2,6},{6,2},{3,7},{7,3},{8,12},{12,8},{9,1... | collective-permute-start | bytes 3145736 | tf_op jit(solution)/shard_map/ppermute | solution.py:23
  563.3 132.1 %collective-permute-start.58 = (bf16[512,1024]{1,0:T(8,128)(2,1)}, bf16[512,1024]{1,0:T(8,128)(2,1)}, u32[]{:S(2)}, u32[]{:S(2)}) collective-permute-start(bf16[512,1024]{1,0:T(8,128)(2,1)} %add_convert_fusion.10), channel_id=1, source_target_pairs={{0,4},{4,0},{1,5},{5,1},{2,6},{6,2},{3,7},{7,3},{8,12},{12,8},{9,1... | collective-permute-start | bytes 3145736 | tf_op jit(solution)/shard_map/ppermute | solution.py:23
  583.7 354.8 %collective-permute-start.137 = (bf16[1024,1024]{1,0:T(8,128)(2,1)}, bf16[1024,1024]{1,0:T(8,128)(2,1)}, u32[]{:S(2)}, u32[]{:S(2)}) collective-permute-start(bf16[1024,1024]{1,0:T(8,128)(2,1)} %convolution_convert_fusion.8), channel_id=1, source_target_pairs={{0,16},{16,0},{1,17},{17,1},{2,18},{18,2},{3,19},{19,3},{4,20},{20... | collective-permute-start | bytes 6291464 | tf_op jit(solution)/shard_map/ppermute | solution.py:23
  634.0 261.0 %collective-permute-start.109 = (bf16[128,1024]{1,0:T(8,128)(2,1)S(1)}, bf16[128,1024]{1,0:T(8,128)(2,1)}, u32[]{:S(2)}, u32[]{:S(2)}) collective-permute-start(bf16[128,1024]{1,0:T(8,128)(2,1)S(1)} %bitcast.743), channel_id=1, source_target_pairs={{0,4},{4,0},{1,5},{5,1},{2,6},{6,2},{3,7},{7,3},{8,12},{12,8},{9,1... | collective-permute-start | bytes 786440 | tf_op jit(solution)/shard_map/ppermute | solution.py:23
  688.1 184.8 %collective-permute-start.92 = (bf16[256,1024]{1,0:T(8,128)(2,1)}, bf16[256,1024]{1,0:T(8,128)(2,1)}, u32[]{:S(2)}, u32[]{:S(2)}) collective-permute-start(bf16[256,1024]{1,0:T(8,128)(2,1)} %convolution_convert_fusion.14), channel_id=1, source_target_pairs={{0,16},{16,0},{1,17},{17,1},{2,18},{18,2},{3,19},{19,3},{4,20},{20... | collective-permute-start | bytes 1572872 | tf_op jit(solution)/shard_map/ppermute | solution.py:23
  697.9 173.4 %collective-permute-start.61 = (bf16[128,512]{1,0:T(8,128)(2,1)}, bf16[128,512]{1,0:T(8,128)(2,1)}, u32[]{:S(2)}, u32[]{:S(2)}) collective-permute-start(bf16[128,512]{1,0:T(8,128)(2,1)} %get-tuple-element.217), channel_id=1, source_target_pairs={{0,1},{1,2},{2,3},{3,0},{4,5},{5,6},{6,7},{7,4},{8,9},{9,10},{10,1... | collective-permute-start | bytes 393224 | tf_op jit(solution)/shard_map/ppermute | solution.py:27
  699.7 163.6 %collective-permute-start.59 = (bf16[128,512]{1,0:T(8,128)(2,1)}, bf16[128,512]{1,0:T(8,128)(2,1)S(1)}, u32[]{:S(2)}, u32[]{:S(2)}) collective-permute-start(bf16[128,512]{1,0:T(8,128)(2,1)} %get-tuple-element.220), channel_id=1, source_target_pairs={{0,3},{1,0},{2,1},{3,2},{4,7},{5,4},{6,5},{7,6},{8,11},{9,8},{10,9... | collective-permute-start | bytes 393224 | tf_op jit(solution)/shard_map/ppermute | solution.py:27
  870.7 65.3 %collective-permute-start.69 = (bf16[512,1024]{1,0:T(8,128)(2,1)}, bf16[512,1024]{1,0:T(8,128)(2,1)S(1)}, u32[]{:S(2)}, u32[]{:S(2)}) collective-permute-start(bf16[512,1024]{1,0:T(8,128)(2,1)} %get-tuple-element.143), channel_id=1, source_target_pairs={{0,4},{4,0},{1,5},{5,1},{2,6},{6,2},{3,7},{7,3},{8,12},{12,8},{9,1... | collective-permute-start | bytes 3145736 | tf_op jit(solution)/shard_map/ppermute | solution.py:23
  891.0 72.0 %collective-permute-start.83 = (bf16[512,1536]{1,0:T(8,128)(2,1)}, bf16[512,1536]{1,0:T(8,128)(2,1)S(1)}, u32[]{:S(2)}, u32[]{:S(2)}) collective-permute-start(bf16[512,1536]{1,0:T(8,128)(2,1)} %convolution_convert_fusion), channel_id=1, source_target_pairs={{0,16},{16,0},{1,17},{17,1},{2,18},{18,2},{3,19},{19,3},{4,20},{20... | collective-permute-start | bytes 4718600 | tf_op jit(solution)/shard_map/ppermute | solution.py:23
  933.3 148.8 %collective-permute-start.110 = (bf16[512,2048]{1,0:T(8,128)(2,1)}, bf16[512,2048]{1,0:T(8,128)(2,1)S(1)}, u32[]{:S(2)}, u32[]{:S(2)}) collective-permute-start(bf16[512,2048]{1,0:T(8,128)(2,1)} %convolution_convert_fusion.6), channel_id=1, source_target_pairs={{0,16},{16,0},{1,17},{17,1},{2,18},{18,2},{3,19},{19,3},{4,20},{20... | collective-permute-start | bytes 6291464 | tf_op jit(solution)/shard_map/ppermute | solution.py:23
  936.0 151.5 %collective-permute-start.119 = (bf16[512,2048]{1,0:T(8,128)(2,1)}, bf16[512,2048]{1,0:T(8,128)(2,1)S(1)}, u32[]{:S(2)}, u32[]{:S(2)}) collective-permute-start(bf16[512,2048]{1,0:T(8,128)(2,1)} %convolution_convert_fusion.4), channel_id=1, source_target_pairs={{0,8},{8,0},{1,9},{9,1},{2,10},{10,2},{3,11},{11,3},{4,12},{12,4},... | collective-permute-start | bytes 6291464 | tf_op jit(solution)/shard_map/ppermute | solution.py:23
  961.4 176.0 %collective-permute-start.128 = (bf16[1024,1024]{1,0:T(8,128)(2,1)S(1)}, bf16[1024,1024]{1,0:T(8,128)(2,1)S(1)}, u32[]{:S(2)}, u32[]{:S(2)}) collective-permute-start(bf16[1024,1024]{1,0:T(8,128)(2,1)S(1)} %copy-done.165), channel_id=1, source_target_pairs={{0,8},{8,0},{1,9},{9,1},{2,10},{10,2},{3,11},{11,3},{4,12},{12,4},... | collective-permute-start | bytes 6291464 | tf_op jit(solution)/shard_map/ppermute | solution.py:23
  964.2 115.8 %collective-permute-start.138 = (bf16[4,128,1024]{2,1,0:T(8,128)(2,1)S(1)}, bf16[4,128,1024]{2,1,0:T(8,128)(2,1)S(1)}, u32[]{:S(2)}, u32[]{:S(2)}) collective-permute-start(bf16[4,128,1024]{2,1,0:T(8,128)(2,1)S(1)} %bitcast.781), channel_id=1, source_target_pairs={{0,8},{8,0},{1,9},{9,1},{2,10},{10,2},{3,11},{11,3},{4,12},{12,4},... | collective-permute-start | bytes 3145736 | tf_op jit(solution)/shard_map/ppermute | solution.py:23
  968.0 125.8 %collective-permute-start.84 = (bf16[4,64,1536]{2,1,0:T(8,128)(2,1)S(1)}, bf16[4,64,1536]{2,1,0:T(8,128)(2,1)S(1)}, u32[]{:S(2)}, u32[]{:S(2)}) collective-permute-start(bf16[4,64,1536]{2,1,0:T(8,128)(2,1)S(1)} %bitcast.791), channel_id=1, source_target_pairs={{0,8},{8,0},{1,9},{9,1},{2,10},{10,2},{3,11},{11,3},{4,12},{12,4},... | collective-permute-start | bytes 2359304 | tf_op jit(solution)/shard_map/ppermute | solution.py:23
  1083.4 55.2 %collective-permute-start.139 = (bf16[128,1024]{1,0:T(8,128)(2,1)S(1)}, bf16[128,1024]{1,0:T(8,128)(2,1)S(1)}, u32[]{:S(2)}, u32[]{:S(2)}) collective-permute-start(bf16[128,1024]{1,0:T(8,128)(2,1)S(1)} %get-tuple-element.157), channel_id=1, source_target_pairs={{0,1},{1,2},{2,3},{3,0},{4,5},{5,6},{6,7},{7,4},{8,9},{9,10},{10,1... | collective-permute-start | bytes 786440 | tf_op jit(solution)/shard_map/ppermute | solution.py:27
  (295 other events, 4576.8 us)
Sparse Core Ops, SparseCore 0:
  735.8 118.3 all-reduce.2

commit v2 on v1

v2 whole, which is shorter than its diff:
```python
import math

import jax
import jax.numpy as jnp
from jax import lax
from jax.experimental import pallas as pl
from jax.experimental.pallas import tpu as pltpu
from jax.sharding import Mesh
from jax.sharding import PartitionSpec as P

H = 16
ROT = 16
LAYERS = 2
EPS = 1e-05
ROOT_HALF = math.sqrt(0.5)
F32 = jnp.float32
BF16 = jnp.bfloat16
AXES = ("outer", "ybit", "xbit", "core")
VMEM_LIMIT = 48 * 1024 * 1024


def swap(x, axis):
    return lax.ppermute(x, axis, [(0, 1), (1, 0)])


def spin(x, k, span):
    return lax.ppermute(x, "shard", [(j, (j + k) % span) for j in range(span)])


def dot(a, b):
    return jnp.dot(a, b, preferred_element_type=F32)


def dot_t(a, b):
    return lax.dot_general(a, b, (((1,), (1,)), ((), ())), preferred_element_type=F32)


class Place:
    def __init__(self, span):
        self.span = span
        self.z = lax.axis_index("shard")
        self.c = lax.axis_index("core")
        self.bx = lax.axis_index("xbit")
        self.by = lax.axis_index("ybit")
        self.q = 2 * self.by + self.bx
        self.scalars = jnp.stack([self.z, self.q, self.c]).astype(jnp.int32)


def from_relative(blocks, place):
    span = place.span
    order = [blocks[(-m) % span] for m in range(2 * span - 1)]
    return lax.dynamic_slice_in_dim(
        jnp.stack(order), lax.rem(span - place.z, span), span, 0
    )


def by_core(place, own, other, axis):
    return jnp.where(
        place.c == 0,
        jnp.concatenate([own, other], axis),
        jnp.concatenate([other, own], axis),
    )


def copy_call(body, out_shape, copies, operands, place):
    def kernel(scalars, *refs):
        ins, out, sems = refs[: len(operands)], refs[len(operands)], refs[-1]
        started = []
        for slot, (src, dst) in enumerate(body(scalars, ins, out)):
            copy = pltpu.make_async_copy(src, dst, sems.at[slot])
            copy.start()
            started.append(copy)
        for copy in started:
            copy.wait()

    size = 2 * math.prod(out_shape.shape) * out_shape.dtype.itemsize
    return pl.pallas_call(
        kernel,
        out_shape=out_shape,
        in_specs=[pl.BlockSpec(memory_space=pltpu.SMEM)]
        + [pl.BlockSpec(memory_space=pl.ANY)] * len(operands),
        out_specs=pl.BlockSpec(memory_space=pltpu.VMEM),
        scratch_shapes=[pltpu.SemaphoreType.DMA((copies,))],
        compiler_params=pltpu.CompilerParams(vmem_limit_bytes=VMEM_LIMIT),
        cost_estimate=pl.CostEstimate(flops=0, bytes_accessed=size, transcendentals=0),
    )(place.scalars, *operands)


def pick_columns(weights, layer, width, place):
    rows, columns = weights.shape[1:]
    count = columns // (2 * width)

    def body(scalars, ins, out):
        core = scalars[2]
        for j in range(count):
            start = pl.multiple_of((2 * j + core) * width, width)
            yield (
                ins[0].at[layer, :, pl.ds(start, width)],
                out.at[:, pl.ds(j * width, width)],
            )

    shape = jax.ShapeDtypeStruct((rows, count * width), weights.dtype)
    return copy_call(body, shape, count, [weights], place)


def pick_rows(arrays, layer, place):
    halves = [w.shape[1] // 2 for w in arrays]

    def body(scalars, ins, out):
        start = 0
        for ref, half in zip(ins, halves, strict=True):
            first = pl.multiple_of(scalars[2] * half, half)
            yield ref.at[layer, pl.ds(first, half)], out.at[pl.ds(start, half)]
            start += half

    shape = jax.ShapeDtypeStruct((sum(halves), arrays[0].shape[2]), arrays[0].dtype)
    return copy_call(body, shape, len(arrays), list(arrays), place)


def other_shards(table, place):
    span = place.span

    def body(scalars, ins, out):
        for k in range(1, span):
            source = lax.rem(scalars[0] + (span - k), span)
            for i in range(2):
                yield ins[0].at[source, i], out.at[i, k - 1]

    shape = jax.ShapeDtypeStruct((2, span - 1, *table.shape[2:]), table.dtype)
    return copy_call(body, shape, 2 * (span - 1), [table], place)


def flipped(q, flip):
    return lax.bitwise_xor(q, jnp.int32(flip))


def assemble(half, near, near_x, near_y, far_a, far_b, place):
    span = place.span
    eighth, columns = half.shape[0] // 8, half.shape[1]

    def body(scalars, ins, out):
        z, q = scalars[0], scalars[1]
        yield ins[0], out.at[z]
        for k in range(1, span):
            source = lax.rem(z + (span - k), span)
            for i in range(2):
                for flip in range(3):
                    yield ins[1 + flip].at[i, k - 1], out.at[source, flipped(q, flip), i]
                yield ins[4 + i].at[k - 1], out.at[source, flipped(q, 3), i]

    shape = jax.ShapeDtypeStruct((span, 4, 2, eighth, columns), half.dtype)
    half = half.reshape(4, 2, eighth, columns)
    operands = [half, near, near_x, near_y, far_a, far_b]
    out = copy_call(body, shape, 1 + 8 * (span - 1), operands, place)
    return out.reshape(8 * span * eighth, columns)


def weight_gradient(left, right, place):
    span = place.span
    tokens, columns = left.shape[0], right.shape[1]
    rows = left.shape[1] // span
    eighth = rows // 8

    def kernel(scalars, left_ref, right_ref, own, pass_a, pass_b, send_a, send_b, table):
        q = scalars[1]
        product = lax.dot_general(
            left_ref[...],
            right_ref[...],
            (((0,), (0,)), ((), ())),
            preferred_element_type=F32,
        ).astype(BF16)
        for j in range(8):
            table[j // 2, j % 2] = product[j * eighth : (j + 1) * eighth]
        near_x, near_y, far = flipped(q, 1), flipped(q, 2), flipped(q, 3)
        own[0, 0], own[0, 1] = table[q, 0], table[q, 1]
        pass_a[0], pass_b[0] = table[near_y, 0], table[near_x, 1]
        send_a[0, 0], send_a[1, 0] = table[near_x, 0], table[far, 0]
        send_b[0, 0], send_b[1, 0] = table[near_y, 1], table[far, 1]

    block = (eighth, columns)
    one = pl.BlockSpec((1, *block), lambda k, s: (k, 0, 0))
    two = pl.BlockSpec((2, 1, *block), lambda k, s: (0, k, 0, 0))
    return pl.pallas_call(
        kernel,
        grid_spec=pltpu.PrefetchScalarGridSpec(
            num_scalar_prefetch=1,
            grid=(span,),
            in_specs=[
                pl.BlockSpec((tokens, rows), lambda k, s: (0, lax.rem(s[0] + k, span))),
                pl.BlockSpec((tokens, columns), lambda k, s: (0, 0)),
            ],
            out_specs=[
                pl.BlockSpec((1, 2, *block), lambda k, s: (k, 0, 0, 0)),
                one,
                one,
                two,
                two,
            ],
            scratch_shapes=[pltpu.VMEM((4, 2, *block), BF16)],
        ),
        out_shape=[
            jax.ShapeDtypeStruct((span, 2, *block), BF16),
            jax.ShapeDtypeStruct((span, *block), BF16),
            jax.ShapeDtypeStruct((span, *block), BF16),
            jax.ShapeDtypeStruct((2, span, *block), BF16),
            jax.ShapeDtypeStruct((2, span, *block), BF16),
        ],
        compiler_params=pltpu.CompilerParams(vmem_limit_bytes=VMEM_LIMIT),
        cost_estimate=pl.CostEstimate(
            flops=2 * tokens * span * rows * columns,
            bytes_accessed=2 * (tokens * (span * rows + columns) + span * rows * columns),
            transcendentals=0,
        ),
    )(place.scalars, left, right)


def combine(own, got_a, got_b, more_a, more_b):
    span, _, eighth, columns = own.shape
    part = columns // 4 if columns % 512 == 0 else columns

    def kernel(own_ref, ga_ref, gb_ref, ma_ref, mb_ref, *outs):
        for k in range(span):
            for i, (got, more) in enumerate(((ga_ref, ma_ref), (gb_ref, mb_ref))):
                total = own_ref[k, i].astype(F32) + got[0, k].astype(F32)
                outs[k][i] = (total + more[k].astype(F32)).astype(BF16)

    got = pl.BlockSpec((1, span, eighth, part), lambda j: (0, 0, 0, j))
    more = pl.BlockSpec((span, eighth, part), lambda j: (0, 0, j))
    out = pl.BlockSpec((2, eighth, part), lambda j: (0, 0, j))
    return pl.pallas_call(
        kernel,
        grid=(columns // part,),
        in_specs=[
            pl.BlockSpec((span, 2, eighth, part), lambda j: (0, 0, 0, j)),
            got,
            got,
            more,
            more,
        ],
        out_specs=[out] * span,
        out_shape=[jax.ShapeDtypeStruct((2, eighth, columns), BF16)] * span,
        compiler_params=pltpu.CompilerParams(vmem_limit_bytes=VMEM_LIMIT),
        cost_estimate=pl.CostEstimate(
            flops=4 * span * eighth * columns,
            bytes_accessed=16 * span * eighth * columns,
            transcendentals=0,
        ),
    )(own, got_a, got_b, more_a, more_b)


def finish_columns(parts, width, layer, previous):
    _, _, rows, columns = parts.shape

    def kernel(part_ref, *rest):
        out_ref = rest[-1]
        for core in range(2):
            for j in range(columns // width):
                start = (2 * j + core) * width
                out_ref[0, :, start : start + width] = part_ref[
                    0, core, :, j * width : (j + 1) * width
                ].astype(F32)

    operands, in_specs, aliases = (
        [parts],
        [pl.BlockSpec((1, 2, rows, columns), lambda q: (q, 0, 0, 0))],
        {},
    )
    if previous is not None:
        operands.append(previous)
        in_specs.append(pl.BlockSpec(memory_space=pl.ANY))
        aliases = {1: 0}
    return pl.pallas_call(
        kernel,
        grid=(4,),
        in_specs=in_specs,
        out_specs=pl.BlockSpec((1, rows, 2 * columns), lambda q: (layer, q, 0)),
        out_shape=jax.ShapeDtypeStruct((LAYERS, 4 * rows, 2 * columns), F32),
        input_output_aliases=aliases,
        compiler_params=pltpu.CompilerParams(vmem_limit_bytes=VMEM_LIMIT),
        cost_estimate=pl.CostEstimate(
            flops=0, bytes_accessed=48 * rows * columns, transcendentals=0
        ),
    )(*operands)


def finish_rows(parts, first_rows, layer, previous):
    _, _, quarter, columns = parts.shape
    sizes = (first_rows, 4 * quarter - first_rows)

    def kernel(part_ref, *rest):
        first, second = rest[-2:]
        for q in range(4):
            start, stop = q * quarter, (q + 1) * quarter
            cut = min(max(first_rows, start), stop)
            if cut > start:
                first[0, :, start:cut] = part_ref[q, :, : cut - start].astype(F32)
            if stop > cut:
                second[0, :, cut - first_rows : stop - first_rows] = part_ref[
                    q, :, cut - start :
                ].astype(F32)

    half = columns // 4 if columns % 512 == 0 else columns
    operands, aliases = [parts], {}
    in_specs = [pl.BlockSpec((4, 2, quarter, half), lambda j: (0, 0, 0, j))]
    if previous is not None:
        operands += list(previous)
        in_specs += [pl.BlockSpec(memory_space=pl.ANY)] * 2
        aliases = {1: 0, 2: 1}
    return pl.pallas_call(
        kernel,
        grid=(columns // half,),
        in_specs=in_specs,
        out_specs=[
            pl.BlockSpec((1, 2, size, half), lambda j: (layer, 0, 0, j)) for size in sizes
        ],
        out_shape=[
            jax.ShapeDtypeStruct((LAYERS, 2, size, columns), F32) for size in sizes
        ],
        input_output_aliases=aliases,
        compiler_params=pltpu.CompilerParams(vmem_limit_bytes=VMEM_LIMIT),
        cost_estimate=pl.CostEstimate(
            flops=0, bytes_accessed=48 * quarter * columns, transcendentals=0
        ),
    )(*operands)


def row_to_chip(x, place):
    span = place.span
    rows, tokens, width = x.shape
    half = width // 2
    mine = lax.dynamic_slice_in_dim(x, place.c * half, half, 2)
    theirs = lax.dynamic_slice_in_dim(x, (1 - place.c) * half, half, 2)
    rows_all = by_core(place, mine, swap(theirs, "core"), 0)
    blocks = []
    for k in range(span):
        block = lax.dynamic_index_in_dim(
            rows_all, lax.rem(place.z + k, span), 0, keepdims=False
        )
        blocks.append(block if k == 0 else spin(block, k, span))
    own = from_relative(blocks, place).reshape(span * tokens, half)
    return by_core(place, own, swap(own, "core"), 1)


def chip_to_rows(y, rows, place):
    span = place.span
    width = y.shape[1]
    tokens = y.shape[0] // span
    half = width // 2
    mine = lax.dynamic_slice_in_dim(y, place.c * half, half, 1)
    mine = mine.reshape(span, tokens, half)
    blocks = []
    for k in range(span):
        block = lax.dynamic_index_in_dim(
            mine, lax.rem(place.z + k, span), 0, keepdims=False
        )
        blocks.append(block if k == 0 else spin(block, k, span))
    stacked = from_relative(blocks, place)
    own = lax.dynamic_slice_in_dim(stacked, place.c * rows, rows, 0)
    theirs = lax.dynamic_slice_in_dim(stacked, (1 - place.c) * rows, rows, 0)
    return by_core(place, own, swap(theirs, "core"), 2)


class Slots:
    def __init__(self):
        self.parts = []

    def add(self, part, done):
        self.parts.append([part, next(part), done])

    def step(self, extra=()):
        pending, extra = lax.optimization_barrier(
            ([part[1] for part in self.parts], extra)
        )
        alive = []
        for part, arrived in zip(self.parts, pending, strict=True):
            try:
                part[1] = part[0].send(arrived)
                alive.append(part)
            except StopIteration as end:
                part[2](end.value)
        self.parts = alive
        return extra


def gather_weight(half, place):
    eighth, columns = half.shape[0] // 8, half.shape[1]
    mine = lax.dynamic_index_in_dim(
        half.reshape(4, 2, eighth, columns), place.q, 0, keepdims=False
    )
    mine = yield mine
    every = yield lax.all_gather(mine, "shard")
    near = other_shards(every, place)
    near_x, near_y = yield [swap(near, "xbit"), swap(near, "ybit")]
    far_a, far_b = yield [swap(near_x[0], "ybit"), swap(near_y[1], "xbit")]
    return assemble(half, near, near_x, near_y, far_a, far_b, place)


def reduce_weight(left, right, place):
    span = place.span
    own, pass_a, pass_b, send_a, send_b = yield weight_gradient(left, right, place)
    got_a, got_b = yield [swap(send_a, "xbit"), swap(send_b, "ybit")]
    onward_a = (pass_a.astype(F32) + got_a[1].astype(F32)).astype(BF16)
    onward_b = (pass_b.astype(F32) + got_b[1].astype(F32)).astype(BF16)
    more_a, more_b = yield [swap(onward_a, "ybit"), swap(onward_b, "xbit")]
    total = combine(own, got_a, got_b, more_a, more_b)
    arrived = yield [spin(total[k], k, span) for k in range(1, span)]
    summed = total[0].astype(F32)
    for other in arrived:
        summed = summed + other.astype(F32)
    summed = summed.astype(BF16)
    if lax.axis_size("outer") > 1:
        summed = lax.psum(summed, "outer")
    parts = lax.all_gather(summed, ("ybit", "xbit", "core"))
    _, eighth, columns = summed.shape
    return parts.reshape(4, 2, 2 * eighth, columns)


def gather_small(vectors, place):
    flat = jnp.concatenate([v.reshape(-1) for v in vectors])
    blocks = [flat] + [spin(flat, k, place.span) for k in range(1, place.span)]
    table = from_relative(blocks, place)
    out, start = [], 0
    for v in vectors:
        part = table[:, start : start + v.size].reshape(place.span, *v.shape)
        start += v.size
        part = jnp.moveaxis(part, 0, -2)
        out.append(part.reshape(*v.shape[:-1], -1).astype(F32))
    return out


def blocks_of(length):
    step = 128 if length % 128 == 0 else length
    return [(i * step, step) for i in range(length // step)]


def seen(seg_col, seg_row, start, step):
    stop = start + step
    row = start + lax.broadcasted_iota(jnp.int32, (step, stop), 0)
    col = lax.broadcasted_iota(jnp.int32, (step, stop), 1)
    return (col <= row) & (seg_col[start:stop, :] == seg_row[:, :stop])


def turn(u, tables):
    keep, upper, lower = tables
    half, lanes = ROT // 2, u.shape[1]
    return u * keep + pltpu.roll(u, lanes - half, 1) * upper + pltpu.roll(u, half, 1) * lower


def turn_back(d, tables):
    keep, upper, lower = tables
    half, lanes = ROT // 2, d.shape[1]
    return d * keep + pltpu.roll(d * upper, half, 1) + pltpu.roll(d * lower, lanes - half, 1)


def attend_kernel(scale, head, *refs):
    q_in, k_in, v_in, keep, upper, lower, seg_col, seg_row = refs[:8]
    q_ref, k_ref, v_ref, o_ref, lse_ref = refs[8:]
    tables = keep[...], upper[...], lower[...]
    q_ref[...] = turn(q_in[...], tables).astype(BF16)
    k_ref[...] = turn(k_in[...], tables).astype(BF16)
    v_ref[...] = v_in[...].astype(BF16)
    for start, step in blocks_of(q_ref.shape[0]):
        stop = start + step
        mask = seen(seg_col, seg_row, start, step)
        for h in range(q_ref.shape[1] // head):
            lanes = slice(h * head, (h + 1) * head)
            scores = dot_t(q_ref[start:stop, lanes], k_ref[:stop, lanes]) * scale
            scores = jnp.where(mask, scores, -1e30)
            top = jnp.max(scores, -1, keepdims=True)
            expo = jnp.exp(scores - top)
            total = jnp.sum(expo, -1, keepdims=True)
            probs = (expo * (1.0 / total)).astype(BF16)
            o_ref[start:stop, lanes] = dot(probs, v_ref[:stop, lanes]).astype(BF16)
            lse_ref[h, start:stop, :] = top + jnp.log(total)


def attend_back_kernel(scale, head, *refs):
    q_ref, k_ref, v_ref, do_ref, lse_ref, keep, upper, lower, seg_col, seg_row = refs[:10]
    dq_out, dk_out, dv_out, dq_ref, dk_ref, dv_ref = refs[10:]
    dk_ref[...] = jnp.zeros_like(dk_ref)
    dv_ref[...] = jnp.zeros_like(dv_ref)
    over_rows = (((0,), (0,)), ((), ()))
    for start, step in blocks_of(q_ref.shape[0]):
        stop = start + step
        mask = seen(seg_col, seg_row, start, step)
        for h in range(q_ref.shape[1] // head):
            lanes = slice(h * head, (h + 1) * head)
            query = q_ref[start:stop, lanes]
            keys = k_ref[:stop, lanes]
            grad = do_ref[start:stop, lanes]
            scores = dot_t(query, keys) * scale
            probs = jnp.exp(jnp.where(mask, scores - lse_ref[h, start:stop, :], -1e30))
            d_probs = dot_t(grad, v_ref[:stop, lanes])
            delta = jnp.sum(probs * d_probs, -1, keepdims=True)
            d_scores = (probs * (d_probs - delta)).astype(BF16)
            dq_ref[start:stop, lanes] = dot(d_scores, keys) * scale
            dk_ref[:stop, lanes] += (
                lax.dot_general(d_scores, query, over_rows, preferred_element_type=F32) * scale
            )
            dv_ref[:stop, lanes] += lax.dot_general(
                probs.astype(BF16), grad, over_rows, preferred_element_type=F32
            )
    tables = keep[...], upper[...], lower[...]
    dq_out[...] = turn_back(dq_ref[...], tables).astype(BF16)
    dk_out[...] = turn_back(dk_ref[...], tables).astype(BF16)
    dv_out[...] = dv_ref[...].astype(BF16)


def attention_specs(length, width, head):
    group = max(head, 128)
    count = width // group
    wide = pl.BlockSpec((length, group), lambda i: (0, i))
    lse = pl.BlockSpec((group // head, length, 1), lambda i: (i, 0, 0))
    same = [pl.BlockSpec((length, group), lambda i: (0, 0))] * 3 + [
        pl.BlockSpec((length, 1), lambda i: (0, 0)),
        pl.BlockSpec((1, length), lambda i: (0, 0)),
    ]
    return group, count, wide, lse, same


def attend(projected, fixed, head):
    length, width = projected.shape[0], projected.shape[1] // 3
    group, count, wide, lse, same = attention_specs(length, width, head)

    def kernel(*refs):
        attend_kernel(1.0 / math.sqrt(head), head, *refs)

    low = jax.ShapeDtypeStruct((length, width), BF16)
    return pl.pallas_call(
        kernel,
        grid=(count,),
        in_specs=[
            wide,
            pl.BlockSpec((length, group), lambda i: (0, count + i)),
            pl.BlockSpec((length, group), lambda i: (0, 2 * count + i)),
            *same,
        ],
        out_specs=[wide, wide, wide, wide, lse],
        out_shape=[
            low,
            low,
            low,
            low,
            jax.ShapeDtypeStruct((width // head, length, 1), F32),
        ],
        compiler_params=pltpu.CompilerParams(vmem_limit_bytes=VMEM_LIMIT),
        cost_estimate=pl.CostEstimate(
            flops=4 * length * length * width,
            bytes_accessed=20 * length * width,
            transcendentals=width // head * length * length,
        ),
    )(projected, projected, projected, *fixed)


def attend_back(query, keys, values, d_mixed, lse_all, fixed, head):
    length, width = query.shape
    group, count, wide, lse, same = attention_specs(length, width, head)

    def kernel(*refs):
        attend_back_kernel(1.0 / math.sqrt(head), head, *refs)

    out = jax.ShapeDtypeStruct((length, width), BF16)
    return pl.pallas_call(
        kernel,
        grid=(count,),
        in_specs=[wide, wide, wide, wide, lse, *same],
        out_specs=[wide, wide, wide],
        out_shape=[out, out, out],
        scratch_shapes=[pltpu.VMEM((length, group), F32)] * 3,
        compiler_params=pltpu.CompilerParams(vmem_limit_bytes=VMEM_LIMIT),
        cost_estimate=pl.CostEstimate(
            flops=10 * length * length * width,
            bytes_accessed=20 * length * width,
            transcendentals=width // head * length * length,
        ),
    )(query, keys, values, d_mixed, lse_all, *fixed)


def rotary_tables(positions, head):
    half = ROT // 2
    inverse = jnp.power(10000.0, -2.0 * jnp.arange(half, dtype=F32) / ROT)
    angles = positions.astype(F32)[:, None] * inverse
    cos, sin = jnp.cos(angles), jnp.sin(angles)
    rest = jnp.zeros((positions.shape[0], head - ROT), F32)
    none = jnp.zeros_like(sin)
    keep = [cos, cos, rest + 1.0]
    upper = [-sin, none, rest]
    lower = [none, sin, rest]
    times = max(1, 128 // head)
    return [jnp.concatenate(t * times, 1) for t in (keep, upper, lower)]


def normalise(x):
    centred = x - jnp.mean(x, -1, keepdims=True)
    spread = jnp.mean(centred * centred, -1, keepdims=True)
    inverse = lax.rsqrt(spread + EPS)
    return centred * inverse, inverse


def interleave(first, second, span):
    a, b = first.shape[1] // span, second.shape[1] // span
    parts = []
    for k in range(span):
        parts += [first[:, k * a : (k + 1) * a], second[:, k * b : (k + 1) * b]]
    return jnp.concatenate(parts, 1)


def separate(both, a, b, span):
    parts = [both[:, k * (a + b) : (k + 1) * (a + b)] for k in range(span)]
    first = jnp.concatenate([p[:, :a] for p in parts], 1)
    return first, jnp.concatenate([p[:, a:] for p in parts], 1)


def forward_layer(x, weights, small, fixed, head, span):
    w_qkv, w_up, w_last = weights
    gains, shifts, b_qkv, b_out, b_up, b_down = small
    xhat, inverse = normalise(x)
    attn_low = (xhat * gains[0] + shifts[0]).astype(BF16)
    mlp_low = (xhat * gains[1] + shifts[1]).astype(BF16)
    projected = dot(attn_low, w_qkv) + b_qkv
    query, keys, values, mixed_low, lse = attend(projected, fixed, head)
    hidden_pre = dot(mlp_low, w_up) + b_up
    cdf = 0.5 * (1.0 + lax.erf(hidden_pre * ROOT_HALF))
    hidden_low = (hidden_pre * cdf).astype(BF16)
    last_low = interleave(mixed_low, hidden_low, span)
    part = dot(last_low, w_last).astype(BF16)
    other = swap(part, "core")
    y = x + (part.astype(F32) + other.astype(F32) + b_out + b_down)
    attention = (query, keys, values, lse)
    return y, (xhat, inverse, attn_low, mlp_low, attention, hidden_pre, last_low)


def backward_layer(dy, weights, small, saved, fixed, head, place, slots, done):
    w_qkv, w_up, w_last = weights
    gains = small[0]
    xhat, inverse, attn_low, mlp_low, attention, hidden_pre, last_low = saved
    query, keys, values, lse = attention
    span = place.span
    dy_low = dy.astype(BF16)
    slots.add(reduce_weight(last_low, dy_low, place), done(2))
    d_branch_b = jnp.sum(dy_low.astype(F32), 0)

    dy_low = slots.step(dy_low)
    d_mixed, d_hidden = separate(
        dot_t(dy_low, w_last), query.shape[1] // span, hidden_pre.shape[1] // span, span
    )
    d_mixed = d_mixed.astype(BF16)
    cdf = 0.5 * (1.0 + lax.erf(hidden_pre * ROOT_HALF))
    density = jnp.exp(-0.5 * hidden_pre * hidden_pre) * (1.0 / math.sqrt(2.0 * math.pi))
    d_pre = (d_hidden * (cdf + hidden_pre * density)).astype(BF16)
    slots.add(reduce_weight(mlp_low, d_pre, place), done(1))
    d_up_b = jnp.sum(d_pre.astype(F32), 0)

    d_mixed, d_pre = slots.step((d_mixed, d_pre))
    d_qkv = jnp.concatenate(
        attend_back(query, keys, values, d_mixed, lse, fixed, head), 1
    )
    slots.add(reduce_weight(attn_low, d_qkv, place), done(0))
    d_mlp = dot_t(d_pre, w_up)

    d_qkv, d_mlp = slots.step((d_qkv, d_mlp))
    d_qkv_b = jnp.sum(d_qkv.astype(F32), 0)
    d_attn = dot_t(d_qkv, w_qkv)
    part = (d_attn * gains[0] + d_mlp * gains[1]).astype(BF16)
    d_xhat = part.astype(F32) + swap(part, "core").astype(F32)
    dx = dy + inverse * (
        d_xhat
        - jnp.mean(d_xhat, -1, keepdims=True)
        - xhat * jnp.mean(d_xhat * xhat, -1, keepdims=True)
    )
    d_gains = jnp.stack([jnp.sum(d_attn * xhat, 0), jnp.sum(d_mlp * xhat, 0)])
    d_shifts = jnp.stack([jnp.sum(d_attn, 0), jnp.sum(d_mlp, 0)])
    return dx, (d_gains, d_shifts, d_qkv_b, d_branch_b, d_up_b)


def pick_vector(v, width, place):
    return jnp.take(v.reshape(*v.shape[:-1], -1, 2, width), place.c, axis=-2).reshape(
        *v.shape[:-1], -1
    )


def spread_vector(v, width, place):
    blocks = v.reshape(-1, 1, width)
    here = (jnp.arange(2) == place.c)[None, :, None]
    return jnp.where(here, blocks, 0.0).reshape(-1)


def reduce_small(layers, head_cols, ff_cols, place):
    span = place.span
    parts = []
    for d_gains, d_shifts, d_qkv_b, d_branch_b, d_up_b in layers:
        parts += [
            d_gains,
            d_shifts,
            spread_vector(d_qkv_b, head_cols, place),
            jnp.where(place.c == 0, d_branch_b, 0.0),
            spread_vector(d_up_b, ff_cols, place),
        ]
    tables = [p.reshape(-1, span, p.shape[-1] // span) for p in parts]
    flat = jnp.concatenate(
        [jnp.moveaxis(t, 1, 0).reshape(span, -1, 128) for t in tables], 1
    )
    for axis in ("core", "xbit", "ybit"):
        flat = flat + swap(flat, axis)
    if lax.axis_size("outer") > 1:
        flat = lax.psum(flat, "outer")
    mine = [
        lax.dynamic_index_in_dim(flat, lax.rem(place.z + k, span), 0, keepdims=False)
        for k in range(span)
    ]
    total = mine[0]
    for k in range(1, span):
        total = total + spin(mine[k], k, span)
    total = total.reshape(-1)
    out, start = [], 0
    for p in parts:
        size = p.size // span
        out.append(total[start : start + size].reshape(*p.shape[:-1], p.shape[-1] // span))
        start += size
    count = len(parts) // len(layers)
    return [jnp.stack(out[i::count]) for i in range(count)]


def on_device(span, *arguments):
    (
        hidden_in,
        segments,
        norm_gains,
        norm_biases,
        qkv_weight,
        qkv_bias,
        out_weight,
        out_bias,
        up_weight,
        up_bias,
        down_weight,
        down_bias,
        out_grad,
    ) = arguments
    place = Place(span)
    rows = hidden_in.shape[0]
    width = hidden_in.shape[2]
    head = width // H
    head_cols = width // (2 * span)
    ff_cols = up_weight.shape[2] // (2 * span)
    assert 2 * rows == span

    halves = []
    for layer in range(LAYERS):
        halves += [
            pick_columns(qkv_weight, layer, head_cols, place),
            pick_columns(up_weight, layer, ff_cols, place),
            pick_rows((out_weight, down_weight), layer, place),
        ]
    gathered = [None] * len(halves)
    slots = Slots()
    for index in range(len(halves) + 3):
        if index < len(halves):

            def arrived(value, index=index):
                gathered[index] = value

            slots.add(gather_weight(halves[index], place), arrived)
        slots.step()
    weights = [gathered[3 * layer : 3 * layer + 3] for layer in range(LAYERS)]

    both = row_to_chip(jnp.concatenate([hidden_in, out_grad], 2), place)
    stream, dy = both[:, :width].astype(F32), both[:, width:].astype(F32)
    seg_all = by_core(place, segments, swap(segments, "core"), 0)
    seg = lax.dynamic_index_in_dim(seg_all, place.z, 0, keepdims=False)
    seg_col, seg_row = seg[:, None], seg[None, :]
    length = seg.shape[0]
    earlier = jnp.sum((seg_row < seg_col).astype(jnp.int32), -1)
    positions = jnp.arange(length, dtype=jnp.int32) - earlier
    fixed = (*rotary_tables(positions, head), seg_col, seg_row)

    small = gather_small(
        [norm_gains, norm_biases, qkv_bias, out_bias, up_bias, down_bias], place
    )
    gains, shifts, b_qkv, b_out, b_up, b_down = small
    b_qkv = pick_vector(b_qkv, head_cols, place)
    b_up = pick_vector(b_up, ff_cols, place)
    smalls = [
        (gains[i], shifts[i], b_qkv[i], b_out[i], b_up[i], b_down[i]) for i in range(LAYERS)
    ]

    kept = []
    for layer in range(LAYERS):
        stream, saved = forward_layer(
            stream, weights[layer], smalls[layer], fixed, head, span
        )
        kept.append(saved)

    big = [None] * 3
    little = [None] * LAYERS
    slots = Slots()

    def done_for(layer):
        def of(index):
            def done(parts):
                if index == 2:
                    first_rows = out_weight.shape[1] // 2
                    big[2] = finish_rows(parts, first_rows, layer, big[2])
                else:
                    by = (head_cols, ff_cols)[index]
                    big[index] = finish_columns(parts, by, layer, big[index])

            return done

        return of

    for layer in reversed(range(LAYERS)):
        dy, little[layer] = backward_layer(
            dy,
            weights[layer],
            smalls[layer],
            kept[layer],
            fixed,
            head,
            place,
            slots,
            done_for(layer),
        )
    while slots.parts:
        slots.step()
    results = jnp.concatenate([stream.astype(BF16), dy.astype(BF16)], 1)
    results = chip_to_rows(results, rows, place)
    block_out, in_grad = results[..., :width], results[..., width:].astype(F32)
    d_gains, d_shifts, d_qkv_b, d_branch_b, d_up_b = reduce_small(
        little, head_cols, ff_cols, place
    )
    d_qkv_w, d_up_w, (d_out_w, d_down_w) = big
    d_out_w = d_out_w.reshape(LAYERS, -1, width)
    d_down_w = d_down_w.reshape(LAYERS, -1, width)
    return (
        block_out,
        in_grad,
        d_gains,
        d_shifts,
        d_qkv_w,
        d_qkv_b,
        d_out_w,
        d_branch_b,
        d_up_w,
        d_up_b,
        d_down_w,
        d_branch_b,
    )


def solution(mesh):
    rep, span = mesh.shape["rep"], mesh.shape["shard"]
    fine = Mesh(mesh.devices.reshape(rep // 8, 2, 2, 2, span), (*AXES, "shard"))
    tokens = P(AXES, "shard", None)
    last = P(None, None, "shard")
    middle = P(None, "shard", None)
    vector = P(None, "shard")
    in_specs = (
        tokens,
        P(AXES, None),
        last,
        last,
        middle,
        vector,
        middle,
        vector,
        middle,
        vector,
        middle,
        vector,
        tokens,
    )
    out_specs = (
        tokens,
        tokens,
        last,
        last,
        middle,
        vector,
        middle,
        vector,
        middle,
        vector,
        middle,
        vector,
    )

    def step(*arguments):
        return on_device(span, *arguments)

    return jax.shard_map(
        step, mesh=fine, in_specs=in_specs, out_specs=out_specs, check_vma=False
    )
```

time: 1310 us -> 812 us (0.62)
  waiting for transfers between devices: 676 us -> 198 us
  starting transfers between devices: 184 us -> 112 us
  Pallas kernels: 116 us -> 181 us
  blocking collectives: 0 us -> 36 us
  matrix products: 102 us -> 69.3 us
  other arithmetic: 86.8 us -> 70 us
    ppermute x83 -> x59, waiting for transfers between devices: 369 us -> 78.6 us  [swap(): return lax.ppermute(x, axis, [(0, 1), (1, 0)])]
    psum x1 -> x0, waiting for transfers between devices: 115 us -> none  [reduce_small(): lax.psum(jnp.concatenate([p.reshape(-1) for p in parts]), (*AXES, 'shard'))]
    ppermute x63 -> x30, waiting for transfers between devices: 191 us -> 106 us  [spin(): return lax.ppermute(x, 'shard', [(j, (j + k) % span) for j in range(span)])]
    pallas_call x4 -> x22, Pallas kernels: 58.1 us -> 127 us  [the longest x6 34 us: weight_gradient(): pl.pallas_call(kernel, grid_spec=pltpu.PrefetchScalarGridSpec(num_scalar_...]
    ppermute x63 -> x30, starting transfers between devices: 109 us -> 57.5 us  [spin(): return lax.ppermute(x, 'shard', [(j, (j + k) % span) for j in range(span)])]
    unnamed x443 -> x397, local copies, waits for them, and re-layouts: 36.7 us -> 75 us
    all_gather x0 -> x2, blocking collectives: none -> 36 us  [gather_weight(): every = (yield lax.all_gather(mine, 'shard'))]
    dot_general x24 -> x6, matrix products: 73.9 us -> 37.9 us  [dot(): return jnp.dot(a, b, preferred_element_type=F32)]
  transfers between devices with their start and end apart: 147 -> 99, of which waited for: 64 -> 32; matrix products, arithmetic and copies ran while one was open for 19% -> 22% of each run, Pallas kernels for 7% -> 20%
where the time goes in v2:
time: 812 us; the launch traced here: 803 us
  waiting for transfers between devices  198 us (24%)
  Pallas kernels  181 us (22%)
  local copies, waits for them, and re-layouts  121 us (15%)
  starting transfers between devices  112 us (14%)
  other arithmetic  70 us (9%)
  matrix products  69.3 us (9%)
  blocking collectives  36 us (4%)
  between operations  17 us (2%)
    ppermute x30, waiting for transfers between devices, spin(): return lax.ppermute(x, 'shard', [(j, (j + k) % span) for j in range(span)])  106 us
    ppermute x59, waiting for transfers between devices, swap(): return lax.ppermute(x, axis, [(0, 1), (1, 0)])  78.6 us
    unnamed x397, local copies, waits for them, and re-layouts  75 us
    ppermute x30, starting transfers between devices, spin(): return lax.ppermute(x, 'shard', [(j, (j + k) % span) for j in range(span)])  57.5 us
    pallas_call x18, Pallas kernels, copy_call(): pl.pallas_call(kernel, out_shape=out_shape, in_specs=[pl.BlockSpec(memory...  53.7 us
    ppermute x59, starting transfers between devices, swap(): return lax.ppermute(x, axis, [(0, 1), (1, 0)])  53.1 us
    dot_general x6, matrix products, dot(): return jnp.dot(a, b, preferred_element_type=F32)  37.9 us
    all_gather x2, blocking collectives, gather_weight(): every = (yield lax.all_gather(mine, 'shard'))  36 us
  transfers between devices with their start and end apart: 99, of which 32 were waited for; matrix products, arithmetic and copies ran while one was open for 22% of the time, Pallas kernels for 20%

profile of v2, /device:TPU:0, one launch (start us, length us, event | category | flops | bytes accessed | tf_op | source)
XLA Modules:
  0.0 803.0 jit_solution(17255558217411301404)
XLA Ops:
  21.8 18.4 %all-gather = bf16[8,32,1536]{2,1,0:T(8,128)(2,1)} all-gather(bf16[2,32,1536]{2,1,0:T(8,128)(2,1)S(1)} %dynamic-slice_bitcast_fusion.11), channel_id=2, replica_groups=mesh['outer'=1,'ybit'=2,'xbit'=2,'core'=2,'shard'=4] {'shard'}, dimensions={0}, use_global_device_ids=true | all-gather | bytes 983040 | tf_op jit(solution)/shard_map/all_gather | solution.py:391
  97.6 13.3 %collective-permute-done.2 = bf16[128,1024]{1,0:T(8,128)(2,1)} collective-permute-done((bf16[128,1024]{1,0:T(8,128)(2,1)}, bf16[128,1024]{1,0:T(8,128)(2,1)}, u32[]{:S(2)}, u32[]{:S(2)}) %collective-permute-start.2) | collective-permute-done | bytes 262176 | tf_op jit(solution)/shard_map/ppermute | solution.py:27
  136.9 14.4 %collective-permute-done.11.refs_5_ = bf16[3,32,1536]{2,1,0:T(8,128)(2,1)S(1)} collective-permute-done((bf16[3,32,1536]{2,1,0:T(8,128)(2,1)S(1)}, bf16[3,32,1536]{2,1,0:T(8,128)(2,1)S(1)}, u32[]{:S(2)}, u32[]{:S(2)}) %collective-permute-start.11) | collective-permute-done | bytes 294944 | tf_op jit(solution)/shard_map/ppermute | solution.py:23
  176.9 14.7 %shard_map.227 = (bf16[512,512]{1,0:T(8,128)(2,1)S(1)}, bf16[512,512]{1,0:T(8,128)(2,1)S(1)}, bf16[512,512]{1,0:T(8,128)(2,1)S(1)}, bf16[512,512]{1,0:T(8,128)(2,1)S(1)}, f32[8,512,1]{2,1,0:T(8,128)S(1)}) custom-call(f32[512,1536]{1,0:T(8,128)} %convolution_add_fusion.1.refs_0_.refs_1_.refs_2_, f32[512,1536]{1,0:T(8,128)} %convolution_add_fusion.1.refs_0_.refs_1_.refs_2_, ...), custom_call_target="tpu_custom_call" | custom-call | flops 536870912 | bytes 5242880 | tf_op jit(solution)/shard_map/pallas_call | solution.py:529
  193.8 17.6 %all-gather.3 = bf16[8,32,1536]{2,1,0:T(8,128)(2,1)S(1)} all-gather(bf16[2,32,1536]{2,1,0:T(8,128)(2,1)S(1)} %copy-done.135), channel_id=5, replica_groups=mesh['outer'=1,'ybit'=2,'xbit'=2,'core'=2,'shard'=4] {'shard'}, dimensions={0}, use_global_device_ids=true | all-gather | bytes 983040 | tf_op jit(solution)/shard_map/all_gather | solution.py:391
  248.4 7.6 shard_map.233
  284.2 10.3 %collective-permute-done.25.refs_5_ = bf16[3,32,1536]{2,1,0:T(8,128)(2,1)S(1)} collective-permute-done((bf16[3,32,1536]{2,1,0:T(8,128)(2,1)S(1)}, bf16[3,32,1536]{2,1,0:T(8,128)(2,1)S(1)}, u32[]{:S(2)}, u32[]{:S(2)}) %collective-permute-start.25) | collective-permute-done | bytes 294944 | tf_op jit(solution)/shard_map/ppermute | solution.py:23
  320.4 14.6 %shard_map.236 = (bf16[512,512]{1,0:T(8,128)(2,1)S(1)}, bf16[512,512]{1,0:T(8,128)(2,1)S(1)}, bf16[512,512]{1,0:T(8,128)(2,1)S(1)}, bf16[512,512]{1,0:T(8,128)(2,1)S(1)}, f32[8,512,1]{2,1,0:T(8,128)S(1)}) custom-call(f32[512,1536]{1,0:T(8,128)} %convolution_add_fusion.refs_0_.refs_1_.refs_2_, f32[512,1536]{1,0:T(8,128)} %convolution_add_fusion.refs_0_.refs_1_.refs_2_, ...), custom_call_target="tpu_custom_call" | custom-call | flops 536870912 | bytes 5242880 | tf_op jit(solution)/shard_map/pallas_call | solution.py:529
  355.1 6.8 shard_map.240
  363.9 8.0 shard_map.239
  397.4 16.8 %shard_map.242 = (bf16[512,512]{1,0:T(8,128)(2,1)S(1)}, bf16[512,512]{1,0:T(8,128)(2,1)S(1)}, bf16[512,512]{1,0:T(8,128)(2,1)S(1)}) custom-call(bf16[512,512]{1,0:T(8,128)(2,1)S(1)} %copy-done.73, bf16[512,512]{1,0:T(8,128)(2,1)S(1)} %copy-done.75, bf16[512,512]{1,0:T(8,128)(2,1)S(1)} %copy-done.77, bf16[512,512]{1,0:T(8,128)(2,1)S(1)} %pad_maximum_fusion.refs_3_, ...), custom_call_target="tpu_custom_call" | custom-call | flops 1342177280 | bytes 5242880 | tf_op jit(solution)/shard_map/pallas_call | solution.py:563
  426.0 9.5 %collective-permute-done.39.ga_ref = bf16[2,4,32,2048]{3,2,1,0:T(8,128)(2,1)S(1)} collective-permute-done((bf16[2,4,32,2048]{3,2,1,0:T(8,128)(2,1)}, bf16[2,4,32,2048]{3,2,1,0:T(8,128)(2,1)S(1)}, u32[]{:S(2)}, u32[]{:S(2)}) %collective-permute-start.39) | collective-permute-done | bytes 1048608 | tf_op jit(solution)/shard_map/ppermute | solution.py:23
  456.1 11.9 %collective-permute-done.43 = bf16[2,80,1024]{2,1,0:T(8,128)(2,1)S(1)} collective-permute-done((bf16[2,80,1024]{2,1,0:T(8,128)(2,1)S(1)}, bf16[2,80,1024]{2,1,0:T(8,128)(2,1)S(1)}, u32[]{:S(2)}, u32[]{:S(2)}) %collective-permute-start.43) | collective-permute-done | bytes 327712 | tf_op jit(solution)/shard_map/ppermute | solution.py:27
  526.6 21.4 %collective-permute-done.52.ma_ref = bf16[4,32,1536]{2,1,0:T(8,128)(2,1)S(1)} collective-permute-done((bf16[4,32,1536]{2,1,0:T(8,128)(2,1)S(1)}, bf16[4,32,1536]{2,1,0:T(8,128)(2,1)S(1)}, u32[]{:S(2)}, u32[]{:S(2)}) %collective-permute-start.52) | collective-permute-done | bytes 393248 | tf_op jit(solution)/shard_map/ppermute | solution.py:23
  568.4 16.6 %shard_map.249 = (bf16[512,512]{1,0:T(8,128)(2,1)S(1)}, bf16[512,512]{1,0:T(8,128)(2,1)S(1)}, bf16[512,512]{1,0:T(8,128)(2,1)S(1)}) custom-call(bf16[512,512]{1,0:T(8,128)(2,1)S(1)} %copy-done.63, bf16[512,512]{1,0:T(8,128)(2,1)S(1)} %copy-done.65, bf16[512,512]{1,0:T(8,128)(2,1)S(1)} %copy-done.67, bf16[512,512]{1,0:T(8,128)(2,1)S(1)} %pad_maximum_fusion.1.refs_3_, ...), custom_call_target="tpu_custom_call" | custom-call | flops 1342177280 | bytes 5242880 | tf_op jit(solution)/shard_map/pallas_call | solution.py:563
  585.6 9.6 %collective-permute-done.57 = bf16[2,32,1536]{2,1,0:T(8,128)(2,1)S(1)} collective-permute-done((bf16[2,32,1536]{2,1,0:T(8,128)(2,1)S(1)}, bf16[2,32,1536]{2,1,0:T(8,128)(2,1)S(1)}, u32[]{:S(2)}, u32[]{:S(2)}) %collective-permute-start.57) | collective-permute-done | bytes 196640 | tf_op jit(solution)/shard_map/ppermute | solution.py:27
  621.5 11.4 %collective-permute-done.75 = bf16[2,80,1024]{2,1,0:T(8,128)(2,1)} collective-permute-done((bf16[2,80,1024]{2,1,0:T(8,128)(2,1)}, bf16[2,80,1024]{2,1,0:T(8,128)(2,1)}, u32[]{:S(2)}, u32[]{:S(2)}) %collective-permute-start.75) | collective-permute-done | bytes 327712 | tf_op jit(solution)/shard_map/ppermute | solution.py:27
  633.2 9.8 %collective-permute-done.76 = bf16[2,80,1024]{2,1,0:T(8,128)(2,1)S(1)} collective-permute-done((bf16[2,80,1024]{2,1,0:T(8,128)(2,1)}, bf16[2,80,1024]{2,1,0:T(8,128)(2,1)S(1)}, u32[]{:S(2)}, u32[]{:S(2)}) %collective-permute-start.76) | collective-permute-done | bytes 327712 | tf_op jit(solution)/shard_map/ppermute | solution.py:27
  643.0 6.8 collective-permute-done.77.ma_ref
  660.2 7.1 collective-permute-done.81
  667.3 7.0 collective-permute-done.82
  699.4 7.2 convolution_convert_fusion
  727.6 7.3 collective-permute-start.64
  745.6 11.7 %collective-permute-done.65 = bf16[128,1024]{1,0:T(8,128)(2,1)S(1)} collective-permute-done((bf16[128,1024]{1,0:T(8,128)(2,1)}, bf16[128,1024]{1,0:T(8,128)(2,1)S(1)}, u32[]{:S(2)}, u32[]{:S(2)}) %collective-permute-start.65) | collective-permute-done | bytes 262176 | tf_op jit(solution)/shard_map/ppermute | solution.py:27
  (804 shorter events, 506.2 us)
Async XLA Ops:
  7.2 113.5 %all-gather.23.cloned.1.call-start = ((), (), s32[]{:S(2)}) async-start(), calls=%async_computation | async-start | bytes 1310720 | tf_op jit(solution)/shard_map/all_gather | solution.py:391
  11.9 63.7 %collective-permute-start.7 = (bf16[6656]{0:T(1024)(128)(2,1)S(1)}, bf16[6656]{0:T(1024)(128)(2,1)S(1)}, u32[]{:S(2)}, u32[]{:S(2)}) collective-permute-start(bf16[6656]{0:T(1024)(128)(2,1)S(1)} %constant_dynamic-update-slice_fusion.10), channel_id=1, source_target_pairs={{0,1},{1,2},{2,3},{3,0},{4,5},{5,6},{6,7},{7,4},{8,9},{9,10},{10,1... | collective-permute-start | bytes 39944 | tf_op jit(solution)/shard_map/ppermute | solution.py:27
  14.9 60.7 %collective-permute-start.6 = (bf16[6656]{0:T(1024)(128)(2,1)S(1)}, bf16[6656]{0:T(1024)(128)(2,1)}, u32[]{:S(2)}, u32[]{:S(2)}) collective-permute-start(bf16[6656]{0:T(1024)(128)(2,1)S(1)} %constant_dynamic-update-slice_fusion.10), channel_id=1, source_target_pairs={{0,2},{1,3},{2,0},{3,1},{4,6},{5,7},{6,4},{7,5},{8,10},{9,11},{10,... | collective-permute-start | bytes 39944 | tf_op jit(solution)/shard_map/ppermute | solution.py:27
  17.5 58.9 %collective-permute-start.5 = (bf16[6656]{0:T(1024)(128)(2,1)S(1)}, bf16[6656]{0:T(1024)(128)(2,1)}, u32[]{:S(2)}, u32[]{:S(2)}) collective-permute-start(bf16[6656]{0:T(1024)(128)(2,1)S(1)} %constant_dynamic-update-slice_fusion.10), channel_id=1, source_target_pairs={{0,3},{1,0},{2,1},{3,2},{4,7},{5,4},{6,5},{7,6},{8,11},{9,8},{10,9... | collective-permute-start | bytes 39944 | tf_op jit(solution)/shard_map/ppermute | solution.py:27
  18.9 45.1 %collective-permute-start.14 = (s32[2,512]{1,0:T(2,128)}, s32[2,512]{1,0:T(2,128)S(1)}, u32[]{:S(2)}, u32[]{:S(2)}) collective-permute-start(s32[2,512]{1,0:T(2,128)} %param.14), channel_id=1, source_target_pairs={{0,4},{4,0},{1,5},{5,1},{2,6},{6,2},{3,7},{7,3},{8,12},{12,8},{9,1... | collective-permute-start | bytes 12296 | tf_op jit(solution)/shard_map/ppermute | solution.py:23
  42.5 115.2 %all-gather.25.cloned.1.call-start = ((), (), s32[]{:S(2)}) async-start(), calls=%async_computation.1 | async-start | bytes 1638400 | tf_op jit(solution)/shard_map/all_gather | solution.py:391
  45.9 74.8 %collective-permute-start.9 = (bf16[2,3,32,1536]{3,2,1,0:T(8,128)(2,1)}, bf16[2,3,32,1536]{3,2,1,0:T(8,128)(2,1)}, u32[]{:S(2)}, u32[]{:S(2)}) collective-permute-start(bf16[2,3,32,1536]{3,2,1,0:T(8,128)(2,1)} %shard_map.222.refs_1_), channel_id=1, source_target_pairs={{0,16},{16,0},{1,17},{17,1},{2,18},{18,2},{3,19},{19,3},{4,20},{20... | collective-permute-start | bytes 1769480 | tf_op jit(solution)/shard_map/ppermute | solution.py:23
  64.0 56.7 %collective-permute-start.8 = (bf16[2,3,32,1536]{3,2,1,0:T(8,128)(2,1)}, bf16[2,3,32,1536]{3,2,1,0:T(8,128)(2,1)}, u32[]{:S(2)}, u32[]{:S(2)}) collective-permute-start(bf16[2,3,32,1536]{3,2,1,0:T(8,128)(2,1)} %shard_map.222.refs_1_), channel_id=1, source_target_pairs={{0,8},{8,0},{1,9},{9,1},{2,10},{10,2},{3,11},{11,3},{4,12},{12,4},... | collective-permute-start | bytes 1769480 | tf_op jit(solution)/shard_map/ppermute | solution.py:23
  125.7 118.2 %all-gather.27.cloned.1.call-start = ((), (), s32[]{:S(2)}) async-start(), calls=%async_computation.2 | async-start | bytes 1310720 | tf_op jit(solution)/shard_map/all_gather | solution.py:391
  161.0 51.9 %collective-permute-start.18 = (bf16[2,3,80,1024]{3,2,1,0:T(8,128)(2,1)S(1)}, bf16[2,3,80,1024]{3,2,1,0:T(8,128)(2,1)S(1)}, u32[]{:S(2)}, u32[]{:S(2)}) collective-permute-start(bf16[2,3,80,1024]{3,2,1,0:T(8,128)(2,1)S(1)} %shard_map.228.refs_1_), channel_id=1, source_target_pairs={{0,16},{16,0},{1,17},{17,1},{2,18},{18,2},{3,19},{19,3},{4,20},{20... | collective-permute-start | bytes 2949128 | tf_op jit(solution)/shard_map/ppermute | solution.py:23
  162.6 50.4 %collective-permute-start.17 = (bf16[2,3,80,1024]{3,2,1,0:T(8,128)(2,1)S(1)}, bf16[2,3,80,1024]{3,2,1,0:T(8,128)(2,1)}, u32[]{:S(2)}, u32[]{:S(2)}) collective-permute-start(bf16[2,3,80,1024]{3,2,1,0:T(8,128)(2,1)S(1)} %shard_map.228.refs_1_), channel_id=1, source_target_pairs={{0,8},{8,0},{1,9},{9,1},{2,10},{10,2},{3,11},{11,3},{4,12},{12,4},... | collective-permute-start | bytes 2949128 | tf_op jit(solution)/shard_map/ppermute | solution.py:23
  166.1 45.3 %collective-permute-start.16 = (bf16[3,32,2048]{2,1,0:T(8,128)(2,1)S(1)}, bf16[3,32,2048]{2,1,0:T(8,128)(2,1)S(1)}, u32[]{:S(2)}, u32[]{:S(2)}) collective-permute-start(bf16[3,32,2048]{2,1,0:T(8,128)(2,1)S(1)} %slice_bitcast_fusion.6), channel_id=1, source_target_pairs={{0,8},{8,0},{1,9},{9,1},{2,10},{10,2},{3,11},{11,3},{4,12},{12,4},... | collective-permute-start | bytes 1179656 | tf_op jit(solution)/shard_map/ppermute | solution.py:23
  166.7 45.5 %collective-permute-start.15 = (bf16[3,32,2048]{2,1,0:T(8,128)(2,1)S(1)}, bf16[3,32,2048]{2,1,0:T(8,128)(2,1)S(1)}, u32[]{:S(2)}, u32[]{:S(2)}) collective-permute-start(bf16[3,32,2048]{2,1,0:T(8,128)(2,1)S(1)} %slice_bitcast_fusion.7), channel_id=1, source_target_pairs={{0,16},{16,0},{1,17},{17,1},{2,18},{18,2},{3,19},{19,3},{4,20},{20... | collective-permute-start | bytes 1179656 | tf_op jit(solution)/shard_map/ppermute | solution.py:23
  218.4 82.0 %all-gather.29.cloned.1.call-start = ((), (), s32[]{:S(2)}) async-start(), calls=%async_computation.3 | async-start | bytes 1638400 | tf_op jit(solution)/shard_map/all_gather | solution.py:391
  269.8 500.8 %all-gather.37.cloned.1.call-start = ((), (), s32[]{:S(2)}) async-start(), calls=%async_computation.7 | async-start | bytes 2949120 | tf_op jit(solution)/shard_map/all_gather | solution.py:413
  485.0 290.3 %all-gather.41.cloned.1.call-start = ((), (), s32[]{:S(2)}) async-start(), calls=%async_computation.9 | async-start | bytes 2359296 | tf_op jit(solution)/shard_map/all_gather | solution.py:413
  500.6 48.1 %collective-permute-start.54 = (bf16[2,4,80,1024]{3,2,1,0:T(8,128)(2,1)S(1)}, bf16[2,4,80,1024]{3,2,1,0:T(8,128)(2,1)S(1)}, u32[]{:S(2)}, u32[]{:S(2)}) collective-permute-start(bf16[2,4,80,1024]{3,2,1,0:T(8,128)(2,1)S(1)} %copy-done.114), channel_id=1, source_target_pairs={{0,8},{8,0},{1,9},{9,1},{2,10},{10,2},{3,11},{11,3},{4,12},{12,4},... | collective-permute-start | bytes 3932168 | tf_op jit(solution)/shard_map/ppermute | solution.py:23
  501.2 47.5 %collective-permute-start.55 = (bf16[2,4,80,1024]{3,2,1,0:T(8,128)(2,1)}, bf16[2,4,80,1024]{3,2,1,0:T(8,128)(2,1)}, u32[]{:S(2)}, u32[]{:S(2)}) collective-permute-start(bf16[2,4,80,1024]{3,2,1,0:T(8,128)(2,1)} %get-tuple-element.304), channel_id=1, source_target_pairs={{0,16},{16,0},{1,17},{17,1},{2,18},{18,2},{3,19},{19,3},{4,20},{20... | collective-permute-start | bytes 3932168 | tf_op jit(solution)/shard_map/ppermute | solution.py:23
  549.6 229.6 %all-gather.33.cloned.1.call-start = ((), (), s32[]{:S(2)}) async-start(), calls=%async_computation.5 | async-start | bytes 1769472 | tf_op jit(solution)/shard_map/all_gather | solution.py:413
  557.4 43.8 %collective-permute-start.60 = (bf16[4,80,1024]{2,1,0:T(8,128)(2,1)S(1)}, bf16[4,80,1024]{2,1,0:T(8,128)(2,1)S(1)}, u32[]{:S(2)}, u32[]{:S(2)}) collective-permute-start(bf16[4,80,1024]{2,1,0:T(8,128)(2,1)S(1)} %fusion.34), channel_id=1, source_target_pairs={{0,8},{8,0},{1,9},{9,1},{2,10},{10,2},{3,11},{11,3},{4,12},{12,4},... | collective-permute-start | bytes 1966088 | tf_op jit(solution)/shard_map/ppermute | solution.py:23
  559.8 43.6 %collective-permute-start.61 = (bf16[2,4,32,2048]{3,2,1,0:T(8,128)(2,1)S(1)}, bf16[2,4,32,2048]{3,2,1,0:T(8,128)(2,1)S(1)}, u32[]{:S(2)}, u32[]{:S(2)}) collective-permute-start(bf16[2,4,32,2048]{3,2,1,0:T(8,128)(2,1)S(1)} %copy-done.118), channel_id=1, source_target_pairs={{0,8},{8,0},{1,9},{9,1},{2,10},{10,2},{3,11},{11,3},{4,12},{12,4},... | collective-permute-start | bytes 3145736 | tf_op jit(solution)/shard_map/ppermute | solution.py:23
  616.9 166.0 %all-gather.31.cloned.1.call-start = ((), (), s32[]{:S(2)}) async-start(), calls=%async_computation.4 | async-start | bytes 1769472 | tf_op jit(solution)/shard_map/all_gather | solution.py:413
  696.5 89.9 %all-gather.39.cloned.1.call-start = ((), (), s32[]{:S(2)}) async-start(), calls=%async_computation.8 | async-start | bytes 2359296 | tf_op jit(solution)/shard_map/all_gather | solution.py:413
  697.4 93.1 %all-gather.35.cloned.1.call-start = ((), (), s32[]{:S(2)}) async-start(), calls=%async_computation.6 | async-start | bytes 2949120 | tf_op jit(solution)/shard_map/all_gather | solution.py:413
  (252 other events, 2920.8 us)
Sparse Core Ops, SparseCore 0:
  42.7 27.5 all-gather.22
  125.8 31.8 all-gather.24
  218.5 25.4 all-gather.26
  269.9 30.3 all-gather.28
  485.1 46.3 all-gather.36
  549.7 35.0 all-gather.40
  617.0 30.3 all-gather.32
  696.6 29.4 all-gather.30
  728.0 28.1 all-gather.38
  758.0 30.1 all-gather.34

commit v3 on v2

--- a/solution.py
+++ b/solution.py
@@ -17,6 +17,8 @@
 BF16 = jnp.bfloat16
 AXES = ("outer", "ybit", "xbit", "core")
 VMEM_LIMIT = 48 * 1024 * 1024
+FORWARD_ROWS = 256
+BACKWARD_ROWS = 512
 
 
 def swap(x, axis):
@@ -89,32 +91,62 @@
 def pick_columns(weights, layer, width, place):
     rows, columns = weights.shape[1:]
     count = columns // (2 * width)
-
-    def body(scalars, ins, out):
-        core = scalars[2]
-        for j in range(count):
-            start = pl.multiple_of((2 * j + core) * width, width)
-            yield (
-                ins[0].at[layer, :, pl.ds(start, width)],
-                out.at[:, pl.ds(j * width, width)],
-            )
-
-    shape = jax.ShapeDtypeStruct((rows, count * width), weights.dtype)
-    return copy_call(body, shape, count, [weights], place)
+    group = 2 if count % 2 == 0 else 1
+
+    def kernel(scalars, *refs):
+        out = refs[-1]
+        for j in range(group):
+            out[:, j * width : (j + 1) * width] = refs[j][0]
+
+    def spec(j):
+        return pl.BlockSpec(
+            (1, rows, width), lambda i, s: (layer, 0, 2 * (group * i + j) + s[2])
+        )
+
+    return pl.pallas_call(
+        kernel,
+        grid_spec=pltpu.PrefetchScalarGridSpec(
+            num_scalar_prefetch=1,
+            grid=(count // group,),
+            in_specs=[spec(j) for j in range(group)],
+            out_specs=pl.BlockSpec((rows, group * width), lambda i, s: (0, i)),
+        ),
+        out_shape=jax.ShapeDtypeStruct((rows, count * width), weights.dtype),
+        compiler_params=pltpu.CompilerParams(vmem_limit_bytes=VMEM_LIMIT),
+        cost_estimate=pl.CostEstimate(
+            flops=0, bytes_accessed=4 * rows * count * width, transcendentals=0
+        ),
+    )(place.scalars, *[weights] * group)
 
 
 def pick_rows(arrays, layer, place):
     halves = [w.shape[1] // 2 for w in arrays]
-
-    def body(scalars, ins, out):
+    columns = arrays[0].shape[2]
+    part = columns // 4 if columns % 512 == 0 else columns
+
+    def kernel(scalars, *refs):
         start = 0
-        for ref, half in zip(ins, halves, strict=True):
-            first = pl.multiple_of(scalars[2] * half, half)
-            yield ref.at[layer, pl.ds(first, half)], out.at[pl.ds(start, half)]
+        for ref, half in zip(refs, halves, strict=False):
+            refs[-1][start : start + half] = ref[0]
             start += half
 
-    shape = jax.ShapeDtypeStruct((sum(halves), arrays[0].shape[2]), arrays[0].dtype)
-    return copy_call(body, shape, len(arrays), list(arrays), place)
+    return pl.pallas_call(
+        kernel,
+        grid_spec=pltpu.PrefetchScalarGridSpec(
+            num_scalar_prefetch=1,
+            grid=(columns // part,),
+            in_specs=[
+                pl.BlockSpec((1, half, part), lambda i, s: (layer, s[2], i))
+                for half in halves
+            ],
+            out_specs=pl.BlockSpec((sum(halves), part), lambda i, s: (0, i)),
+        ),
+        out_shape=jax.ShapeDtypeStruct((sum(halves), columns), arrays[0].dtype),
+        compiler_params=pltpu.CompilerParams(vmem_limit_bytes=VMEM_LIMIT),
+        cost_estimate=pl.CostEstimate(
+            flops=0, bytes_accessed=4 * sum(halves) * columns, transcendentals=0
+        ),
+    )(place.scalars, *arrays)
 
 
 def other_shards(table, place):
@@ -137,21 +169,58 @@
 def assemble(half, near, near_x, near_y, far_a, far_b, place):
     span = place.span
     eighth, columns = half.shape[0] // 8, half.shape[1]
-
-    def body(scalars, ins, out):
+    block = (eighth, columns)
+
+    def kernel(scalars, half_ref, n_ref, x_ref, y_ref, a_ref, b_ref, out):
         z, q = scalars[0], scalars[1]
-        yield ins[0], out.at[z]
-        for k in range(1, span):
-            source = lax.rem(z + (span - k), span)
+        own = pl.program_id(0) == z
+
+        @pl.when(own)
+        def _():
+            out[0] = half_ref[...]
+
+        @pl.when(jnp.logical_not(own))
+        def _():
             for i in range(2):
-                for flip in range(3):
-                    yield ins[1 + flip].at[i, k - 1], out.at[source, flipped(q, flip), i]
-                yield ins[4 + i].at[k - 1], out.at[source, flipped(q, 3), i]
-
-    shape = jax.ShapeDtypeStruct((span, 4, 2, eighth, columns), half.dtype)
-    half = half.reshape(4, 2, eighth, columns)
-    operands = [half, near, near_x, near_y, far_a, far_b]
-    out = copy_call(body, shape, 1 + 8 * (span - 1), operands, place)
+                for flip, ref in enumerate((n_ref, x_ref, y_ref)):
+                    out[0, flipped(q, flip), i] = ref[i, 0]
+            out[0, flipped(q, 3), 0] = a_ref[0]
+            out[0, flipped(q, 3), 1] = b_ref[0]
+
+    def behind(j, s):
+        return jnp.maximum(lax.rem(s[0] + span - j, span), 1) - 1
+
+    near_spec = pl.BlockSpec((2, 1, *block), lambda j, s: (0, behind(j, s), 0, 0))
+    far_spec = pl.BlockSpec((1, *block), lambda j, s: (behind(j, s), 0, 0))
+    out = pl.pallas_call(
+        kernel,
+        grid_spec=pltpu.PrefetchScalarGridSpec(
+            num_scalar_prefetch=1,
+            grid=(span,),
+            in_specs=[
+                pl.BlockSpec((4, 2, *block), lambda j, s: (0, 0, 0, 0)),
+                near_spec,
+                near_spec,
+                near_spec,
+                far_spec,
+                far_spec,
+            ],
+            out_specs=pl.BlockSpec((1, 4, 2, *block), lambda j, s: (j, 0, 0, 0, 0)),
+        ),
+        out_shape=jax.ShapeDtypeStruct((span, 4, 2, *block), half.dtype),
+        compiler_params=pltpu.CompilerParams(vmem_limit_bytes=VMEM_LIMIT),
+        cost_estimate=pl.CostEstimate(
+            flops=0, bytes_accessed=32 * span * eighth * columns, transcendentals=0
+        ),
+    )(
+        place.scalars,
+        half.reshape(4, 2, *block),
+        near,
+        near_x,
+        near_y,
+        far_a,
+        far_b,
+    )
     return out.reshape(8 * span * eighth, columns)
 
 
@@ -324,21 +393,27 @@
     )(*operands)
 
 
+def spread(blocks, place):
+    span = place.span
+    out = []
+    for k in range(span):
+        block = lax.dynamic_index_in_dim(
+            blocks, lax.rem(place.z + k, span), 0, keepdims=False
+        )
+        out.append(block if k == 0 else spin(block, k, span))
+    return out
+
+
 def row_to_chip(x, place):
-    span = place.span
     rows, tokens, width = x.shape
     half = width // 2
     mine = lax.dynamic_slice_in_dim(x, place.c * half, half, 2)
     theirs = lax.dynamic_slice_in_dim(x, (1 - place.c) * half, half, 2)
-    rows_all = by_core(place, mine, swap(theirs, "core"), 0)
-    blocks = []
-    for k in range(span):
-        block = lax.dynamic_index_in_dim(
-            rows_all, lax.rem(place.z + k, span), 0, keepdims=False
-        )
-        blocks.append(block if k == 0 else spin(block, k, span))
-    own = from_relative(blocks, place).reshape(span * tokens, half)
-    return by_core(place, own, swap(own, "core"), 1)
+    theirs = yield swap(theirs, "core")
+    blocks = yield spread(by_core(place, mine, theirs, 0), place)
+    own = from_relative(blocks, place).reshape(place.span * tokens, half)
+    other = yield swap(own, "core")
+    return by_core(place, own, other, 1)
 
 
 def chip_to_rows(y, rows, place):
@@ -347,17 +422,12 @@
     tokens = y.shape[0] // span
     half = width // 2
     mine = lax.dynamic_slice_in_dim(y, place.c * half, half, 1)
-    mine = mine.reshape(span, tokens, half)
-    blocks = []
-    for k in range(span):
-        block = lax.dynamic_index_in_dim(
-            mine, lax.rem(place.z + k, span), 0, keepdims=False
-        )
-        blocks.append(block if k == 0 else spin(block, k, span))
+    blocks = yield spread(mine.reshape(span, tokens, half), place)
     stacked = from_relative(blocks, place)
     own = lax.dynamic_slice_in_dim(stacked, place.c * rows, rows, 0)
     theirs = lax.dynamic_slice_in_dim(stacked, (1 - place.c) * rows, rows, 0)
-    return by_core(place, own, swap(theirs, "core"), 2)
+    other = yield swap(theirs, "core")
+    return by_core(place, own, other, 2)
 
 
 class Slots:
@@ -382,14 +452,20 @@
         return extra
 
 
-def gather_weight(half, place):
+def gather_weight(half, by_call, wait, place):
+    span = place.span
     eighth, columns = half.shape[0] // 8, half.shape[1]
     mine = lax.dynamic_index_in_dim(
         half.reshape(4, 2, eighth, columns), place.q, 0, keepdims=False
     )
-    mine = yield mine
-    every = yield lax.all_gather(mine, "shard")
-    near = other_shards(every, place)
+    if wait:
+        mine = yield mine
+    if by_call:
+        every = yield lax.all_gather(mine, "shard")
+        near = other_shards(every, place)
+    else:
+        arrived = yield [spin(mine, k, span) for k in range(1, span)]
+        near = jnp.stack(arrived, 1)
     near_x, near_y = yield [swap(near, "xbit"), swap(near, "ybit")]
     far_a, far_b = yield [swap(near_x[0], "ybit"), swap(near_y[1], "xbit")]
     return assemble(half, near, near_x, near_y, far_a, far_b, place)
@@ -410,14 +486,14 @@
     summed = summed.astype(BF16)
     if lax.axis_size("outer") > 1:
         summed = lax.psum(summed, "outer")
-    parts = lax.all_gather(summed, ("ybit", "xbit", "core"))
+    parts = yield lax.all_gather(summed, ("ybit", "xbit", "core"))
     _, eighth, columns = summed.shape
     return parts.reshape(4, 2, 2 * eighth, columns)
 
 
 def gather_small(vectors, place):
     flat = jnp.concatenate([v.reshape(-1) for v in vectors])
-    blocks = [flat] + [spin(flat, k, place.span) for k in range(1, place.span)]
+    blocks = yield [flat] + [spin(flat, k, place.span) for k in range(1, place.span)]
     table = from_relative(blocks, place)
     out, start = [], 0
     for v in vectors:
@@ -428,16 +504,18 @@
     return out
 
 
-def blocks_of(length):
-    step = 128 if length % 128 == 0 else length
+def blocks_of(length, step):
+    step = step if length % step == 0 else length
     return [(i * step, step) for i in range(length // step)]
 
 
-def seen(seg_col, seg_row, start, step):
-    stop = start + step
-    row = start + lax.broadcasted_iota(jnp.int32, (step, stop), 0)
-    col = lax.broadcasted_iota(jnp.int32, (step, stop), 1)
-    return (col <= row) & (seg_col[start:stop, :] == seg_row[:, :stop])
+def fill_bias(bias, seg_col, seg_row):
+    @pl.when(pl.program_id(0) == 0)
+    def _():
+        row = lax.broadcasted_iota(jnp.int32, bias.shape, 0)
+        col = lax.broadcasted_iota(jnp.int32, bias.shape, 1)
+        mask = (col <= row) & (seg_col[...] == seg_row[...])
+        bias[...] = jnp.where(mask, 0.0, -1e30)
 
 
 def turn(u, tables):
@@ -454,18 +532,18 @@
 
 def attend_kernel(scale, head, *refs):
     q_in, k_in, v_in, keep, upper, lower, seg_col, seg_row = refs[:8]
-    q_ref, k_ref, v_ref, o_ref, lse_ref = refs[8:]
+    q_ref, k_ref, v_ref, o_ref, lse_ref, bias = refs[8:]
+    fill_bias(bias, seg_col, seg_row)
     tables = keep[...], upper[...], lower[...]
     q_ref[...] = turn(q_in[...], tables).astype(BF16)
     k_ref[...] = turn(k_in[...], tables).astype(BF16)
     v_ref[...] = v_in[...].astype(BF16)
-    for start, step in blocks_of(q_ref.shape[0]):
+    for start, step in blocks_of(q_ref.shape[0], FORWARD_ROWS):
         stop = start + step
-        mask = seen(seg_col, seg_row, start, step)
         for h in range(q_ref.shape[1] // head):
             lanes = slice(h * head, (h + 1) * head)
-            scores = dot_t(q_ref[start:stop, lanes], k_ref[:stop, lanes]) * scale
-            scores = jnp.where(mask, scores, -1e30)
+            query = q_ref[start:stop, lanes] * scale
+            scores = dot_t(query, k_ref[:stop, lanes]) + bias[start:stop, :stop]
             top = jnp.max(scores, -1, keepdims=True)
             expo = jnp.exp(scores - top)
             total = jnp.sum(expo, -1, keepdims=True)
@@ -476,30 +554,35 @@
 
 def attend_back_kernel(scale, head, *refs):
     q_ref, k_ref, v_ref, do_ref, lse_ref, keep, upper, lower, seg_col, seg_row = refs[:10]
-    dq_out, dk_out, dv_out, dq_ref, dk_ref, dv_ref = refs[10:]
-    dk_ref[...] = jnp.zeros_like(dk_ref)
-    dv_ref[...] = jnp.zeros_like(dv_ref)
+    dq_out, dk_out, dv_out, dq_ref, dk_ref, dv_ref, bias = refs[10:]
+    fill_bias(bias, seg_col, seg_row)
     over_rows = (((0,), (0,)), ((), ()))
-    for start, step in blocks_of(q_ref.shape[0]):
+    length = q_ref.shape[0]
+    if len(blocks_of(length, BACKWARD_ROWS)) > 1:
+        dk_ref[...] = jnp.zeros_like(dk_ref)
+        dv_ref[...] = jnp.zeros_like(dv_ref)
+    for start, step in blocks_of(length, BACKWARD_ROWS):
         stop = start + step
-        mask = seen(seg_col, seg_row, start, step)
         for h in range(q_ref.shape[1] // head):
             lanes = slice(h * head, (h + 1) * head)
-            query = q_ref[start:stop, lanes]
+            query = q_ref[start:stop, lanes] * scale
             keys = k_ref[:stop, lanes]
             grad = do_ref[start:stop, lanes]
-            scores = dot_t(query, keys) * scale
-            probs = jnp.exp(jnp.where(mask, scores - lse_ref[h, start:stop, :], -1e30))
+            scores = dot_t(query, keys) + bias[start:stop, :stop]
+            probs = jnp.exp(scores - lse_ref[h, start:stop, :])
             d_probs = dot_t(grad, v_ref[:stop, lanes])
             delta = jnp.sum(probs * d_probs, -1, keepdims=True)
             d_scores = (probs * (d_probs - delta)).astype(BF16)
             dq_ref[start:stop, lanes] = dot(d_scores, keys) * scale
-            dk_ref[:stop, lanes] += (
-                lax.dot_general(d_scores, query, over_rows, preferred_element_type=F32) * scale
-            )
-            dv_ref[:stop, lanes] += lax.dot_general(
+            d_key = lax.dot_general(d_scores, query, over_rows, preferred_element_type=F32)
+            d_value = lax.dot_general(
                 probs.astype(BF16), grad, over_rows, preferred_element_type=F32
             )
+            if step == length:
+                dk_ref[:, lanes], dv_ref[:, lanes] = d_key, d_value
+            else:
+                dk_ref[:stop, lanes] += d_key
+                dv_ref[:stop, lanes] += d_value
     tables = keep[...], upper[...], lower[...]
     dq_out[...] = turn_back(dq_ref[...], tables).astype(BF16)
     dk_out[...] = turn_back(dk_ref[...], tables).astype(BF16)
@@ -543,6 +626,7 @@
             low,
             jax.ShapeDtypeStruct((width // head, length, 1), F32),
         ],
+        scratch_shapes=[pltpu.VMEM((length, length), F32)],
         compiler_params=pltpu.CompilerParams(vmem_limit_bytes=VMEM_LIMIT),
         cost_estimate=pl.CostEstimate(
             flops=4 * length * length * width,
@@ -566,7 +650,8 @@
         in_specs=[wide, wide, wide, wide, lse, *same],
         out_specs=[wide, wide, wide],
         out_shape=[out, out, out],
-        scratch_shapes=[pltpu.VMEM((length, group), F32)] * 3,
+        scratch_shapes=[pltpu.VMEM((length, group), F32)] * 3
+        + [pltpu.VMEM((length, length), F32)],
         compiler_params=pltpu.CompilerParams(vmem_limit_bytes=VMEM_LIMIT),
         cost_estimate=pl.CostEstimate(
             flops=10 * length * length * width,
@@ -701,16 +786,12 @@
         [jnp.moveaxis(t, 1, 0).reshape(span, -1, 128) for t in tables], 1
     )
     for axis in ("core", "xbit", "ybit"):
-        flat = flat + swap(flat, axis)
+        other = yield swap(flat, axis)
+        flat = flat + other
     if lax.axis_size("outer") > 1:
         flat = lax.psum(flat, "outer")
-    mine = [
-        lax.dynamic_index_in_dim(flat, lax.rem(place.z + k, span), 0, keepdims=False)
-        for k in range(span)
-    ]
-    total = mine[0]
-    for k in range(1, span):
-        total = total + spin(mine[k], k, span)
+    blocks = yield spread(flat, place)
+    total = sum(blocks)
     total = total.reshape(-1)
     out, start = [], 0
     for p in parts:
@@ -752,21 +833,31 @@
             pick_columns(up_weight, layer, ff_cols, place),
             pick_rows((out_weight, down_weight), layer, place),
         ]
-    gathered = [None] * len(halves)
+    found = {}
+
+    def keep(name):
+        def done(value):
+            found[name] = value
+
+        return done
+
     slots = Slots()
-    for index in range(len(halves) + 3):
-        if index < len(halves):
-
-            def arrived(value, index=index):
-                gathered[index] = value
-
-            slots.add(gather_weight(halves[index], place), arrived)
+    slots.add(gather_weight(halves[0], False, False, place), keep(0))
+    both = jnp.concatenate([hidden_in, out_grad], 2)
+    slots.add(row_to_chip(both, place), keep("rows"))
+    vectors = [norm_gains, norm_biases, qkv_bias, out_bias, up_bias, down_bias]
+    slots.add(gather_small(vectors, place), keep("vectors"))
+    seg_other = swap(segments, "core")
+    for index in range(1, len(halves)):
+        slots.add(gather_weight(halves[index], index % 3 != 0, True, place), keep(index))
         slots.step()
-    weights = [gathered[3 * layer : 3 * layer + 3] for layer in range(LAYERS)]
-
-    both = row_to_chip(jnp.concatenate([hidden_in, out_grad], 2), place)
+    while slots.parts:
+        slots.step()
+    weights = [[found[3 * layer + i] for i in range(3)] for layer in range(LAYERS)]
+
+    both = found["rows"]
     stream, dy = both[:, :width].astype(F32), both[:, width:].astype(F32)
-    seg_all = by_core(place, segments, swap(segments, "core"), 0)
+    seg_all = by_core(place, segments, seg_other, 0)
     seg = lax.dynamic_index_in_dim(seg_all, place.z, 0, keepdims=False)
     seg_col, seg_row = seg[:, None], seg[None, :]
     length = seg.shape[0]
@@ -774,10 +865,7 @@
     positions = jnp.arange(length, dtype=jnp.int32) - earlier
     fixed = (*rotary_tables(positions, head), seg_col, seg_row)
 
-    small = gather_small(
-        [norm_gains, norm_biases, qkv_bias, out_bias, up_bias, down_bias], place
-    )
-    gains, shifts, b_qkv, b_out, b_up, b_down = small
+    gains, shifts, b_qkv, b_out, b_up, b_down = found["vectors"]
     b_qkv = pick_vector(b_qkv, head_cols, place)
     b_up = pick_vector(b_up, ff_cols, place)
     smalls = [
@@ -821,14 +909,14 @@
             slots,
             done_for(layer),
         )
+    results = jnp.concatenate([stream.astype(BF16), dy.astype(BF16)], 1)
+    slots.add(chip_to_rows(results, rows, place), keep("results"))
+    slots.add(reduce_small(little, head_cols, ff_cols, place), keep("sums"))
     while slots.parts:
         slots.step()
-    results = jnp.concatenate([stream.astype(BF16), dy.astype(BF16)], 1)
-    results = chip_to_rows(results, rows, place)
+    results = found["results"]
     block_out, in_grad = results[..., :width], results[..., width:].astype(F32)
-    d_gains, d_shifts, d_qkv_b, d_branch_b, d_up_b = reduce_small(
-        little, head_cols, ff_cols, place
-    )
+    d_gains, d_shifts, d_qkv_b, d_branch_b, d_up_b = found["sums"]
     d_qkv_w, d_up_w, (d_out_w, d_down_w) = big
     d_out_w = d_out_w.reshape(LAYERS, -1, width)
     d_down_w = d_down_w.reshape(LAYERS, -1, width)

time: 812 us -> 795 us (0.979)
  blocking collectives: 36 us -> 0 us
  Pallas kernels: 181 us -> 151 us
  local copies, waits for them, and re-layouts: 121 us -> 142 us
  waiting for transfers between devices: 198 us -> 211 us
  starting transfers between devices: 112 us -> 122 us
    pallas_call x18 -> x4, Pallas kernels: 53.7 us -> 8.86 us  [copy_call(): pl.pallas_call(kernel, out_shape=out_shape, in_specs=[pl.BlockSpec(memory...]
    pallas_call x0 -> x12, Pallas kernels: none -> 37.8 us  [the longest x6 28.2 us: assemble(): pl.pallas_call(kernel, grid_spec=pltpu.PrefetchScalarGridSpec(num_scalar_...]
    all_gather x2 -> x0, blocking collectives: 36 us -> none  [gather_weight(): every = (yield lax.all_gather(mine, 'shard'))]
    unnamed x397 -> x487, local copies, waits for them, and re-layouts: 75 us -> 89 us
    all_gather x6, waiting for transfers between devices: 0.01 us -> 13.3 us  [reduce_weight(): parts = (yield lax.all_gather(summed, ('ybit', 'xbit', 'core')))]
    pallas_call x2, Pallas kernels: 33.4 us -> 23.4 us  [attend_back(): pl.pallas_call(kernel, grid=(count,), in_specs=[wide, wide, wide, wide, l...]
    pallas_call x2, Pallas kernels: 29.3 us -> 20.6 us  [attend(): pl.pallas_call(kernel, grid=(count,), in_specs=[wide, pl.BlockSpec((lengt...]
    ppermute x30 -> x36, starting transfers between devices: 57.5 us -> 65.6 us  [spin(): return lax.ppermute(x, 'shard', [(j, (j + k) % span) for j in range(span)])]
  transfers between devices with their start and end apart: 99 -> 105, of which waited for: 32 -> 28; matrix products, arithmetic and copies ran while one was open for 22% -> 23% of each run, Pallas kernels for 20% -> 18%
where the time goes in v3:
time: 795 us; the launch traced here: 786 us
  waiting for transfers between devices  211 us (27%)
  Pallas kernels  151 us (19%)
  local copies, waits for them, and re-layouts  142 us (18%)
  starting transfers between devices  122 us (15%)
  other arithmetic  75.3 us (9%)
  matrix products  66.1 us (8%)
  between operations  17.1 us (2%)
    ppermute x36, waiting for transfers between devices, spin(): return lax.ppermute(x, 'shard', [(j, (j + k) % span) for j in range(span)])  105 us
    unnamed x487, local copies, waits for them, and re-layouts  89 us
    ppermute x59, waiting for transfers between devices, swap(): return lax.ppermute(x, axis, [(0, 1), (1, 0)])  81.1 us
    ppermute x36, starting transfers between devices, spin(): return lax.ppermute(x, 'shard', [(j, (j + k) % span) for j in range(span)])  65.6 us
    ppermute x59, starting transfers between devices, swap(): return lax.ppermute(x, axis, [(0, 1), (1, 0)])  55.5 us
    dot_general x6, matrix products, dot(): return jnp.dot(a, b, preferred_element_type=F32)  35.9 us
    pallas_call x6, Pallas kernels, weight_gradient(): pl.pallas_call(kernel, grid_spec=pltpu.PrefetchScalarGridSpec(num_scalar_...  33.3 us
    dot_general x6, matrix products, dot_t(): lax.dot_general(a, b, (((1,), (1,)), ((), ())), preferred_element_type=F32)  30.2 us
  transfers between devices with their start and end apart: 105, of which 28 were waited for; matrix products, arithmetic and copies ran while one was open for 23% of the time, Pallas kernels for 18%

profile of v3, /device:TPU:0, one launch (start us, length us, event | category | flops | bytes accessed | tf_op | source)
XLA Modules:
  0.0 785.5 jit_solution(14199094767285505821)
XLA Ops:
  80.2 12.1 %collective-permute-done.11 = bf16[128,1024]{1,0:T(8,128)(2,1)} collective-permute-done((bf16[128,1024]{1,0:T(8,128)(2,1)}, bf16[128,1024]{1,0:T(8,128)(2,1)}, u32[]{:S(2)}, u32[]{:S(2)}) %collective-permute-start.11) | collective-permute-done | bytes 262176 | tf_op jit(solution)/shard_map/ppermute | solution.py:29
  92.2 20.8 %collective-permute-done.10 = bf16[128,1024]{1,0:T(8,128)(2,1)} collective-permute-done((bf16[128,1024]{1,0:T(8,128)(2,1)}, bf16[128,1024]{1,0:T(8,128)(2,1)}, u32[]{:S(2)}, u32[]{:S(2)}) %collective-permute-start.10) | collective-permute-done | bytes 262176 | tf_op jit(solution)/shard_map/ppermute | solution.py:29
  130.2 13.6 %collective-permute-done.13.b_ref = bf16[3,32,1536]{2,1,0:T(8,128)(2,1)S(1)} collective-permute-done((bf16[3,32,1536]{2,1,0:T(8,128)(2,1)S(1)}, bf16[3,32,1536]{2,1,0:T(8,128)(2,1)S(1)}, u32[]{:S(2)}, u32[]{:S(2)}) %collective-permute-start.13) | collective-permute-done | bytes 294944 | tf_op jit(solution)/shard_map/ppermute | solution.py:25
  175.5 10.3 %shard_map.226 = (bf16[512,512]{1,0:T(8,128)(2,1)S(1)}, bf16[512,512]{1,0:T(8,128)(2,1)S(1)}, bf16[512,512]{1,0:T(8,128)(2,1)S(1)}, bf16[512,512]{1,0:T(8,128)(2,1)S(1)}, f32[8,512,1]{2,1,0:T(8,128)S(1)}) custom-call(f32[512,1536]{1,0:T(8,128)} %convolution_add_fusion.1.refs_0_.refs_1_.refs_2_, f32[512,1536]{1,0:T(8,128)} %convolution_add_fusion.1.refs_0_.refs_1_.refs_2_, ...), custom_call_target="tpu_custom_call" | custom-call | flops 536870912 | bytes 5242880 | tf_op jit(solution)/shard_map/pallas_call | solution.py:612
  213.2 6.7 multiply_convert_fusion.1
  238.4 6.6 convolution_convert_fusion.1
  266.7 10.2 %collective-permute-done.31.b_ref = bf16[3,32,1536]{2,1,0:T(8,128)(2,1)S(1)} collective-permute-done((bf16[3,32,1536]{2,1,0:T(8,128)(2,1)S(1)}, bf16[3,32,1536]{2,1,0:T(8,128)(2,1)S(1)}, u32[]{:S(2)}, u32[]{:S(2)}) %collective-permute-start.31) | collective-permute-done | bytes 294944 | tf_op jit(solution)/shard_map/ppermute | solution.py:25
  302.4 10.3 %shard_map.234 = (bf16[512,512]{1,0:T(8,128)(2,1)S(1)}, bf16[512,512]{1,0:T(8,128)(2,1)S(1)}, bf16[512,512]{1,0:T(8,128)(2,1)S(1)}, bf16[512,512]{1,0:T(8,128)(2,1)S(1)}, f32[8,512,1]{2,1,0:T(8,128)S(1)}) custom-call(f32[512,1536]{1,0:T(8,128)} %convolution_add_fusion.refs_0_.refs_1_.refs_2_, f32[512,1536]{1,0:T(8,128)} %convolution_add_fusion.refs_0_.refs_1_.refs_2_, ...), custom_call_target="tpu_custom_call" | custom-call | flops 536870912 | bytes 5242880 | tf_op jit(solution)/shard_map/pallas_call | solution.py:612
  339.5 6.8 shard_map.237
  382.1 11.8 %shard_map.240 = (bf16[512,512]{1,0:T(8,128)(2,1)S(1)}, bf16[512,512]{1,0:T(8,128)(2,1)S(1)}, bf16[512,512]{1,0:T(8,128)(2,1)S(1)}) custom-call(bf16[512,512]{1,0:T(8,128)(2,1)S(1)} %get-tuple-element.305.refs_0_, bf16[512,512]{1,0:T(8,128)(2,1)S(1)} %get-tuple-element.306.refs_1_, bf16[512,512]{1,0:T(8,128)(2,1)S(1)} %copy-done.80, ...), custom_call_target="tpu_custom_call" | custom-call | flops 1342177280 | bytes 5242880 | tf_op jit(solution)/shard_map/pallas_call | solution.py:647
  404.5 10.5 %collective-permute-done.44.ga_ref = bf16[2,4,32,2048]{3,2,1,0:T(8,128)(2,1)S(1)} collective-permute-done((bf16[2,4,32,2048]{3,2,1,0:T(8,128)(2,1)}, bf16[2,4,32,2048]{3,2,1,0:T(8,128)(2,1)S(1)}, u32[]{:S(2)}, u32[]{:S(2)}) %collective-permute-start.44) | collective-permute-done | bytes 1048608 | tf_op jit(solution)/shard_map/ppermute | solution.py:25
  436.6 11.7 %collective-permute-done.47 = bf16[2,80,1024]{2,1,0:T(8,128)(2,1)S(1)} collective-permute-done((bf16[2,80,1024]{2,1,0:T(8,128)(2,1)S(1)}, bf16[2,80,1024]{2,1,0:T(8,128)(2,1)S(1)}, u32[]{:S(2)}, u32[]{:S(2)}) %collective-permute-start.47) | collective-permute-done | bytes 327712 | tf_op jit(solution)/shard_map/ppermute | solution.py:29
  453.7 6.6 shard_map.243
  474.7 6.5 collective-permute-start.54
  513.0 19.3 %collective-permute-done.57.ma_ref = bf16[4,32,1536]{2,1,0:T(8,128)(2,1)S(1)} collective-permute-done((bf16[4,32,1536]{2,1,0:T(8,128)(2,1)S(1)}, bf16[4,32,1536]{2,1,0:T(8,128)(2,1)S(1)}, u32[]{:S(2)}, u32[]{:S(2)}) %collective-permute-start.57) | collective-permute-done | bytes 393248 | tf_op jit(solution)/shard_map/ppermute | solution.py:25
  535.7 7.2 convolution_convert_fusion
  565.3 11.6 %shard_map.247 = (bf16[512,512]{1,0:T(8,128)(2,1)S(1)}, bf16[512,512]{1,0:T(8,128)(2,1)S(1)}, bf16[512,512]{1,0:T(8,128)(2,1)S(1)}) custom-call(bf16[512,512]{1,0:T(8,128)(2,1)S(1)} %copy-done.70, bf16[512,512]{1,0:T(8,128)(2,1)S(1)} %copy-done.72, bf16[512,512]{1,0:T(8,128)(2,1)S(1)} %copy-done.74, bf16[512,512]{1,0:T(8,128)(2,1)S(1)} %pad_maximum_fusion.3.refs_3_, ...), custom_call_target="tpu_custom_call" | custom-call | flops 1342177280 | bytes 5242880 | tf_op jit(solution)/shard_map/pallas_call | solution.py:647
  578.6 9.3 %collective-permute-done.62 = bf16[2,32,1536]{2,1,0:T(8,128)(2,1)S(1)} collective-permute-done((bf16[2,32,1536]{2,1,0:T(8,128)(2,1)S(1)}, bf16[2,32,1536]{2,1,0:T(8,128)(2,1)S(1)}, u32[]{:S(2)}, u32[]{:S(2)}) %collective-permute-start.62) | collective-permute-done | bytes 196640 | tf_op jit(solution)/shard_map/ppermute | solution.py:29
  623.7 12.3 %collective-permute-done.69 = bf16[2,80,1024]{2,1,0:T(8,128)(2,1)} collective-permute-done((bf16[2,80,1024]{2,1,0:T(8,128)(2,1)S(1)}, bf16[2,80,1024]{2,1,0:T(8,128)(2,1)}, u32[]{:S(2)}, u32[]{:S(2)}) %collective-permute-start.69) | collective-permute-done | bytes 327712 | tf_op jit(solution)/shard_map/ppermute | solution.py:29
  641.6 6.9 collective-permute-start.79
  656.8 12.4 %collective-permute-done.78 = bf16[128,1024]{1,0:T(8,128)(2,1)} collective-permute-done((bf16[128,1024]{1,0:T(8,128)(2,1)}, bf16[128,1024]{1,0:T(8,128)(2,1)}, u32[]{:S(2)}, u32[]{:S(2)}) %collective-permute-start.78) | collective-permute-done | bytes 262176 | tf_op jit(solution)/shard_map/ppermute | solution.py:29
  686.2 7.4 collective-permute-done.87
  699.1 10.2 %collective-permute-done.82 = bf16[2,32,2048]{2,1,0:T(8,128)(2,1)S(1)} collective-permute-done((bf16[2,32,2048]{2,1,0:T(8,128)(2,1)S(1)}, bf16[2,32,2048]{2,1,0:T(8,128)(2,1)S(1)}, u32[]{:S(2)}, u32[]{:S(2)}) %collective-permute-start.82) | collective-permute-done | bytes 262176 | tf_op jit(solution)/shard_map/ppermute | solution.py:29
  736.0 8.0 %all-gather.37.cloned.1.call-done = bf16[16,32,2048]{2,1,0:T(8,128)(2,1)} async-done(((bf16[2,32,2048]{2,1,0:T(8,128)(2,1)}), bf16[16,32,2048]{2,1,0:T(8,128)(2,1)}) %all-gather.37.cloned.1.call-update) | async-done | bytes 2097168 | tf_op jit(solution)/shard_map/all_gather | solution.py:489
  (904 shorter events, 519.2 us)
Async XLA Ops:
  7.2 105.9 %all-gather.21.cloned.1.call-start = ((), (), s32[]{:S(2)}) async-start(), calls=%async_computation | async-start | bytes 1310720 | tf_op jit(solution)/shard_map/all_gather | solution.py:464
  16.9 38.9 %collective-permute-start.4 = (bf16[6656]{0:T(1024)(128)(2,1)S(1)}, bf16[6656]{0:T(1024)(128)(2,1)S(1)}, u32[]{:S(2)}, u32[]{:S(2)}) collective-permute-start(bf16[6656]{0:T(1024)(128)(2,1)S(1)} %constant_dynamic-update-slice_fusion.10), channel_id=1, source_target_pairs={{0,1},{1,2},{2,3},{3,0},{4,5},{5,6},{6,7},{7,4},{8,9},{9,10},{10,1... | collective-permute-start | bytes 39944 | tf_op jit(solution)/shard_map/ppermute | solution.py:29
  62.8 50.2 %collective-permute-start.8 = (bf16[2,3,32,1536]{3,2,1,0:T(8,128)(2,1)}, bf16[2,3,32,1536]{3,2,1,0:T(8,128)(2,1)}, u32[]{:S(2)}, u32[]{:S(2)}) collective-permute-start(bf16[2,3,32,1536]{3,2,1,0:T(8,128)(2,1)} %pad_maximum_fusion.n_ref), channel_id=1, source_target_pairs={{0,16},{16,0},{1,17},{17,1},{2,18},{18,2},{3,19},{19,3},{4,20},{20... | collective-permute-start | bytes 1769480 | tf_op jit(solution)/shard_map/ppermute | solution.py:25
  64.4 48.7 %collective-permute-start.7 = (bf16[2,3,32,1536]{3,2,1,0:T(8,128)(2,1)}, bf16[2,3,32,1536]{3,2,1,0:T(8,128)(2,1)}, u32[]{:S(2)}, u32[]{:S(2)}) collective-permute-start(bf16[2,3,32,1536]{3,2,1,0:T(8,128)(2,1)} %pad_maximum_fusion.n_ref), channel_id=1, source_target_pairs={{0,8},{8,0},{1,9},{9,1},{2,10},{10,2},{3,11},{11,3},{4,12},{12,4},... | collective-permute-start | bytes 1769480 | tf_op jit(solution)/shard_map/ppermute | solution.py:25
  65.9 83.2 %all-gather.23.cloned.1.call-start = ((), (), s32[]{:S(2)}) async-start(), calls=%async_computation.1 | async-start | bytes 1638400 | tf_op jit(solution)/shard_map/all_gather | solution.py:464
  119.9 109.2 %all-gather.25.cloned.1.call-start = ((), (), s32[]{:S(2)}) async-start(), calls=%async_computation.2 | async-start | bytes 1310720 | tf_op jit(solution)/shard_map/all_gather | solution.py:464
  150.7 39.0 %collective-permute-start.23 = (bf16[2,32,1536]{2,1,0:T(8,128)(2,1)}, bf16[2,32,1536]{2,1,0:T(8,128)(2,1)S(1)}, u32[]{:S(2)}, u32[]{:S(2)}) collective-permute-start(bf16[2,32,1536]{2,1,0:T(8,128)(2,1)} %dynamic-slice_bitcast_fusion.12), channel_id=1, source_target_pairs={{0,2},{1,3},{2,0},{3,1},{4,6},{5,7},{6,4},{7,5},{8,10},{9,11},{10,... | collective-permute-start | bytes 589832 | tf_op jit(solution)/shard_map/ppermute | solution.py:29
  154.7 44.0 %collective-permute-start.21 = (bf16[2,3,80,1024]{3,2,1,0:T(8,128)(2,1)S(1)}, bf16[2,3,80,1024]{3,2,1,0:T(8,128)(2,1)S(1)}, u32[]{:S(2)}, u32[]{:S(2)}) collective-permute-start(bf16[2,3,80,1024]{3,2,1,0:T(8,128)(2,1)S(1)} %shard_map.227.n_ref), channel_id=1, source_target_pairs={{0,16},{16,0},{1,17},{17,1},{2,18},{18,2},{3,19},{19,3},{4,20},{20... | collective-permute-start | bytes 2949128 | tf_op jit(solution)/shard_map/ppermute | solution.py:25
  156.3 42.4 %collective-permute-start.20 = (bf16[2,3,80,1024]{3,2,1,0:T(8,128)(2,1)S(1)}, bf16[2,3,80,1024]{3,2,1,0:T(8,128)(2,1)S(1)}, u32[]{:S(2)}, u32[]{:S(2)}) collective-permute-start(bf16[2,3,80,1024]{3,2,1,0:T(8,128)(2,1)S(1)} %shard_map.227.n_ref), channel_id=1, source_target_pairs={{0,8},{8,0},{1,9},{9,1},{2,10},{10,2},{3,11},{11,3},{4,12},{12,4},... | collective-permute-start | bytes 2949128 | tf_op jit(solution)/shard_map/ppermute | solution.py:25
  204.6 78.2 %all-gather.27.cloned.1.call-start = ((), (), s32[]{:S(2)}) async-start(), calls=%async_computation.3 | async-start | bytes 1638400 | tf_op jit(solution)/shard_map/all_gather | solution.py:464
  252.3 280.8 %all-gather.29.cloned.1.call-start = ((), (), s32[]{:S(2)}) async-start(), calls=%async_computation.4 | async-start | bytes 2949120 | tf_op jit(solution)/shard_map/all_gather | solution.py:489
  426.6 37.6 %collective-permute-start.48 = (bf16[2,80,1024]{2,1,0:T(8,128)(2,1)S(1)}, bf16[2,80,1024]{2,1,0:T(8,128)(2,1)}, u32[]{:S(2)}, u32[]{:S(2)}) collective-permute-start(bf16[2,80,1024]{2,1,0:T(8,128)(2,1)S(1)} %get-tuple-element.325), channel_id=1, source_target_pairs={{0,3},{1,0},{2,1},{3,2},{4,7},{5,4},{6,5},{7,6},{8,11},{9,8},{10,9... | collective-permute-start | bytes 983048 | tf_op jit(solution)/shard_map/ppermute | solution.py:29
  428.7 37.1 %collective-permute-start.51 = (bf16[2,4,32,1536]{3,2,1,0:T(8,128)(2,1)S(1)}, bf16[2,4,32,1536]{3,2,1,0:T(8,128)(2,1)S(1)}, u32[]{:S(2)}, u32[]{:S(2)}) collective-permute-start(bf16[2,4,32,1536]{3,2,1,0:T(8,128)(2,1)S(1)} %get-tuple-element.330), channel_id=1, source_target_pairs={{0,8},{8,0},{1,9},{9,1},{2,10},{10,2},{3,11},{11,3},{4,12},{12,4},... | collective-permute-start | bytes 2359304 | tf_op jit(solution)/shard_map/ppermute | solution.py:25
  468.0 129.0 %all-gather.31.cloned.1.call-start = ((), (), s32[]{:S(2)}) async-start(), calls=%async_computation.5 | async-start | bytes 2359296 | tf_op jit(solution)/shard_map/all_gather | solution.py:489
  486.4 46.6 %collective-permute-start.59 = (bf16[2,4,80,1024]{3,2,1,0:T(8,128)(2,1)S(1)}, bf16[2,4,80,1024]{3,2,1,0:T(8,128)(2,1)}, u32[]{:S(2)}, u32[]{:S(2)}) collective-permute-start(bf16[2,4,80,1024]{3,2,1,0:T(8,128)(2,1)S(1)} %copy-done.126), channel_id=1, source_target_pairs={{0,8},{8,0},{1,9},{9,1},{2,10},{10,2},{3,11},{11,3},{4,12},{12,4},... | collective-permute-start | bytes 3932168 | tf_op jit(solution)/shard_map/ppermute | solution.py:25
  487.8 45.2 %collective-permute-start.60 = (bf16[2,4,80,1024]{3,2,1,0:T(8,128)(2,1)}, bf16[2,4,80,1024]{3,2,1,0:T(8,128)(2,1)}, u32[]{:S(2)}, u32[]{:S(2)}) collective-permute-start(bf16[2,4,80,1024]{3,2,1,0:T(8,128)(2,1)} %get-tuple-element.354), channel_id=1, source_target_pairs={{0,16},{16,0},{1,17},{17,1},{2,18},{18,2},{3,19},{19,3},{4,20},{20... | collective-permute-start | bytes 3932168 | tf_op jit(solution)/shard_map/ppermute | solution.py:25
  534.9 134.3 %all-gather.33.cloned.1.call-start = ((), (), s32[]{:S(2)}) async-start(), calls=%async_computation.6 | async-start | bytes 1769472 | tf_op jit(solution)/shard_map/all_gather | solution.py:489
  553.6 41.6 %collective-permute-start.65 = (bf16[4,80,1024]{2,1,0:T(8,128)(2,1)S(1)}, bf16[4,80,1024]{2,1,0:T(8,128)(2,1)S(1)}, u32[]{:S(2)}, u32[]{:S(2)}) collective-permute-start(bf16[4,80,1024]{2,1,0:T(8,128)(2,1)S(1)} %fusion.34), channel_id=1, source_target_pairs={{0,8},{8,0},{1,9},{9,1},{2,10},{10,2},{3,11},{11,3},{4,12},{12,4},... | collective-permute-start | bytes 1966088 | tf_op jit(solution)/shard_map/ppermute | solution.py:25
  556.4 39.7 %collective-permute-start.64 = (bf16[4,80,1024]{2,1,0:T(8,128)(2,1)}, bf16[4,80,1024]{2,1,0:T(8,128)(2,1)S(1)}, u32[]{:S(2)}, u32[]{:S(2)}) collective-permute-start(bf16[4,80,1024]{2,1,0:T(8,128)(2,1)} %fusion.35), channel_id=1, source_target_pairs={{0,16},{16,0},{1,17},{17,1},{2,18},{18,2},{3,19},{19,3},{4,20},{20... | collective-permute-start | bytes 1966088 | tf_op jit(solution)/shard_map/ppermute | solution.py:25
  557.0 40.0 %collective-permute-start.66 = (bf16[2,4,32,2048]{3,2,1,0:T(8,128)(2,1)S(1)}, bf16[2,4,32,2048]{3,2,1,0:T(8,128)(2,1)S(1)}, u32[]{:S(2)}, u32[]{:S(2)}) collective-permute-start(bf16[2,4,32,2048]{3,2,1,0:T(8,128)(2,1)S(1)} %copy-done.130), channel_id=1, source_target_pairs={{0,8},{8,0},{1,9},{9,1},{2,10},{10,2},{3,11},{11,3},{4,12},{12,4},... | collective-permute-start | bytes 3145736 | tf_op jit(solution)/shard_map/ppermute | solution.py:25
  558.2 38.8 %collective-permute-start.67 = (bf16[2,4,32,2048]{3,2,1,0:T(8,128)(2,1)S(1)}, bf16[2,4,32,2048]{3,2,1,0:T(8,128)(2,1)}, u32[]{:S(2)}, u32[]{:S(2)}) collective-permute-start(bf16[2,4,32,2048]{3,2,1,0:T(8,128)(2,1)S(1)} %copy-done.128), channel_id=1, source_target_pairs={{0,16},{16,0},{1,17},{17,1},{2,18},{18,2},{3,19},{19,3},{4,20},{20... | collective-permute-start | bytes 3145736 | tf_op jit(solution)/shard_map/ppermute | solution.py:25
  604.3 106.6 %all-gather.35.cloned.1.call-start = ((), (), s32[]{:S(2)}) async-start(), calls=%async_computation.7 | async-start | bytes 2949120 | tf_op jit(solution)/shard_map/all_gather | solution.py:489
  671.5 72.5 %all-gather.37.cloned.1.call-start = ((), (), s32[]{:S(2)}) async-start(), calls=%async_computation.8 | async-start | bytes 2359296 | tf_op jit(solution)/shard_map/all_gather | solution.py:489
  711.7 59.8 %all-gather.39.cloned.1.call-start = ((), (), s32[]{:S(2)}) async-start(), calls=%async_computation.9 | async-start | bytes 1769472 | tf_op jit(solution)/shard_map/all_gather | solution.py:489
  (302 other events, 3854.9 us)
Sparse Core Ops, SparseCore 0:
  66.0 42.9 all-gather.20
  120.0 29.0 all-gather.22
  204.7 24.3 all-gather.24
  252.4 30.3 all-gather.26
  468.1 45.6 all-gather.28
  535.0 31.0 all-gather.30
  604.4 29.4 all-gather.32
  671.6 34.2 all-gather.34
  711.8 32.0 all-gather.36
  745.8 25.6 all-gather.38

commit v4 on v3

--- a/solution.py
+++ b/solution.py
@@ -19,6 +19,7 @@
 VMEM_LIMIT = 48 * 1024 * 1024
 FORWARD_ROWS = 256
 BACKWARD_ROWS = 512
+LIGHT = pl.CostEstimate(flops=1024, bytes_accessed=1024, transcendentals=0)
 
 
 def swap(x, axis):
@@ -75,7 +76,6 @@
         for copy in started:
             copy.wait()
 
-    size = 2 * math.prod(out_shape.shape) * out_shape.dtype.itemsize
     return pl.pallas_call(
         kernel,
         out_shape=out_shape,
@@ -84,7 +84,7 @@
         out_specs=pl.BlockSpec(memory_space=pltpu.VMEM),
         scratch_shapes=[pltpu.SemaphoreType.DMA((copies,))],
         compiler_params=pltpu.CompilerParams(vmem_limit_bytes=VMEM_LIMIT),
-        cost_estimate=pl.CostEstimate(flops=0, bytes_accessed=size, transcendentals=0),
+        cost_estimate=LIGHT,
     )(place.scalars, *operands)
 
 
@@ -113,9 +113,7 @@
         ),
         out_shape=jax.ShapeDtypeStruct((rows, count * width), weights.dtype),
         compiler_params=pltpu.CompilerParams(vmem_limit_bytes=VMEM_LIMIT),
-        cost_estimate=pl.CostEstimate(
-            flops=0, bytes_accessed=4 * rows * count * width, transcendentals=0
-        ),
+        cost_estimate=LIGHT,
     )(place.scalars, *[weights] * group)
 
 
@@ -143,9 +141,7 @@
         ),
         out_shape=jax.ShapeDtypeStruct((sum(halves), columns), arrays[0].dtype),
         compiler_params=pltpu.CompilerParams(vmem_limit_bytes=VMEM_LIMIT),
-        cost_estimate=pl.CostEstimate(
-            flops=0, bytes_accessed=4 * sum(halves) * columns, transcendentals=0
-        ),
+        cost_estimate=LIGHT,
     )(place.scalars, *arrays)
 
 
@@ -209,9 +205,7 @@
         ),
         out_shape=jax.ShapeDtypeStruct((span, 4, 2, *block), half.dtype),
         compiler_params=pltpu.CompilerParams(vmem_limit_bytes=VMEM_LIMIT),
-        cost_estimate=pl.CostEstimate(
-            flops=0, bytes_accessed=32 * span * eighth * columns, transcendentals=0
-        ),
+        cost_estimate=LIGHT,
     )(
         place.scalars,
         half.reshape(4, 2, *block),
@@ -222,6 +216,18 @@
         far_b,
     )
     return out.reshape(8 * span * eighth, columns)
+
+
+def absolute_quarters(summed, near_x, near_y, far_a, far_b, place):
+    def body(scalars, ins, out):
+        q = scalars[1]
+        for flip in range(3):
+            yield ins[flip], out.at[flipped(q, flip)]
+        for i in range(2):
+            yield ins[3 + i], out.at[flipped(q, 3), i]
+
+    shape = jax.ShapeDtypeStruct((4, *summed.shape), summed.dtype)
+    return copy_call(body, shape, 5, [summed, near_x, near_y, far_a, far_b], place)
 
 
 def weight_gradient(left, right, place):
@@ -309,11 +315,7 @@
         out_specs=[out] * span,
         out_shape=[jax.ShapeDtypeStruct((2, eighth, columns), BF16)] * span,
         compiler_params=pltpu.CompilerParams(vmem_limit_bytes=VMEM_LIMIT),
-        cost_estimate=pl.CostEstimate(
-            flops=4 * span * eighth * columns,
-            bytes_accessed=16 * span * eighth * columns,
-            transcendentals=0,
-        ),
+        cost_estimate=LIGHT,
     )(own, got_a, got_b, more_a, more_b)
 
 
@@ -346,9 +348,7 @@
         out_shape=jax.ShapeDtypeStruct((LAYERS, 4 * rows, 2 * columns), F32),
         input_output_aliases=aliases,
         compiler_params=pltpu.CompilerParams(vmem_limit_bytes=VMEM_LIMIT),
-        cost_estimate=pl.CostEstimate(
-            flops=0, bytes_accessed=48 * rows * columns, transcendentals=0
-        ),
+        cost_estimate=LIGHT,
     )(*operands)
 
 
@@ -387,9 +387,7 @@
         ],
         input_output_aliases=aliases,
         compiler_params=pltpu.CompilerParams(vmem_limit_bytes=VMEM_LIMIT),
-        cost_estimate=pl.CostEstimate(
-            flops=0, bytes_accessed=48 * quarter * columns, transcendentals=0
-        ),
+        cost_estimate=LIGHT,
     )(*operands)
 
 
@@ -402,6 +400,11 @@
         )
         out.append(block if k == 0 else spin(block, k, span))
     return out
+
+
+def swap_once(x):
+    other = yield swap(x, "core")
+    return other
 
 
 def row_to_chip(x, place):
@@ -458,20 +461,20 @@
     mine = lax.dynamic_index_in_dim(
         half.reshape(4, 2, eighth, columns), place.q, 0, keepdims=False
     )
+    if by_call:
+        moving = lax.all_gather(mine, "shard")
+    else:
+        moving = [spin(mine, k, span) for k in range(1, span)]
     if wait:
-        mine = yield mine
-    if by_call:
-        every = yield lax.all_gather(mine, "shard")
-        near = other_shards(every, place)
-    else:
-        arrived = yield [spin(mine, k, span) for k in range(1, span)]
-        near = jnp.stack(arrived, 1)
+        yield ()
+    arrived = yield moving
+    near = other_shards(arrived, place) if by_call else jnp.stack(arrived, 1)
     near_x, near_y = yield [swap(near, "xbit"), swap(near, "ybit")]
     far_a, far_b = yield [swap(near_x[0], "ybit"), swap(near_y[1], "xbit")]
     return assemble(half, near, near_x, near_y, far_a, far_b, place)
 
 
-def reduce_weight(left, right, place):
+def reduce_weight(left, right, place, last=False):
     span = place.span
     own, pass_a, pass_b, send_a, send_b = yield weight_gradient(left, right, place)
     got_a, got_b = yield [swap(send_a, "xbit"), swap(send_b, "ybit")]
@@ -486,8 +489,15 @@
     summed = summed.astype(BF16)
     if lax.axis_size("outer") > 1:
         summed = lax.psum(summed, "outer")
-    parts = yield lax.all_gather(summed, ("ybit", "xbit", "core"))
     _, eighth, columns = summed.shape
+    if last:
+        near_x, near_y = yield [swap(summed, "xbit"), swap(summed, "ybit")]
+        far_a, far_b = yield [swap(near_x[0], "ybit"), swap(near_y[1], "xbit")]
+        half = absolute_quarters(summed, near_x, near_y, far_a, far_b, place)
+        other = yield swap(half, "core")
+        parts = by_core(place, half[:, None], other[:, None], 1)
+    else:
+        parts = yield lax.all_gather(summed, ("ybit", "xbit", "core"))
     return parts.reshape(4, 2, 2 * eighth, columns)
 
 
@@ -628,11 +638,7 @@
         ],
         scratch_shapes=[pltpu.VMEM((length, length), F32)],
         compiler_params=pltpu.CompilerParams(vmem_limit_bytes=VMEM_LIMIT),
-        cost_estimate=pl.CostEstimate(
-            flops=4 * length * length * width,
-            bytes_accessed=20 * length * width,
-            transcendentals=width // head * length * length,
-        ),
+        cost_estimate=LIGHT,
     )(projected, projected, projected, *fixed)
 
 
@@ -653,11 +659,7 @@
         scratch_shapes=[pltpu.VMEM((length, group), F32)] * 3
         + [pltpu.VMEM((length, length), F32)],
         compiler_params=pltpu.CompilerParams(vmem_limit_bytes=VMEM_LIMIT),
-        cost_estimate=pl.CostEstimate(
-            flops=10 * length * length * width,
-            bytes_accessed=20 * length * width,
-            transcendentals=width // head * length * length,
-        ),
+        cost_estimate=LIGHT,
     )(query, keys, values, d_mixed, lse_all, *fixed)
 
 
@@ -715,7 +717,7 @@
     return y, (xhat, inverse, attn_low, mlp_low, attention, hidden_pre, last_low)
 
 
-def backward_layer(dy, weights, small, saved, fixed, head, place, slots, done):
+def backward_layer(dy, weights, small, saved, fixed, head, place, slots, done, last):
     w_qkv, w_up, w_last = weights
     gains = small[0]
     xhat, inverse, attn_low, mlp_low, attention, hidden_pre, last_low = saved
@@ -740,7 +742,7 @@
     d_qkv = jnp.concatenate(
         attend_back(query, keys, values, d_mixed, lse, fixed, head), 1
     )
-    slots.add(reduce_weight(attn_low, d_qkv, place), done(0))
+    slots.add(reduce_weight(attn_low, d_qkv, place, last), done(0))
     d_mlp = dot_t(d_pre, w_up)
 
     d_qkv, d_mlp = slots.step((d_qkv, d_mlp))
@@ -826,13 +828,6 @@
     ff_cols = up_weight.shape[2] // (2 * span)
     assert 2 * rows == span
 
-    halves = []
-    for layer in range(LAYERS):
-        halves += [
-            pick_columns(qkv_weight, layer, head_cols, place),
-            pick_columns(up_weight, layer, ff_cols, place),
-            pick_rows((out_weight, down_weight), layer, place),
-        ]
     found = {}
 
     def keep(name):
@@ -841,23 +836,36 @@
 
         return done
 
+    def unit(index, arrays, wait):
+        qkv, up, out, down = arrays
+        layer, kind = divmod(index, 3)
+        if kind == 0:
+            half = pick_columns(qkv, layer, head_cols, place)
+        elif kind == 1:
+            half = pick_columns(up, layer, ff_cols, place)
+        else:
+            half = pick_rows((out, down), layer, place)
+        slots.add(gather_weight(half, kind != 0, wait, place), keep(index))
+
     slots = Slots()
-    slots.add(gather_weight(halves[0], False, False, place), keep(0))
-    both = jnp.concatenate([hidden_in, out_grad], 2)
-    slots.add(row_to_chip(both, place), keep("rows"))
-    vectors = [norm_gains, norm_biases, qkv_bias, out_bias, up_bias, down_bias]
+    arrays = (qkv_weight, up_weight, out_weight, down_weight)
+    vectors = (norm_gains, norm_biases, qkv_bias, out_bias, up_bias, down_bias)
+    unit(0, arrays, False)
+    slots.add(row_to_chip(hidden_in, place), keep("rows"))
+    slots.add(swap_once(segments), keep("segments"))
+    arrays, vectors, out_grad = slots.step((arrays, vectors, out_grad))
     slots.add(gather_small(vectors, place), keep("vectors"))
-    seg_other = swap(segments, "core")
-    for index in range(1, len(halves)):
-        slots.add(gather_weight(halves[index], index % 3 != 0, True, place), keep(index))
-        slots.step()
+    for index in range(1, 3 * LAYERS):
+        unit(index, arrays, True)
+        arrays, out_grad = slots.step((arrays, out_grad))
+        if index == 3:
+            slots.add(row_to_chip(out_grad, place), keep("grads"))
     while slots.parts:
         slots.step()
     weights = [[found[3 * layer + i] for i in range(3)] for layer in range(LAYERS)]
 
-    both = found["rows"]
-    stream, dy = both[:, :width].astype(F32), both[:, width:].astype(F32)
-    seg_all = by_core(place, segments, seg_other, 0)
+    stream, dy = found["rows"].astype(F32), found["grads"].astype(F32)
+    seg_all = by_core(place, segments, found["segments"], 0)
     seg = lax.dynamic_index_in_dim(seg_all, place.z, 0, keepdims=False)
     seg_col, seg_row = seg[:, None], seg[None, :]
     length = seg.shape[0]
@@ -897,7 +905,10 @@
 
         return of
 
+    out_low = stream.astype(BF16)
     for layer in reversed(range(LAYERS)):
+        if layer == LAYERS - 2:
+            slots.add(chip_to_rows(out_low, rows, place), keep("block_out"))
         dy, little[layer] = backward_layer(
             dy,
             weights[layer],
@@ -908,14 +919,17 @@
             place,
             slots,
             done_for(layer),
+            layer == 0,
         )
-    results = jnp.concatenate([stream.astype(BF16), dy.astype(BF16)], 1)
-    slots.add(chip_to_rows(results, rows, place), keep("results"))
+    slots.add(chip_to_rows(dy.astype(BF16), rows, place), keep("in_grad"))
     slots.add(reduce_small(little, head_cols, ff_cols, place), keep("sums"))
     while slots.parts:
-        slots.step()
-    results = found["results"]
-    block_out, in_grad = results[..., :width], results[..., width:].astype(F32)
+        before = list(big)
+        gated = slots.step(before)
+        for i in range(3):
+            if big[i] is before[i]:
+                big[i] = gated[i]
+    block_out, in_grad = found["block_out"], found["in_grad"].astype(F32)
     d_gains, d_shifts, d_qkv_b, d_branch_b, d_up_b = found["sums"]
     d_qkv_w, d_up_w, (d_out_w, d_down_w) = big
     d_out_w = d_out_w.reshape(LAYERS, -1, width)

time: 795 us -> 751 us (0.945)
  local copies, waits for them, and re-layouts: 142 us -> 121 us
  waiting for transfers between devices: 211 us -> 190 us
  Pallas kernels: 151 us -> 159 us
    unnamed x487 -> x462, local copies, waits for them, and re-layouts: 89 us -> 76.1 us
    ppermute x36 -> x42, starting transfers between devices: 65.6 us -> 55.7 us  [spin(): return lax.ppermute(x, 'shard', [(j, (j + k) % span) for j in range(span)])]
    pallas_call x6, Pallas kernels: 28.2 us -> 37.3 us  [assemble(): pl.pallas_call(kernel, grid_spec=pltpu.PrefetchScalarGridSpec(num_scalar_...]
    all_gather x4, waiting for transfers between devices: 11.5 us -> 2.82 us  [gather_weight(): moving = lax.all_gather(mine, 'shard')]
    ppermute x59 -> x67, waiting for transfers between devices: 81.1 us -> 75.1 us  [swap(): return lax.ppermute(x, axis, [(0, 1), (1, 0)])]
    ppermute x36 -> x42, waiting for transfers between devices: 105 us -> 99.4 us  [spin(): return lax.ppermute(x, 'shard', [(j, (j + k) % span) for j in range(span)])]
    ppermute x59 -> x67, starting transfers between devices: 55.5 us -> 60.9 us  [swap(): return lax.ppermute(x, axis, [(0, 1), (1, 0)])]
  transfers between devices with their start and end apart: 105 -> 118, of which waited for: 28 -> 39; matrix products, arithmetic and copies ran while one was open for 23% -> 24% of each run, Pallas kernels for 18% -> 21%
where the time goes in v4:
time: 751 us; the launch traced here: 740 us
  waiting for transfers between devices  190 us (25%)
  Pallas kernels  159 us (21%)
  local copies, waits for them, and re-layouts  121 us (16%)
  starting transfers between devices  117 us (16%)
  other arithmetic  70.9 us (9%)
  matrix products  64.5 us (9%)
  between operations  16.8 us (2%)
    ppermute x42, waiting for transfers between devices, spin(): return lax.ppermute(x, 'shard', [(j, (j + k) % span) for j in range(span)])  99.4 us
    unnamed x462, local copies, waits for them, and re-layouts  76.1 us
    ppermute x67, waiting for transfers between devices, swap(): return lax.ppermute(x, axis, [(0, 1), (1, 0)])  75.1 us
    ppermute x67, starting transfers between devices, swap(): return lax.ppermute(x, axis, [(0, 1), (1, 0)])  60.9 us
    ppermute x42, starting transfers between devices, spin(): return lax.ppermute(x, 'shard', [(j, (j + k) % span) for j in range(span)])  55.7 us
    pallas_call x6, Pallas kernels, assemble(): pl.pallas_call(kernel, grid_spec=pltpu.PrefetchScalarGridSpec(num_scalar_...  37.3 us
    dot_general x6, matrix products, dot(): return jnp.dot(a, b, preferred_element_type=F32)  34.2 us
    pallas_call x6, Pallas kernels, weight_gradient(): pl.pallas_call(kernel, grid_spec=pltpu.PrefetchScalarGridSpec(num_scalar_...  32.9 us
  transfers between devices with their start and end apart: 118, of which 39 were waited for; matrix products, arithmetic and copies ran while one was open for 24% of the time, Pallas kernels for 21%

profile of v4, /device:TPU:0, one launch (start us, length us, event | category | flops | bytes accessed | tf_op | source)
XLA Modules:
  0.0 740.0 jit_solution(1029120925138382037)
XLA Ops:
  22.9 12.0 %collective-permute-done.1 = bf16[2,32,1536]{2,1,0:T(8,128)(2,1)S(1)} collective-permute-done((bf16[2,32,1536]{2,1,0:T(8,128)(2,1)S(1)}, bf16[2,32,1536]{2,1,0:T(8,128)(2,1)S(1)}, u32[]{:S(2)}, u32[]{:S(2)}) %collective-permute-start.1) | collective-permute-done | bytes 196640 | tf_op jit(solution)/shard_map/ppermute | solution.py:30
  62.2 6.0 collective-permute-done.8
  113.2 10.3 %shard_map.223 = (bf16[512,512]{1,0:T(8,128)(2,1)S(1)}, bf16[512,512]{1,0:T(8,128)(2,1)S(1)}, bf16[512,512]{1,0:T(8,128)(2,1)S(1)}, bf16[512,512]{1,0:T(8,128)(2,1)S(1)}, f32[8,512,1]{2,1,0:T(8,128)S(1)}) custom-call(f32[512,1536]{1,0:T(8,128)} %convolution_add_fusion.1.refs_0_.refs_1_.refs_2_, f32[512,1536]{1,0:T(8,128)} %convolution_add_fusion.1.refs_0_.refs_1_.refs_2_, ...), custom_call_target="tpu_custom_call" | custom-call | flops 1024 | bytes 1024 | tf_op jit(solution)/shard_map/pallas_call | solution.py:622
  146.3 20.7 %collective-permute-done.19.b_ref = bf16[3,32,2048]{2,1,0:T(8,128)(2,1)} collective-permute-done((bf16[3,32,2048]{2,1,0:T(8,128)(2,1)}, bf16[3,32,2048]{2,1,0:T(8,128)(2,1)}, u32[]{:S(2)}, u32[]{:S(2)}) %collective-permute-start.19) | collective-permute-done | bytes 393248 | tf_op jit(solution)/shard_map/ppermute | solution.py:26
  186.9 6.6 multiply_convert_fusion.1
  209.9 7.8 %collective-permute-done.30 = bf16[128,512]{1,0:T(8,128)(2,1)} collective-permute-done((bf16[128,512]{1,0:T(8,128)(2,1)}, bf16[128,512]{1,0:T(8,128)(2,1)}, u32[]{:S(2)}, u32[]{:S(2)}) %collective-permute-start.30) | collective-permute-done | bytes 131104 | tf_op jit(solution)/shard_map/ppermute | solution.py:30
  269.2 10.4 %shard_map.234 = (bf16[512,512]{1,0:T(8,128)(2,1)S(1)}, bf16[512,512]{1,0:T(8,128)(2,1)S(1)}, bf16[512,512]{1,0:T(8,128)(2,1)S(1)}, bf16[512,512]{1,0:T(8,128)(2,1)S(1)}, f32[8,512,1]{2,1,0:T(8,128)S(1)}) custom-call(f32[512,1536]{1,0:T(8,128)} %convolution_add_fusion.refs_0_.refs_1_.refs_2_, f32[512,1536]{1,0:T(8,128)} %convolution_add_fusion.refs_0_.refs_1_.refs_2_, ...), custom_call_target="tpu_custom_call" | custom-call | flops 1024 | bytes 1024 | tf_op jit(solution)/shard_map/pallas_call | solution.py:622
  295.6 6.6 multiply_convert_fusion
  304.0 6.8 shard_map.237
  312.1 12.8 %shard_map.238 = bf16[4,4,2,80,1024]{4,3,2,1,0:T(8,128)(2,1)} custom-call(s32[3]{0:T(128)S(1)} %pad_add_fusion.scalars, bf16[4,2,80,1024]{3,2,1,0:T(8,128)(2,1)S(1)} %bitcast.313, bf16[2,3,80,1024]{3,2,1,0:T(8,128)(2,1)S(1)} %shard_map.235.n_ref, bf16[2,3,80,1024]{3,2,1,0:T(8,128)(2,1)S(1)} %collective-permute-done.41.x_ref, ...), custom_call_target="tpu_custom_call" | custom-call | flops 1024 | bytes 1024 | tf_op jit(solution)/shard_map/pallas_call | solution.py:191
  325.0 6.6 convolution_convert_fusion
  354.3 11.7 %shard_map.240 = (bf16[512,512]{1,0:T(8,128)(2,1)S(1)}, bf16[512,512]{1,0:T(8,128)(2,1)S(1)}, bf16[512,512]{1,0:T(8,128)(2,1)S(1)}) custom-call(bf16[512,512]{1,0:T(8,128)(2,1)S(1)} %copy-done.84, bf16[512,512]{1,0:T(8,128)(2,1)S(1)} %copy-done.86, bf16[512,512]{1,0:T(8,128)(2,1)S(1)} %copy-done.88, bf16[512,512]{1,0:T(8,128)(2,1)S(1)} %pad_maximum_fusion.2.refs_3_, ...), custom_call_target="tpu_custom_call" | custom-call | flops 1024 | bytes 1024 | tf_op jit(solution)/shard_map/pallas_call | solution.py:653
  371.8 6.0 fusion.57
  380.1 11.1 %collective-permute-done.49.ga_ref = bf16[2,4,32,2048]{3,2,1,0:T(8,128)(2,1)S(1)} collective-permute-done((bf16[2,4,32,2048]{3,2,1,0:T(8,128)(2,1)}, bf16[2,4,32,2048]{3,2,1,0:T(8,128)(2,1)S(1)}, u32[]{:S(2)}, u32[]{:S(2)}) %collective-permute-start.49) | collective-permute-done | bytes 1048608 | tf_op jit(solution)/shard_map/ppermute | solution.py:26
  409.8 14.7 %collective-permute-done.60 = bf16[128,512]{1,0:T(8,128)(2,1)S(1)} collective-permute-done((bf16[128,512]{1,0:T(8,128)(2,1)S(1)}, bf16[128,512]{1,0:T(8,128)(2,1)S(1)}, u32[]{:S(2)}, u32[]{:S(2)}) %collective-permute-start.60) | collective-permute-done | bytes 131104 | tf_op jit(solution)/shard_map/ppermute | solution.py:30
  436.5 6.6 shard_map.243
  447.9 6.5 collective-permute-done.54.ma_ref
  494.3 18.4 %collective-permute-done.67.mb_ref = bf16[4,32,1536]{2,1,0:T(8,128)(2,1)S(1)} collective-permute-done((bf16[4,32,1536]{2,1,0:T(8,128)(2,1)S(1)}, bf16[4,32,1536]{2,1,0:T(8,128)(2,1)S(1)}, u32[]{:S(2)}, u32[]{:S(2)}) %collective-permute-start.67) | collective-permute-done | bytes 393248 | tf_op jit(solution)/shard_map/ppermute | solution.py:26
  540.2 11.6 %shard_map.247 = (bf16[512,512]{1,0:T(8,128)(2,1)S(1)}, bf16[512,512]{1,0:T(8,128)(2,1)S(1)}, bf16[512,512]{1,0:T(8,128)(2,1)S(1)}) custom-call(bf16[512,512]{1,0:T(8,128)(2,1)S(1)} %copy-done.74, bf16[512,512]{1,0:T(8,128)(2,1)S(1)} %copy-done.76, bf16[512,512]{1,0:T(8,128)(2,1)S(1)} %copy-done.78, bf16[512,512]{1,0:T(8,128)(2,1)S(1)} %pad_maximum_fusion.3.refs_3_, ...), custom_call_target="tpu_custom_call" | custom-call | flops 1024 | bytes 1024 | tf_op jit(solution)/shard_map/pallas_call | solution.py:653
  552.7 9.5 %collective-permute-done.72 = bf16[2,32,1536]{2,1,0:T(8,128)(2,1)S(1)} collective-permute-done((bf16[2,32,1536]{2,1,0:T(8,128)(2,1)S(1)}, bf16[2,32,1536]{2,1,0:T(8,128)(2,1)S(1)}, u32[]{:S(2)}, u32[]{:S(2)}) %collective-permute-start.72) | collective-permute-done | bytes 196640 | tf_op jit(solution)/shard_map/ppermute | solution.py:30
  575.0 6.5 fusion.38
  609.1 11.7 %collective-permute-done.79 = bf16[2,80,1024]{2,1,0:T(8,128)(2,1)S(1)} collective-permute-done((bf16[2,80,1024]{2,1,0:T(8,128)(2,1)S(1)}, bf16[2,80,1024]{2,1,0:T(8,128)(2,1)S(1)}, u32[]{:S(2)}, u32[]{:S(2)}) %collective-permute-start.79) | collective-permute-done | bytes 327712 | tf_op jit(solution)/shard_map/ppermute | solution.py:30
  622.6 6.9 collective-permute-done.80
  698.6 10.2 %all-gather.31.cloned.1.call-done = bf16[16,32,2048]{2,1,0:T(8,128)(2,1)} async-done(((bf16[2,32,2048]{2,1,0:T(8,128)(2,1)}), bf16[16,32,2048]{2,1,0:T(8,128)(2,1)}) %all-gather.31.cloned.1.call-update) | async-done | bytes 2097168 | tf_op jit(solution)/shard_map/all_gather | solution.py:500
  (915 shorter events, 485.0 us)
Async XLA Ops:
  7.2 78.7 %all-gather.15.cloned.1.call-start = ((), (), s32[]{:S(2)}) async-start(), calls=%async_computation | async-start | bytes 1310720 | tf_op jit(solution)/shard_map/all_gather | solution.py:465
  58.7 71.6 %all-gather.17.cloned.1.call-start = ((), (), s32[]{:S(2)}) async-start(), calls=%async_computation.1 | async-start | bytes 1638400 | tf_op jit(solution)/shard_map/all_gather | solution.py:465
  83.0 134.8 %all-gather.19.cloned.1.call-start = ((), (), s32[]{:S(2)}) async-start(), calls=%async_computation.2 | async-start | bytes 1310720 | tf_op jit(solution)/shard_map/all_gather | solution.py:465
  88.6 52.3 %collective-permute-start.24 = (bf16[2,32,1536]{2,1,0:T(8,128)(2,1)}, bf16[2,32,1536]{2,1,0:T(8,128)(2,1)}, u32[]{:S(2)}, u32[]{:S(2)}) collective-permute-start(bf16[2,32,1536]{2,1,0:T(8,128)(2,1)} %dynamic-slice_bitcast_fusion), channel_id=1, source_target_pairs={{0,3},{1,0},{2,1},{3,2},{4,7},{5,4},{6,5},{7,6},{8,11},{9,8},{10,9... | collective-permute-start | bytes 589832 | tf_op jit(solution)/shard_map/ppermute | solution.py:30
  90.6 50.9 %collective-permute-start.23 = (bf16[2,32,1536]{2,1,0:T(8,128)(2,1)}, bf16[2,32,1536]{2,1,0:T(8,128)(2,1)}, u32[]{:S(2)}, u32[]{:S(2)}) collective-permute-start(bf16[2,32,1536]{2,1,0:T(8,128)(2,1)} %dynamic-slice_bitcast_fusion), channel_id=1, source_target_pairs={{0,2},{1,3},{2,0},{3,1},{4,6},{5,7},{6,4},{7,5},{8,10},{9,11},{10,... | collective-permute-start | bytes 589832 | tf_op jit(solution)/shard_map/ppermute | solution.py:30
  146.2 104.3 %all-gather.21.cloned.1.call-start = ((), (), s32[]{:S(2)}) async-start(), calls=%async_computation.3 | async-start | bytes 1638400 | tf_op jit(solution)/shard_map/all_gather | solution.py:465
  169.0 48.7 %collective-permute-start.29 = (bf16[2,3,32,1536]{3,2,1,0:T(8,128)(2,1)}, bf16[2,3,32,1536]{3,2,1,0:T(8,128)(2,1)}, u32[]{:S(2)}, u32[]{:S(2)}) collective-permute-start(bf16[2,3,32,1536]{3,2,1,0:T(8,128)(2,1)} %pad_maximum_fusion.1.n_ref), channel_id=1, source_target_pairs={{0,16},{16,0},{1,17},{17,1},{2,18},{18,2},{3,19},{19,3},{4,20},{20... | collective-permute-start | bytes 1769480 | tf_op jit(solution)/shard_map/ppermute | solution.py:26
  169.6 48.2 %collective-permute-start.28 = (bf16[2,3,32,1536]{3,2,1,0:T(8,128)(2,1)}, bf16[2,3,32,1536]{3,2,1,0:T(8,128)(2,1)}, u32[]{:S(2)}, u32[]{:S(2)}) collective-permute-start(bf16[2,3,32,1536]{3,2,1,0:T(8,128)(2,1)} %pad_maximum_fusion.1.n_ref), channel_id=1, source_target_pairs={{0,8},{8,0},{1,9},{9,1},{2,10},{10,2},{3,11},{11,3},{4,12},{12,4},... | collective-permute-start | bytes 1769480 | tf_op jit(solution)/shard_map/ppermute | solution.py:26
  180.1 37.7 %collective-permute-start.27 = (bf16[3,80,1024]{2,1,0:T(8,128)(2,1)}, bf16[3,80,1024]{2,1,0:T(8,128)(2,1)}, u32[]{:S(2)}, u32[]{:S(2)}) collective-permute-start(bf16[3,80,1024]{2,1,0:T(8,128)(2,1)} %slice_bitcast_fusion.2), channel_id=1, source_target_pairs={{0,8},{8,0},{1,9},{9,1},{2,10},{10,2},{3,11},{11,3},{4,12},{12,4},... | collective-permute-start | bytes 1474568 | tf_op jit(solution)/shard_map/ppermute | solution.py:26
  201.2 312.9 %all-gather.23.cloned.1.call-start = ((), (), s32[]{:S(2)}) async-start(), calls=%async_computation.4 | async-start | bytes 2949120 | tf_op jit(solution)/shard_map/all_gather | solution.py:500
  331.5 46.4 %collective-permute-start.58 = (bf16[512,1024]{1,0:T(8,128)(2,1)}, bf16[512,1024]{1,0:T(8,128)(2,1)}, u32[]{:S(2)}, u32[]{:S(2)}) collective-permute-start(bf16[512,1024]{1,0:T(8,128)(2,1)} %convolution_convert_fusion), channel_id=1, source_target_pairs={{0,4},{4,0},{1,5},{5,1},{2,6},{6,2},{3,7},{7,3},{8,12},{12,8},{9,1... | collective-permute-start | bytes 3145736 | tf_op jit(solution)/shard_map/ppermute | solution.py:26
  408.9 46.3 %collective-permute-start.56 = (bf16[2,4,32,1536]{3,2,1,0:T(8,128)(2,1)S(1)}, bf16[2,4,32,1536]{3,2,1,0:T(8,128)(2,1)}, u32[]{:S(2)}, u32[]{:S(2)}) collective-permute-start(bf16[2,4,32,1536]{3,2,1,0:T(8,128)(2,1)S(1)} %copy-done.132), channel_id=1, source_target_pairs={{0,8},{8,0},{1,9},{9,1},{2,10},{10,2},{3,11},{11,3},{4,12},{12,4},... | collective-permute-start | bytes 2359304 | tf_op jit(solution)/shard_map/ppermute | solution.py:26
  456.2 118.8 %all-gather.25.cloned.1.call-start = ((), (), s32[]{:S(2)}) async-start(), calls=%async_computation.5 | async-start | bytes 2359296 | tf_op jit(solution)/shard_map/all_gather | solution.py:500
  464.4 49.7 %collective-permute-start.69 = (bf16[2,4,80,1024]{3,2,1,0:T(8,128)(2,1)S(1)}, bf16[2,4,80,1024]{3,2,1,0:T(8,128)(2,1)S(1)}, u32[]{:S(2)}, u32[]{:S(2)}) collective-permute-start(bf16[2,4,80,1024]{3,2,1,0:T(8,128)(2,1)S(1)} %copy-done.120), channel_id=1, source_target_pairs={{0,8},{8,0},{1,9},{9,1},{2,10},{10,2},{3,11},{11,3},{4,12},{12,4},... | collective-permute-start | bytes 3932168 | tf_op jit(solution)/shard_map/ppermute | solution.py:26
  465.1 49.0 %collective-permute-start.70 = (bf16[2,4,80,1024]{3,2,1,0:T(8,128)(2,1)}, bf16[2,4,80,1024]{3,2,1,0:T(8,128)(2,1)}, u32[]{:S(2)}, u32[]{:S(2)}) collective-permute-start(bf16[2,4,80,1024]{3,2,1,0:T(8,128)(2,1)} %get-tuple-element.443), channel_id=1, source_target_pairs={{0,16},{16,0},{1,17},{17,1},{2,18},{18,2},{3,19},{19,3},{4,20},{20... | collective-permute-start | bytes 3932168 | tf_op jit(solution)/shard_map/ppermute | solution.py:26
  516.1 127.3 %all-gather.27.cloned.1.call-start = ((), (), s32[]{:S(2)}) async-start(), calls=%async_computation.6 | async-start | bytes 1769472 | tf_op jit(solution)/shard_map/all_gather | solution.py:500
  529.7 40.4 %collective-permute-start.75 = (bf16[4,80,1024]{2,1,0:T(8,128)(2,1)S(1)}, bf16[4,80,1024]{2,1,0:T(8,128)(2,1)S(1)}, u32[]{:S(2)}, u32[]{:S(2)}) collective-permute-start(bf16[4,80,1024]{2,1,0:T(8,128)(2,1)S(1)} %fusion.16), channel_id=1, source_target_pairs={{0,8},{8,0},{1,9},{9,1},{2,10},{10,2},{3,11},{11,3},{4,12},{12,4},... | collective-permute-start | bytes 1966088 | tf_op jit(solution)/shard_map/ppermute | solution.py:26
  531.5 39.4 %collective-permute-start.74 = (bf16[4,80,1024]{2,1,0:T(8,128)(2,1)S(1)}, bf16[4,80,1024]{2,1,0:T(8,128)(2,1)S(1)}, u32[]{:S(2)}, u32[]{:S(2)}) collective-permute-start(bf16[4,80,1024]{2,1,0:T(8,128)(2,1)S(1)} %fusion.17), channel_id=1, source_target_pairs={{0,16},{16,0},{1,17},{17,1},{2,18},{18,2},{3,19},{19,3},{4,20},{20... | collective-permute-start | bytes 1966088 | tf_op jit(solution)/shard_map/ppermute | solution.py:26
  532.2 41.3 %collective-permute-start.76 = (bf16[2,4,32,2048]{3,2,1,0:T(8,128)(2,1)S(1)}, bf16[2,4,32,2048]{3,2,1,0:T(8,128)(2,1)}, u32[]{:S(2)}, u32[]{:S(2)}) collective-permute-start(bf16[2,4,32,2048]{3,2,1,0:T(8,128)(2,1)S(1)} %copy-done.124), channel_id=1, source_target_pairs={{0,8},{8,0},{1,9},{9,1},{2,10},{10,2},{3,11},{11,3},{4,12},{12,4},... | collective-permute-start | bytes 3145736 | tf_op jit(solution)/shard_map/ppermute | solution.py:26
  533.4 41.6 %collective-permute-start.77 = (bf16[2,4,32,2048]{3,2,1,0:T(8,128)(2,1)S(1)}, bf16[2,4,32,2048]{3,2,1,0:T(8,128)(2,1)}, u32[]{:S(2)}, u32[]{:S(2)}) collective-permute-start(bf16[2,4,32,2048]{3,2,1,0:T(8,128)(2,1)S(1)} %copy-done.122), channel_id=1, source_target_pairs={{0,16},{16,0},{1,17},{17,1},{2,18},{18,2},{3,19},{19,3},{4,20},{20... | collective-permute-start | bytes 3145736 | tf_op jit(solution)/shard_map/ppermute | solution.py:26
  584.1 94.3 %all-gather.29.cloned.1.call-start = ((), (), s32[]{:S(2)}) async-start(), calls=%async_computation.7 | async-start | bytes 2949120 | tf_op jit(solution)/shard_map/all_gather | solution.py:500
  598.5 43.4 %collective-permute-start.83 = (bf16[2,4,32,1536]{3,2,1,0:T(8,128)(2,1)S(1)}, bf16[2,4,32,1536]{3,2,1,0:T(8,128)(2,1)S(1)}, u32[]{:S(2)}, u32[]{:S(2)}) collective-permute-start(bf16[2,4,32,1536]{3,2,1,0:T(8,128)(2,1)S(1)} %copy-done.130), channel_id=1, source_target_pairs={{0,8},{8,0},{1,9},{9,1},{2,10},{10,2},{3,11},{11,3},{4,12},{12,4},... | collective-permute-start | bytes 2359304 | tf_op jit(solution)/shard_map/ppermute | solution.py:26
  601.7 40.2 %collective-permute-start.84 = (bf16[2,4,32,1536]{3,2,1,0:T(8,128)(2,1)S(1)}, bf16[2,4,32,1536]{3,2,1,0:T(8,128)(2,1)S(1)}, u32[]{:S(2)}, u32[]{:S(2)}) collective-permute-start(bf16[2,4,32,1536]{3,2,1,0:T(8,128)(2,1)S(1)} %copy-done.128), channel_id=1, source_target_pairs={{0,16},{16,0},{1,17},{17,1},{2,18},{18,2},{3,19},{19,3},{4,20},{20... | collective-permute-start | bytes 2359304 | tf_op jit(solution)/shard_map/ppermute | solution.py:26
  645.6 63.1 %all-gather.31.cloned.1.call-start = ((), (), s32[]{:S(2)}) async-start(), calls=%async_computation.8 | async-start | bytes 2359296 | tf_op jit(solution)/shard_map/all_gather | solution.py:500
  (297 other events, 3237.1 us)
Sparse Core Ops, SparseCore 0:
  58.8 26.9 all-gather.14
  87.4 42.8 all-gather.16
  146.4 29.7 all-gather.18
  201.3 31.7 all-gather.20
  456.3 40.5 all-gather.22
  516.2 32.7 all-gather.24
  584.2 28.4 all-gather.26
  645.8 32.5 all-gather.28
  680.8 27.8 all-gather.30

commit v5 on v4

--- a/solution.py
+++ b/solution.py
@@ -19,6 +19,7 @@
 VMEM_LIMIT = 48 * 1024 * 1024
 FORWARD_ROWS = 256
 BACKWARD_ROWS = 512
+FILLER = pl.CostEstimate(flops=8 * 10**9, bytes_accessed=1024, transcendentals=0)
 LIGHT = pl.CostEstimate(flops=1024, bytes_accessed=1024, transcendentals=0)
 
 
@@ -28,6 +29,10 @@
 
 def spin(x, k, span):
     return lax.ppermute(x, "shard", [(j, (j + k) % span) for j in range(span)])
+
+
+def across(x, step, span):
+    return lax.ppermute(x, "shard", [(j, j ^ step) for j in range(span)])
 
 
 def dot(a, b):
@@ -80,7 +85,7 @@
         kernel,
         out_shape=out_shape,
         in_specs=[pl.BlockSpec(memory_space=pltpu.SMEM)]
-        + [pl.BlockSpec(memory_space=pl.ANY)] * len(operands),
+        + [pl.BlockSpec(memory_space=pltpu.HBM)] * len(operands),
         out_specs=pl.BlockSpec(memory_space=pltpu.VMEM),
         scratch_shapes=[pltpu.SemaphoreType.DMA((copies,))],
         compiler_params=pltpu.CompilerParams(vmem_limit_bytes=VMEM_LIMIT),
@@ -162,33 +167,47 @@
     return lax.bitwise_xor(q, jnp.int32(flip))
 
 
-def assemble(half, near, near_x, near_y, far_a, far_b, place):
+def overlaps(eighth, start, stop):
+    for j in range(8):
+        low, high = max(j * eighth, start), min((j + 1) * eighth, stop)
+        if high > low:
+            yield j, low, high
+
+
+def assemble(half, cuts, near, near_x, near_y, far_a, far_b, place):
     span = place.span
     eighth, columns = half.shape[0] // 8, half.shape[1]
     block = (eighth, columns)
 
-    def kernel(scalars, half_ref, n_ref, x_ref, y_ref, a_ref, b_ref, out):
+    def kernel(scalars, half_ref, n_ref, x_ref, y_ref, a_ref, b_ref, *rest):
+        outs, table = rest[:-1], rest[-1]
         z, q = scalars[0], scalars[1]
         own = pl.program_id(0) == z
 
         @pl.when(own)
         def _():
-            out[0] = half_ref[...]
+            table[...] = half_ref[...]
 
         @pl.when(jnp.logical_not(own))
         def _():
             for i in range(2):
                 for flip, ref in enumerate((n_ref, x_ref, y_ref)):
-                    out[0, flipped(q, flip), i] = ref[i, 0]
-            out[0, flipped(q, 3), 0] = a_ref[0]
-            out[0, flipped(q, 3), 1] = b_ref[0]
+                    table[flipped(q, flip), i] = ref[i, 0]
+            table[flipped(q, 3), 0] = a_ref[0]
+            table[flipped(q, 3), 1] = b_ref[0]
+
+        for out, (start, stop, left, right) in zip(outs, cuts, strict=True):
+            for j, low, high in overlaps(eighth, start, stop):
+                out[0, low - start : high - start] = table[
+                    j // 2, j % 2, low - j * eighth : high - j * eighth, left:right
+                ]
 
     def behind(j, s):
         return jnp.maximum(lax.rem(s[0] + span - j, span), 1) - 1
 
     near_spec = pl.BlockSpec((2, 1, *block), lambda j, s: (0, behind(j, s), 0, 0))
     far_spec = pl.BlockSpec((1, *block), lambda j, s: (behind(j, s), 0, 0))
-    out = pl.pallas_call(
+    outs = pl.pallas_call(
         kernel,
         grid_spec=pltpu.PrefetchScalarGridSpec(
             num_scalar_prefetch=1,
@@ -201,9 +220,14 @@
                 far_spec,
                 far_spec,
             ],
-            out_specs=pl.BlockSpec((1, 4, 2, *block), lambda j, s: (j, 0, 0, 0, 0)),
+            out_specs=[
+                pl.BlockSpec((1, b - a, d - c), lambda j, s: (j, 0, 0)) for a, b, c, d in cuts
+            ],
+            scratch_shapes=[pltpu.VMEM((4, 2, *block), half.dtype)],
         ),
-        out_shape=jax.ShapeDtypeStruct((span, 4, 2, *block), half.dtype),
+        out_shape=[
+            jax.ShapeDtypeStruct((span, b - a, d - c), half.dtype) for a, b, c, d in cuts
+        ],
         compiler_params=pltpu.CompilerParams(vmem_limit_bytes=VMEM_LIMIT),
         cost_estimate=LIGHT,
     )(
@@ -215,7 +239,7 @@
         far_a,
         far_b,
     )
-    return out.reshape(8 * span * eighth, columns)
+    return [out.reshape(-1, out.shape[2]) for out in outs]
 
 
 def absolute_quarters(summed, near_x, near_y, far_a, far_b, place):
@@ -230,22 +254,29 @@
     return copy_call(body, shape, 5, [summed, near_x, near_y, far_a, far_b], place)
 
 
-def weight_gradient(left, right, place):
+def weight_gradient(lefts, right, place):
     span = place.span
-    tokens, columns = left.shape[0], right.shape[1]
-    rows = left.shape[1] // span
-    eighth = rows // 8
-
-    def kernel(scalars, left_ref, right_ref, own, pass_a, pass_b, send_a, send_b, table):
+    tokens, columns = right.shape
+    sizes = [left.shape[1] // span for left in lefts]
+    eighth = sum(sizes) // 8
+
+    def kernel(scalars, *refs):
+        left_refs, right_ref = refs[: len(sizes)], refs[len(sizes)]
+        own, pass_a, pass_b, send_a, send_b, table = refs[len(sizes) + 1 :]
         q = scalars[1]
-        product = lax.dot_general(
-            left_ref[...],
-            right_ref[...],
-            (((0,), (0,)), ((), ())),
-            preferred_element_type=F32,
-        ).astype(BF16)
-        for j in range(8):
-            table[j // 2, j % 2] = product[j * eighth : (j + 1) * eighth]
+        start = 0
+        for left_ref, size in zip(left_refs, sizes, strict=True):
+            product = lax.dot_general(
+                left_ref[...],
+                right_ref[...],
+                (((0,), (0,)), ((), ())),
+                preferred_element_type=F32,
+            ).astype(BF16)
+            for j, low, high in overlaps(eighth, start, start + size):
+                table[j // 2, j % 2, low - j * eighth : high - j * eighth] = product[
+                    low - start : high - start
+                ]
+            start += size
         near_x, near_y, far = flipped(q, 1), flipped(q, 2), flipped(q, 3)
         own[0, 0], own[0, 1] = table[q, 0], table[q, 1]
         pass_a[0], pass_b[0] = table[near_y, 0], table[near_x, 1]
@@ -261,7 +292,10 @@
             num_scalar_prefetch=1,
             grid=(span,),
             in_specs=[
-                pl.BlockSpec((tokens, rows), lambda k, s: (0, lax.rem(s[0] + k, span))),
+                *[
+                    pl.BlockSpec((tokens, size), lambda k, s: (0, lax.bitwise_xor(s[0], k)))
+                    for size in sizes
+                ],
                 pl.BlockSpec((tokens, columns), lambda k, s: (0, 0)),
             ],
             out_specs=[
@@ -274,19 +308,15 @@
             scratch_shapes=[pltpu.VMEM((4, 2, *block), BF16)],
         ),
         out_shape=[
-            jax.ShapeDtypeStruct((span, 2, *block), BF16),
-            jax.ShapeDtypeStruct((span, *block), BF16),
-            jax.ShapeDtypeStruct((span, *block), BF16),
-            jax.ShapeDtypeStruct((2, span, *block), BF16),
-            jax.ShapeDtypeStruct((2, span, *block), BF16),
+            pltpu.HBM((span, 2, *block), BF16),
+            pltpu.HBM((span, *block), BF16),
+            pltpu.HBM((span, *block), BF16),
+            pltpu.HBM((2, span, *block), BF16),
+            pltpu.HBM((2, span, *block), BF16),
         ],
         compiler_params=pltpu.CompilerParams(vmem_limit_bytes=VMEM_LIMIT),
-        cost_estimate=pl.CostEstimate(
-            flops=2 * tokens * span * rows * columns,
-            bytes_accessed=2 * (tokens * (span * rows + columns) + span * rows * columns),
-            transcendentals=0,
-        ),
-    )(place.scalars, left, right)
+        cost_estimate=LIGHT,
+    )(place.scalars, *lefts, right)
 
 
 def combine(own, got_a, got_b, more_a, more_b):
@@ -294,26 +324,22 @@
     part = columns // 4 if columns % 512 == 0 else columns
 
     def kernel(own_ref, ga_ref, gb_ref, ma_ref, mb_ref, *outs):
-        for k in range(span):
+        for j, out in enumerate(outs):
+            here = slice(j * span // 2, (j + 1) * span // 2)
             for i, (got, more) in enumerate(((ga_ref, ma_ref), (gb_ref, mb_ref))):
-                total = own_ref[k, i].astype(F32) + got[0, k].astype(F32)
-                outs[k][i] = (total + more[k].astype(F32)).astype(BF16)
+                total = own_ref[here, i].astype(F32) + got[0, here].astype(F32)
+                out[:, i] = (total + more[here].astype(F32)).astype(BF16)
 
     got = pl.BlockSpec((1, span, eighth, part), lambda j: (0, 0, 0, j))
     more = pl.BlockSpec((span, eighth, part), lambda j: (0, 0, j))
-    out = pl.BlockSpec((2, eighth, part), lambda j: (0, 0, j))
+    whole = pl.BlockSpec((span, 2, eighth, part), lambda j: (0, 0, 0, j))
+    half = pl.BlockSpec((span // 2, 2, eighth, part), lambda j: (0, 0, 0, j))
     return pl.pallas_call(
         kernel,
         grid=(columns // part,),
-        in_specs=[
-            pl.BlockSpec((span, 2, eighth, part), lambda j: (0, 0, 0, j)),
-            got,
-            got,
-            more,
-            more,
-        ],
-        out_specs=[out] * span,
-        out_shape=[jax.ShapeDtypeStruct((2, eighth, columns), BF16)] * span,
+        in_specs=[whole, got, got, more, more],
+        out_specs=[half, half],
+        out_shape=[jax.ShapeDtypeStruct((span // 2, *own.shape[1:]), BF16)] * 2,
         compiler_params=pltpu.CompilerParams(vmem_limit_bytes=VMEM_LIMIT),
         cost_estimate=LIGHT,
     )(own, got_a, got_b, more_a, more_b)
@@ -391,6 +417,17 @@
     )(*operands)
 
 
+def in_order(blocks, place):
+    span = place.span
+
+    def body(scalars, ins, out):
+        for k in range(span):
+            yield ins[k], out.at[lax.rem(scalars[0] + (span - k), span)]
+
+    shape = jax.ShapeDtypeStruct((span, *blocks[0].shape), blocks[0].dtype)
+    return copy_call(body, shape, span, list(blocks), place)
+
+
 def spread(blocks, place):
     span = place.span
     out = []
@@ -402,11 +439,6 @@
     return out
 
 
-def swap_once(x):
-    other = yield swap(x, "core")
-    return other
-
-
 def row_to_chip(x, place):
     rows, tokens, width = x.shape
     half = width // 2
@@ -414,7 +446,7 @@
     theirs = lax.dynamic_slice_in_dim(x, (1 - place.c) * half, half, 2)
     theirs = yield swap(theirs, "core")
     blocks = yield spread(by_core(place, mine, theirs, 0), place)
-    own = from_relative(blocks, place).reshape(place.span * tokens, half)
+    own = in_order(blocks, place).reshape(place.span * tokens, half)
     other = yield swap(own, "core")
     return by_core(place, own, other, 1)
 
@@ -426,7 +458,7 @@
     half = width // 2
     mine = lax.dynamic_slice_in_dim(y, place.c * half, half, 1)
     blocks = yield spread(mine.reshape(span, tokens, half), place)
-    stacked = from_relative(blocks, place)
+    stacked = in_order(blocks, place)
     own = lax.dynamic_slice_in_dim(stacked, place.c * rows, rows, 0)
     theirs = lax.dynamic_slice_in_dim(stacked, (1 - place.c) * rows, rows, 0)
     other = yield swap(theirs, "core")
@@ -455,7 +487,7 @@
         return extra
 
 
-def gather_weight(half, by_call, wait, place):
+def gather_weight(half, cuts, by_call, wait, place):
     span = place.span
     eighth, columns = half.shape[0] // 8, half.shape[1]
     mine = lax.dynamic_index_in_dim(
@@ -471,22 +503,24 @@
     near = other_shards(arrived, place) if by_call else jnp.stack(arrived, 1)
     near_x, near_y = yield [swap(near, "xbit"), swap(near, "ybit")]
     far_a, far_b = yield [swap(near_x[0], "ybit"), swap(near_y[1], "xbit")]
-    return assemble(half, near, near_x, near_y, far_a, far_b, place)
-
-
-def reduce_weight(left, right, place, last=False):
-    span = place.span
-    own, pass_a, pass_b, send_a, send_b = yield weight_gradient(left, right, place)
+    return assemble(half, cuts, near, near_x, near_y, far_a, far_b, place)
+
+
+def reduce_weight(lefts, right, place, last=False):
+    own, pass_a, pass_b, send_a, send_b = yield weight_gradient(lefts, right, place)
     got_a, got_b = yield [swap(send_a, "xbit"), swap(send_b, "ybit")]
     onward_a = (pass_a.astype(F32) + got_a[1].astype(F32)).astype(BF16)
     onward_b = (pass_b.astype(F32) + got_b[1].astype(F32)).astype(BF16)
     more_a, more_b = yield [swap(onward_a, "ybit"), swap(onward_b, "xbit")]
-    total = combine(own, got_a, got_b, more_a, more_b)
-    arrived = yield [spin(total[k], k, span) for k in range(1, span)]
-    summed = total[0].astype(F32)
-    for other in arrived:
-        summed = summed + other.astype(F32)
-    summed = summed.astype(BF16)
+    keep, send = combine(own, got_a, got_b, more_a, more_b)
+    step = place.span // 2
+    while step > 1:
+        other = yield across(send, step, place.span)
+        step //= 2
+        send = (keep[step:].astype(F32) + other[step:].astype(F32)).astype(BF16)
+        keep = keep[:step].astype(F32) + other[:step].astype(F32)
+    other = yield across(send, step, place.span)
+    summed = (keep[0].astype(F32) + other[0].astype(F32)).astype(BF16)
     if lax.axis_size("outer") > 1:
         summed = lax.psum(summed, "outer")
     _, eighth, columns = summed.shape
@@ -619,6 +653,7 @@
         attend_kernel(1.0 / math.sqrt(head), head, *refs)
 
     low = jax.ShapeDtypeStruct((length, width), BF16)
+    saved = pltpu.HBM((length, width), BF16)
     return pl.pallas_call(
         kernel,
         grid=(count,),
@@ -630,15 +665,15 @@
         ],
         out_specs=[wide, wide, wide, wide, lse],
         out_shape=[
+            saved,
+            saved,
+            saved,
             low,
-            low,
-            low,
-            low,
-            jax.ShapeDtypeStruct((width // head, length, 1), F32),
+            pltpu.HBM((width // head, length, 1), F32),
         ],
         scratch_shapes=[pltpu.VMEM((length, length), F32)],
         compiler_params=pltpu.CompilerParams(vmem_limit_bytes=VMEM_LIMIT),
-        cost_estimate=LIGHT,
+        cost_estimate=FILLER,
     )(projected, projected, projected, *fixed)
 
 
@@ -684,22 +719,8 @@
     return centred * inverse, inverse
 
 
-def interleave(first, second, span):
-    a, b = first.shape[1] // span, second.shape[1] // span
-    parts = []
-    for k in range(span):
-        parts += [first[:, k * a : (k + 1) * a], second[:, k * b : (k + 1) * b]]
-    return jnp.concatenate(parts, 1)
-
-
-def separate(both, a, b, span):
-    parts = [both[:, k * (a + b) : (k + 1) * (a + b)] for k in range(span)]
-    first = jnp.concatenate([p[:, :a] for p in parts], 1)
-    return first, jnp.concatenate([p[:, a:] for p in parts], 1)
-
-
-def forward_layer(x, weights, small, fixed, head, span):
-    w_qkv, w_up, w_last = weights
+def forward_layer(x, weights, small, fixed, head):
+    w_qkv, w_up, w_out, w_down = weights
     gains, shifts, b_qkv, b_out, b_up, b_down = small
     xhat, inverse = normalise(x)
     attn_low = (xhat * gains[0] + shifts[0]).astype(BF16)
@@ -709,40 +730,38 @@
     hidden_pre = dot(mlp_low, w_up) + b_up
     cdf = 0.5 * (1.0 + lax.erf(hidden_pre * ROOT_HALF))
     hidden_low = (hidden_pre * cdf).astype(BF16)
-    last_low = interleave(mixed_low, hidden_low, span)
-    part = dot(last_low, w_last).astype(BF16)
+    part = (dot(mixed_low, w_out) + dot(hidden_low, w_down)).astype(BF16)
     other = swap(part, "core")
     y = x + (part.astype(F32) + other.astype(F32) + b_out + b_down)
     attention = (query, keys, values, lse)
-    return y, (xhat, inverse, attn_low, mlp_low, attention, hidden_pre, last_low)
-
-
-def backward_layer(dy, weights, small, saved, fixed, head, place, slots, done, last):
-    w_qkv, w_up, w_last = weights
+    return y, (xhat, inverse, attn_low, mlp_low, attention, hidden_pre, mixed_low, hidden_low)
+
+
+def backward_layer(dy, weights, small, saved, fixed, head, place, slots, done, last, mover):
+    w_qkv, w_up, w_out, w_down = weights
     gains = small[0]
-    xhat, inverse, attn_low, mlp_low, attention, hidden_pre, last_low = saved
+    xhat, inverse, attn_low, mlp_low, attention, hidden_pre, mixed_low, hidden_low = saved
     query, keys, values, lse = attention
-    span = place.span
     dy_low = dy.astype(BF16)
-    slots.add(reduce_weight(last_low, dy_low, place), done(2))
+    slots.add(reduce_weight([mixed_low, hidden_low], dy_low, place), done(2))
     d_branch_b = jnp.sum(dy_low.astype(F32), 0)
 
     dy_low = slots.step(dy_low)
-    d_mixed, d_hidden = separate(
-        dot_t(dy_low, w_last), query.shape[1] // span, hidden_pre.shape[1] // span, span
-    )
-    d_mixed = d_mixed.astype(BF16)
+    d_hidden = dot_t(dy_low, w_down)
+    d_mixed = dot_t(dy_low, w_out).astype(BF16)
     cdf = 0.5 * (1.0 + lax.erf(hidden_pre * ROOT_HALF))
     density = jnp.exp(-0.5 * hidden_pre * hidden_pre) * (1.0 / math.sqrt(2.0 * math.pi))
     d_pre = (d_hidden * (cdf + hidden_pre * density)).astype(BF16)
-    slots.add(reduce_weight(mlp_low, d_pre, place), done(1))
+    slots.add(reduce_weight([mlp_low], d_pre, place), done(1))
     d_up_b = jnp.sum(d_pre.astype(F32), 0)
 
     d_mixed, d_pre = slots.step((d_mixed, d_pre))
+    if mover is not None:
+        slots.add(*mover)
     d_qkv = jnp.concatenate(
         attend_back(query, keys, values, d_mixed, lse, fixed, head), 1
     )
-    slots.add(reduce_weight(attn_low, d_qkv, place, last), done(0))
+    slots.add(reduce_weight([attn_low], d_qkv, place, last), done(0))
     d_mlp = dot_t(d_pre, w_up)
 
     d_qkv, d_mlp = slots.step((d_qkv, d_mlp))
@@ -836,36 +855,50 @@
 
         return done
 
-    def unit(index, arrays, wait):
+    def unit(name, arrays, wait):
         qkv, up, out, down = arrays
-        layer, kind = divmod(index, 3)
-        if kind == 0:
-            half = pick_columns(qkv, layer, head_cols, place)
-        elif kind == 1:
-            half = pick_columns(up, layer, ff_cols, place)
+        kind, layer = name
+        if kind == "last":
+            half = pick_rows((out, down), layer, place)
+            split = out.shape[1] // 2
+            cuts = [(0, split, 0, width), (split, half.shape[0], 0, width)]
         else:
-            half = pick_rows((out, down), layer, place)
-        slots.add(gather_weight(half, kind != 0, wait, place), keep(index))
+            parts = []
+            if kind != "up":
+                parts.append(pick_columns(qkv, layer, head_cols, place))
+            if kind != "qkv":
+                parts.append(pick_columns(up, layer, ff_cols, place))
+            half = jnp.concatenate(parts, 1) if len(parts) > 1 else parts[0]
+            cuts, start = [], 0
+            for part in parts:
+                cuts.append((0, part.shape[0], start, start + part.shape[1]))
+                start += part.shape[1]
+        slots.add(gather_weight(half, cuts, kind != "qkv", wait, place), keep(name))
 
     slots = Slots()
     arrays = (qkv_weight, up_weight, out_weight, down_weight)
     vectors = (norm_gains, norm_biases, qkv_bias, out_bias, up_bias, down_bias)
-    unit(0, arrays, False)
+    units = [("qkv", 0), ("up", 0), ("last", 0)]
+    for layer in range(1, LAYERS):
+        units += [("both", layer), ("last", layer)]
+    unit(units[0], arrays, False)
     slots.add(row_to_chip(hidden_in, place), keep("rows"))
-    slots.add(swap_once(segments), keep("segments"))
+    seg_other = swap(segments, "core")
     arrays, vectors, out_grad = slots.step((arrays, vectors, out_grad))
     slots.add(gather_small(vectors, place), keep("vectors"))
-    for index in range(1, 3 * LAYERS):
-        unit(index, arrays, True)
+    for name in units[1:]:
+        unit(name, arrays, True)
         arrays, out_grad = slots.step((arrays, out_grad))
-        if index == 3:
-            slots.add(row_to_chip(out_grad, place), keep("grads"))
+    slots.add(row_to_chip(out_grad, place), keep("grads"))
     while slots.parts:
         slots.step()
-    weights = [[found[3 * layer + i] for i in range(3)] for layer in range(LAYERS)]
+    weights = [
+        (*found["qkv", 0], *found["up", 0], *found["last", 0]),
+        *((*found["both", i], *found["last", i]) for i in range(1, LAYERS)),
+    ]
 
     stream, dy = found["rows"].astype(F32), found["grads"].astype(F32)
-    seg_all = by_core(place, segments, found["segments"], 0)
+    seg_all = by_core(place, segments, seg_other, 0)
     seg = lax.dynamic_index_in_dim(seg_all, place.z, 0, keepdims=False)
     seg_col, seg_row = seg[:, None], seg[None, :]
     length = seg.shape[0]
@@ -883,7 +916,7 @@
     kept = []
     for layer in range(LAYERS):
         stream, saved = forward_layer(
-            stream, weights[layer], smalls[layer], fixed, head, span
+            stream, weights[layer], smalls[layer], fixed, head
         )
         kept.append(saved)
 
@@ -907,8 +940,9 @@
 
     out_low = stream.astype(BF16)
     for layer in reversed(range(LAYERS)):
-        if layer == LAYERS - 2:
-            slots.add(chip_to_rows(out_low, rows, place), keep("block_out"))
+        mover = None
+        if layer == 0:
+            mover = (chip_to_rows(out_low, rows, place), keep("block_out"))
         dy, little[layer] = backward_layer(
             dy,
             weights[layer],
@@ -920,6 +954,7 @@
             slots,
             done_for(layer),
             layer == 0,
+            mover,
         )
     slots.add(chip_to_rows(dy.astype(BF16), rows, place), keep("in_grad"))
     slots.add(reduce_small(little, head_cols, ff_cols, place), keep("sums"))

time: 751 us -> 734 us (0.977)
  local copies, waits for them, and re-layouts: 121 us -> 87.7 us
  waiting for transfers between devices: 190 us -> 221 us
  starting transfers between devices: 117 us -> 96.2 us
  matrix products: 64.5 us -> 72.4 us
    ppermute x42 -> x21, waiting for transfers between devices: 99.4 us -> 25.1 us  [spin(): return lax.ppermute(x, 'shard', [(j, (j + k) % span) for j in range(span)])]
    ppermute x0 -> x12, waiting for transfers between devices: none -> 47.6 us  [across(): return lax.ppermute(x, 'shard', [(j, j ^ step) for j in range(span)])]
    ppermute x67 -> x63, waiting for transfers between devices: 75.1 us -> 116 us  [swap(): return lax.ppermute(x, axis, [(0, 1), (1, 0)])]
    unnamed x462 -> x396, local copies, waits for them, and re-layouts: 76.1 us -> 43.9 us
    ppermute x42 -> x21, starting transfers between devices: 55.7 us -> 27.9 us  [spin(): return lax.ppermute(x, 'shard', [(j, (j + k) % span) for j in range(span)])]
    ppermute x0 -> x12, starting transfers between devices: none -> 14.2 us  [across(): return lax.ppermute(x, 'shard', [(j, j ^ step) for j in range(span)])]
    pallas_call x6 -> x5, Pallas kernels: 37.3 us -> 28.4 us  [assemble(): pl.pallas_call(kernel, grid_spec=pltpu.PrefetchScalarGridSpec(num_scalar_...]
    all_gather x5, waiting for transfers between devices: 12.8 us -> 21.2 us  [reduce_weight(): parts = (yield lax.all_gather(summed, ('ybit', 'xbit', 'core')))]
  transfers between devices with their start and end apart: 118 -> 105, of which waited for: 39 -> 32; matrix products, arithmetic and copies ran while one was open for 24% -> 24% of each run, Pallas kernels for 21% -> 20%
where the time goes in v5:
time: 734 us; the launch traced here: 723 us
  waiting for transfers between devices  221 us (30%)
  Pallas kernels  155 us (21%)
  starting transfers between devices  96.2 us (13%)
  local copies, waits for them, and re-layouts  87.7 us (12%)
  other arithmetic  74.6 us (10%)
  matrix products  72.4 us (10%)
  between operations  16.4 us (2%)
    ppermute x63, waiting for transfers between devices, swap(): return lax.ppermute(x, axis, [(0, 1), (1, 0)])  116 us
    ppermute x63, starting transfers between devices, swap(): return lax.ppermute(x, axis, [(0, 1), (1, 0)])  53.5 us
    ppermute x12, waiting for transfers between devices, across(): return lax.ppermute(x, 'shard', [(j, j ^ step) for j in range(span)])  47.6 us
    unnamed x396, local copies, waits for them, and re-layouts  43.9 us
    dot_general x8, matrix products, dot_t(): lax.dot_general(a, b, (((1,), (1,)), ((), ())), preferred_element_type=F32)  37.5 us
    dot_general x8, matrix products, dot(): return jnp.dot(a, b, preferred_element_type=F32)  34.9 us
    pallas_call x6, Pallas kernels, weight_gradient(): pl.pallas_call(kernel, grid_spec=pltpu.PrefetchScalarGridSpec(num_scalar_...  30.8 us
    pallas_call x5, Pallas kernels, assemble(): pl.pallas_call(kernel, grid_spec=pltpu.PrefetchScalarGridSpec(num_scalar_...  28.4 us
  transfers between devices with their start and end apart: 105, of which 32 were waited for; matrix products, arithmetic and copies ran while one was open for 24% of the time, Pallas kernels for 20%

profile of v5, /device:TPU:0, one launch (start us, length us, event | category | flops | bytes accessed | tf_op | source)
XLA Modules:
  0.0 722.7 jit_solution(7807036300535784415)
XLA Ops:
  24.1 9.8 %collective-permute-done.1 = bf16[2,32,1536]{2,1,0:T(8,128)(2,1)S(1)} collective-permute-done((bf16[2,32,1536]{2,1,0:T(8,128)(2,1)}, bf16[2,32,1536]{2,1,0:T(8,128)(2,1)S(1)}, u32[]{:S(2)}, u32[]{:S(2)}) %collective-permute-start.1) | collective-permute-done | bytes 196640 | tf_op jit(solution)/shard_map/ppermute | solution.py:31
  133.1 16.5 %collective-permute-done.19.b_ref = bf16[3,32,2048]{2,1,0:T(8,128)(2,1)S(1)} collective-permute-done((bf16[3,32,2048]{2,1,0:T(8,128)(2,1)}, bf16[3,32,2048]{2,1,0:T(8,128)(2,1)S(1)}, u32[]{:S(2)}, u32[]{:S(2)}) %collective-permute-start.19) | collective-permute-done | bytes 393248 | tf_op jit(solution)/shard_map/ppermute | solution.py:27
  165.7 10.2 %shard_map.224 = (bf16[512,512]{1,0:T(8,128)(2,1)}, bf16[512,512]{1,0:T(8,128)(2,1)}, bf16[512,512]{1,0:T(8,128)(2,1)}, bf16[512,512]{1,0:T(8,128)(2,1)S(1)}, f32[8,512,1]{2,1,0:T(8,128)}) custom-call(f32[512,1536]{1,0:T(8,128)S(1)} %copy-done.123, f32[512,1536]{1,0:T(8,128)S(1)} %copy-done.123, f32[512,1536]{1,0:T(8,128)S(1)} %copy-done.123, ...), custom_call_target="tpu_custom_call" | custom-call | flops 8000000000 | bytes 1024 | tf_op jit(solution)/shard_map/pallas_call | solution.py:657
  186.6 6.8 multiply_convert_fusion.1
  193.4 10.2 %collective-permute-done.23.b_ref = bf16[3,80,1024]{2,1,0:T(8,128)(2,1)} collective-permute-done((bf16[3,80,1024]{2,1,0:T(8,128)(2,1)}, bf16[3,80,1024]{2,1,0:T(8,128)(2,1)}, u32[]{:S(2)}, u32[]{:S(2)}) %collective-permute-start.23) | collective-permute-done | bytes 491552 | tf_op jit(solution)/shard_map/ppermute | solution.py:27
  233.6 10.7 %collective-permute-done.29.b_ref = bf16[3,32,3584]{2,1,0:T(8,128)(2,1)} collective-permute-done((bf16[3,32,3584]{2,1,0:T(8,128)(2,1)}, bf16[3,32,3584]{2,1,0:T(8,128)(2,1)}, u32[]{:S(2)}, u32[]{:S(2)}) %collective-permute-start.29) | collective-permute-done | bytes 688160 | tf_op jit(solution)/shard_map/ppermute | solution.py:27
  254.2 7.4 %shard_map.235 = (bf16[4,256,1536]{2,1,0:T(8,128)(2,1)}, bf16[4,256,2048]{2,1,0:T(8,128)(2,1)}) custom-call(s32[3]{0:T(128)S(1)} %pad_add_fusion.scalars, bf16[4,2,32,3584]{3,2,1,0:T(8,128)(2,1)} %bitcast.289, bf16[2,3,32,3584]{3,2,1,0:T(8,128)(2,1)S(1)} %shard_map.230.n_ref, bf16[2,3,32,3584]{3,2,1,0:T(8,128)(2,1)} %collective-permute-done.24.x_ref, ...), custom_call_target="tpu_custom_call" | custom-call | flops 1024 | bytes 1024 | tf_op jit(solution)/shard_map/pallas_call | solution.py:210
  268.6 10.3 %shard_map.236 = (bf16[512,512]{1,0:T(8,128)(2,1)}, bf16[512,512]{1,0:T(8,128)(2,1)}, bf16[512,512]{1,0:T(8,128)(2,1)}, bf16[512,512]{1,0:T(8,128)(2,1)S(1)}, f32[8,512,1]{2,1,0:T(8,128)}) custom-call(f32[512,1536]{1,0:T(8,128)S(1)} %convolution_add_fusion.refs_0_.refs_1_.refs_2_, f32[512,1536]{1,0:T(8,128)S(1)} %convolution_add_fusion.refs_0_.refs_1_.refs_2_, ...), custom_call_target="tpu_custom_call" | custom-call | flops 8000000000 | bytes 1024 | tf_op jit(solution)/shard_map/pallas_call | solution.py:657
  278.9 6.7 multiply_convert_fusion
  301.6 7.0 convert_reduce_fusion
  315.3 9.9 %collective-permute-done.38.ga_ref = bf16[2,4,80,1024]{3,2,1,0:T(8,128)(2,1)S(1)} collective-permute-done((bf16[2,4,80,1024]{3,2,1,0:T(8,128)(2,1)}, bf16[2,4,80,1024]{3,2,1,0:T(8,128)(2,1)S(1)}, u32[]{:S(2)}, u32[]{:S(2)}) %collective-permute-start.38) | collective-permute-done | bytes 1310752 | tf_op jit(solution)/shard_map/ppermute | solution.py:27
  332.2 11.7 %shard_map.241 = (bf16[512,512]{1,0:T(8,128)(2,1)S(1)}, bf16[512,512]{1,0:T(8,128)(2,1)S(1)}, bf16[512,512]{1,0:T(8,128)(2,1)S(1)}) custom-call(bf16[512,512]{1,0:T(8,128)(2,1)S(1)} %copy-done.81, bf16[512,512]{1,0:T(8,128)(2,1)S(1)} %copy-done.82, bf16[512,512]{1,0:T(8,128)(2,1)S(1)} %copy-done.83, bf16[512,512]{1,0:T(8,128)(2,1)S(1)} %copy-done.84, ...), custom_call_target="tpu_custom_call" | custom-call | flops 1024 | bytes 1024 | tf_op jit(solution)/shard_map/pallas_call | solution.py:688
  355.4 12.0 %collective-permute-done.40.ma_ref = bf16[4,80,1024]{2,1,0:T(8,128)(2,1)S(1)} collective-permute-done((bf16[4,80,1024]{2,1,0:T(8,128)(2,1)}, bf16[4,80,1024]{2,1,0:T(8,128)(2,1)S(1)}, u32[]{:S(2)}, u32[]{:S(2)}) %collective-permute-start.40) | collective-permute-done | bytes 655392 | tf_op jit(solution)/shard_map/ppermute | solution.py:27
  399.6 12.8 %collective-permute-done.44 = bf16[2,2,80,1024]{3,2,1,0:T(8,128)(2,1)S(1)} collective-permute-done((bf16[2,2,80,1024]{3,2,1,0:T(8,128)(2,1)S(1)}, bf16[2,2,80,1024]{3,2,1,0:T(8,128)(2,1)S(1)}, u32[]{:S(2)}, u32[]{:S(2)}) %collective-permute-start.44) | collective-permute-done | bytes 655392 | tf_op jit(solution)/shard_map/ppermute | solution.py:35
  423.0 7.5 %convert_reduce_fusion.1 = (f32[2048]{0:T(1024)}, bf16[512,2048]{1,0:T(8,128)(2,1)S(1)}) fusion(f32[512,2048]{1,0:T(8,128)} %get-tuple-element.648, f32[2048]{0:T(1024)S(1)} %bitcast.342, bf16[512,1024]{1,0:T(8,128)(2,1)S(1)} %get-tuple-element.410.refs_2_, bf16[2048,1024]{1,0:T(8,128)(2,1)} %bitcast.359), kind=kOutput, calls=%fused_computation.15 | convolution fusion | flops 2161113088 | bytes 11550720 | tf_op jit(solution)/shard_map/dot_general | solution.py:43
  437.9 16.3 %collective-permute-done.52.ma_ref = bf16[4,32,1536]{2,1,0:T(8,128)(2,1)} collective-permute-done((bf16[4,32,1536]{2,1,0:T(8,128)(2,1)}, bf16[4,32,1536]{2,1,0:T(8,128)(2,1)}, u32[]{:S(2)}, u32[]{:S(2)}) %collective-permute-start.52) | collective-permute-done | bytes 393248 | tf_op jit(solution)/shard_map/ppermute | solution.py:27
  482.6 11.7 %shard_map.248 = (bf16[512,512]{1,0:T(8,128)(2,1)S(1)}, bf16[512,512]{1,0:T(8,128)(2,1)S(1)}, bf16[512,512]{1,0:T(8,128)(2,1)S(1)}) custom-call(bf16[512,512]{1,0:T(8,128)(2,1)S(1)} %copy-done.77, bf16[512,512]{1,0:T(8,128)(2,1)S(1)} %copy-done.78, bf16[512,512]{1,0:T(8,128)(2,1)S(1)} %copy-done.79, bf16[512,512]{1,0:T(8,128)(2,1)S(1)} %copy-done.80, ...), custom_call_target="tpu_custom_call" | custom-call | flops 1024 | bytes 1024 | tf_op jit(solution)/shard_map/pallas_call | solution.py:688
  515.4 9.5 %collective-permute-done.57 = bf16[2,2,32,1536]{3,2,1,0:T(8,128)(2,1)S(1)} collective-permute-done((bf16[2,2,32,1536]{3,2,1,0:T(8,128)(2,1)S(1)}, bf16[2,2,32,1536]{3,2,1,0:T(8,128)(2,1)S(1)}, u32[]{:S(2)}, u32[]{:S(2)}) %collective-permute-start.57) | collective-permute-done | bytes 393248 | tf_op jit(solution)/shard_map/ppermute | solution.py:35
  560.1 24.2 %collective-permute-done.69.mb_ref = bf16[4,32,2048]{2,1,0:T(8,128)(2,1)S(1)} collective-permute-done((bf16[4,32,2048]{2,1,0:T(8,128)(2,1)S(1)}, bf16[4,32,2048]{2,1,0:T(8,128)(2,1)S(1)}, u32[]{:S(2)}, u32[]{:S(2)}) %collective-permute-start.69) | collective-permute-done | bytes 524320 | tf_op jit(solution)/shard_map/ppermute | solution.py:27
  590.3 7.3 %collective-permute-done.75.refs_2_ = bf16[128,512]{1,0:T(8,128)(2,1)S(1)} collective-permute-done((bf16[128,512]{1,0:T(8,128)(2,1)S(1)}, bf16[128,512]{1,0:T(8,128)(2,1)S(1)}, u32[]{:S(2)}, u32[]{:S(2)}) %collective-permute-start.75) | collective-permute-done | bytes 131104 | tf_op jit(solution)/shard_map/ppermute | solution.py:31
  615.5 12.6 %collective-permute-done.78 = bf16[1,2,80,1024]{3,2,1,0:T(8,128)(2,1)S(1)} collective-permute-done((bf16[1,2,80,1024]{3,2,1,0:T(8,128)(2,1)S(1)}, bf16[1,2,80,1024]{3,2,1,0:T(8,128)(2,1)S(1)}, u32[]{:S(2)}, u32[]{:S(2)}) %collective-permute-start.78) | collective-permute-done | bytes 327712 | tf_op jit(solution)/shard_map/ppermute | solution.py:35
  646.9 8.8 %collective-permute-done.84 = bf16[1,2,32,2048]{3,2,1,0:T(8,128)(2,1)S(1)} collective-permute-done((bf16[1,2,32,2048]{3,2,1,0:T(8,128)(2,1)S(1)}, bf16[1,2,32,2048]{3,2,1,0:T(8,128)(2,1)S(1)}, u32[]{:S(2)}, u32[]{:S(2)}) %collective-permute-start.84) | collective-permute-done | bytes 262176 | tf_op jit(solution)/shard_map/ppermute | solution.py:35
  655.7 8.3 %all-gather.24.cloned.1.call-done = bf16[8,2,80,1024]{3,2,1,0:T(8,128)(2,1)} async-done(((bf16[1,2,80,1024]{3,2,1,0:T(8,128)(2,1)}), bf16[8,2,80,1024]{3,2,1,0:T(8,128)(2,1)}) %all-gather.24.cloned.1.call-update) | async-done | bytes 2621456 | tf_op jit(solution)/shard_map/all_gather | solution.py:534
  681.0 12.8 %all-gather.26.cloned.1.call-done = bf16[8,2,32,2048]{3,2,1,0:T(8,128)(2,1)} async-done(((bf16[1,2,32,2048]{3,2,1,0:T(8,128)(2,1)}), bf16[8,2,32,2048]{3,2,1,0:T(8,128)(2,1)}) %all-gather.26.cloned.1.call-update) | async-done | bytes 2097168 | tf_op jit(solution)/shard_map/all_gather | solution.py:534
  (816 shorter events, 445.4 us)
Async XLA Ops:
  7.2 73.9 %all-gather.10.cloned.1.call-start = ((), (), s32[]{:S(2)}) async-start(), calls=%async_computation | async-start | bytes 1310720 | tf_op jit(solution)/shard_map/all_gather | solution.py:497
  52.4 61.5 %all-gather.12.cloned.1.call-start = ((), (), s32[]{:S(2)}) async-start(), calls=%async_computation.1 | async-start | bytes 1638400 | tf_op jit(solution)/shard_map/all_gather | solution.py:497
  71.7 84.2 %all-gather.14.cloned.1.call-start = ((), (), s32[]{:S(2)}) async-start(), calls=%async_computation.2 | async-start | bytes 2293760 | tf_op jit(solution)/shard_map/all_gather | solution.py:497
  86.4 107.0 %all-gather.16.cloned.1.call-start = ((), (), s32[]{:S(2)}) async-start(), calls=%async_computation.3 | async-start | bytes 1638400 | tf_op jit(solution)/shard_map/all_gather | solution.py:497
  132.8 392.9 %all-gather.18.cloned.1.call-start = ((), (), s32[]{:S(2)}) async-start(), calls=%async_computation.4 | async-start | bytes 2949120 | tf_op jit(solution)/shard_map/all_gather | solution.py:534
  159.8 43.8 %collective-permute-start.25 = (bf16[2,3,32,3584]{3,2,1,0:T(8,128)(2,1)S(1)}, bf16[2,3,32,3584]{3,2,1,0:T(8,128)(2,1)}, u32[]{:S(2)}, u32[]{:S(2)}) collective-permute-start(bf16[2,3,32,3584]{3,2,1,0:T(8,128)(2,1)S(1)} %shard_map.230.n_ref), channel_id=1, source_target_pairs={{0,16},{16,0},{1,17},{17,1},{2,18},{18,2},{3,19},{19,3},{4,20},{20... | collective-permute-start | bytes 4128776 | tf_op jit(solution)/shard_map/ppermute | solution.py:27
  161.3 42.3 %collective-permute-start.24 = (bf16[2,3,32,3584]{3,2,1,0:T(8,128)(2,1)S(1)}, bf16[2,3,32,3584]{3,2,1,0:T(8,128)(2,1)}, u32[]{:S(2)}, u32[]{:S(2)}) collective-permute-start(bf16[2,3,32,3584]{3,2,1,0:T(8,128)(2,1)S(1)} %shard_map.230.n_ref), channel_id=1, source_target_pairs={{0,8},{8,0},{1,9},{9,1},{2,10},{10,2},{3,11},{11,3},{4,12},{12,4},... | collective-permute-start | bytes 4128776 | tf_op jit(solution)/shard_map/ppermute | solution.py:27
  206.8 37.5 %collective-permute-start.31 = (bf16[2,3,80,1024]{3,2,1,0:T(8,128)(2,1)S(1)}, bf16[2,3,80,1024]{3,2,1,0:T(8,128)(2,1)}, u32[]{:S(2)}, u32[]{:S(2)}) collective-permute-start(bf16[2,3,80,1024]{3,2,1,0:T(8,128)(2,1)S(1)} %shard_map.234.n_ref), channel_id=1, source_target_pairs={{0,16},{16,0},{1,17},{17,1},{2,18},{18,2},{3,19},{19,3},{4,20},{20... | collective-permute-start | bytes 2949128 | tf_op jit(solution)/shard_map/ppermute | solution.py:27
  207.4 36.9 %collective-permute-start.30 = (bf16[2,3,80,1024]{3,2,1,0:T(8,128)(2,1)S(1)}, bf16[2,3,80,1024]{3,2,1,0:T(8,128)(2,1)}, u32[]{:S(2)}, u32[]{:S(2)}) collective-permute-start(bf16[2,3,80,1024]{3,2,1,0:T(8,128)(2,1)S(1)} %shard_map.234.n_ref), channel_id=1, source_target_pairs={{0,8},{8,0},{1,9},{9,1},{2,10},{10,2},{3,11},{11,3},{4,12},{12,4},... | collective-permute-start | bytes 2949128 | tf_op jit(solution)/shard_map/ppermute | solution.py:27
  246.2 39.3 %collective-permute-start.36 = (bf16[3,80,1024]{2,1,0:T(8,128)(2,1)}, bf16[3,80,1024]{2,1,0:T(8,128)(2,1)S(1)}, u32[]{:S(2)}, u32[]{:S(2)}) collective-permute-start(bf16[3,80,1024]{2,1,0:T(8,128)(2,1)} %slice_bitcast_fusion.2), channel_id=1, source_target_pairs={{0,8},{8,0},{1,9},{9,1},{2,10},{10,2},{3,11},{11,3},{4,12},{12,4},... | collective-permute-start | bytes 1474568 | tf_op jit(solution)/shard_map/ppermute | solution.py:27
  328.5 38.9 %collective-permute-start.42 = (bf16[2,4,32,2048]{3,2,1,0:T(8,128)(2,1)}, bf16[2,4,32,2048]{3,2,1,0:T(8,128)(2,1)S(1)}, u32[]{:S(2)}, u32[]{:S(2)}) collective-permute-start(bf16[2,4,32,2048]{3,2,1,0:T(8,128)(2,1)} %get-tuple-element.366), channel_id=1, source_target_pairs={{0,8},{8,0},{1,9},{9,1},{2,10},{10,2},{3,11},{11,3},{4,12},{12,4},... | collective-permute-start | bytes 3145736 | tf_op jit(solution)/shard_map/ppermute | solution.py:27
  329.0 38.3 %collective-permute-start.43 = (bf16[2,4,32,2048]{3,2,1,0:T(8,128)(2,1)}, bf16[2,4,32,2048]{3,2,1,0:T(8,128)(2,1)S(1)}, u32[]{:S(2)}, u32[]{:S(2)}) collective-permute-start(bf16[2,4,32,2048]{3,2,1,0:T(8,128)(2,1)} %get-tuple-element.367), channel_id=1, source_target_pairs={{0,16},{16,0},{1,17},{17,1},{2,18},{18,2},{3,19},{19,3},{4,20},{20... | collective-permute-start | bytes 3145736 | tf_op jit(solution)/shard_map/ppermute | solution.py:27
  330.7 36.6 %collective-permute-start.40 = (bf16[4,80,1024]{2,1,0:T(8,128)(2,1)}, bf16[4,80,1024]{2,1,0:T(8,128)(2,1)S(1)}, u32[]{:S(2)}, u32[]{:S(2)}) collective-permute-start(bf16[4,80,1024]{2,1,0:T(8,128)(2,1)} %fusion.19), channel_id=1, source_target_pairs={{0,16},{16,0},{1,17},{17,1},{2,18},{18,2},{3,19},{19,3},{4,20},{20... | collective-permute-start | bytes 1966088 | tf_op jit(solution)/shard_map/ppermute | solution.py:27
  414.4 39.8 %collective-permute-start.54 = (bf16[2,4,80,1024]{3,2,1,0:T(8,128)(2,1)}, bf16[2,4,80,1024]{3,2,1,0:T(8,128)(2,1)S(1)}, u32[]{:S(2)}, u32[]{:S(2)}) collective-permute-start(bf16[2,4,80,1024]{3,2,1,0:T(8,128)(2,1)} %get-tuple-element.408), channel_id=1, source_target_pairs={{0,8},{8,0},{1,9},{9,1},{2,10},{10,2},{3,11},{11,3},{4,12},{12,4},... | collective-permute-start | bytes 3932168 | tf_op jit(solution)/shard_map/ppermute | solution.py:27
  415.7 39.2 %collective-permute-start.55 = (bf16[2,4,80,1024]{3,2,1,0:T(8,128)(2,1)}, bf16[2,4,80,1024]{3,2,1,0:T(8,128)(2,1)}, u32[]{:S(2)}, u32[]{:S(2)}) collective-permute-start(bf16[2,4,80,1024]{3,2,1,0:T(8,128)(2,1)} %get-tuple-element.409), channel_id=1, source_target_pairs={{0,16},{16,0},{1,17},{17,1},{2,18},{18,2},{3,19},{19,3},{4,20},{20... | collective-permute-start | bytes 3932168 | tf_op jit(solution)/shard_map/ppermute | solution.py:27
  418.0 36.1 %collective-permute-start.52 = (bf16[4,32,1536]{2,1,0:T(8,128)(2,1)}, bf16[4,32,1536]{2,1,0:T(8,128)(2,1)}, u32[]{:S(2)}, u32[]{:S(2)}) collective-permute-start(bf16[4,32,1536]{2,1,0:T(8,128)(2,1)} %fusion.31), channel_id=1, source_target_pairs={{0,16},{16,0},{1,17},{17,1},{2,18},{18,2},{3,19},{19,3},{4,20},{20... | collective-permute-start | bytes 1179656 | tf_op jit(solution)/shard_map/ppermute | solution.py:27
  456.0 141.6 %all-gather.20.cloned.1.call-start = ((), (), s32[]{:S(2)}) async-start(), calls=%async_computation.5 | async-start | bytes 2359296 | tf_op jit(solution)/shard_map/all_gather | solution.py:534
  474.6 51.0 %collective-permute-start.60 = (bf16[2,4,32,2048]{3,2,1,0:T(8,128)(2,1)}, bf16[2,4,32,2048]{3,2,1,0:T(8,128)(2,1)}, u32[]{:S(2)}, u32[]{:S(2)}) collective-permute-start(bf16[2,4,32,2048]{3,2,1,0:T(8,128)(2,1)} %get-tuple-element.427), channel_id=1, source_target_pairs={{0,8},{8,0},{1,9},{9,1},{2,10},{10,2},{3,11},{11,3},{4,12},{12,4},... | collective-permute-start | bytes 3145736 | tf_op jit(solution)/shard_map/ppermute | solution.py:27
  475.8 49.9 %collective-permute-start.61 = (bf16[2,4,32,2048]{3,2,1,0:T(8,128)(2,1)}, bf16[2,4,32,2048]{3,2,1,0:T(8,128)(2,1)}, u32[]{:S(2)}, u32[]{:S(2)}) collective-permute-start(bf16[2,4,32,2048]{3,2,1,0:T(8,128)(2,1)} %get-tuple-element.428), channel_id=1, source_target_pairs={{0,16},{16,0},{1,17},{17,1},{2,18},{18,2},{3,19},{19,3},{4,20},{20... | collective-permute-start | bytes 3145736 | tf_op jit(solution)/shard_map/ppermute | solution.py:27
  527.5 105.7 %all-gather.22.cloned.1.call-start = ((), (), s32[]{:S(2)}) async-start(), calls=%async_computation.6 | async-start | bytes 1769472 | tf_op jit(solution)/shard_map/all_gather | solution.py:534
  548.4 37.8 %collective-permute-start.67 = (bf16[2,2,80,1024]{3,2,1,0:T(8,128)(2,1)S(1)}, bf16[2,2,80,1024]{3,2,1,0:T(8,128)(2,1)S(1)}, u32[]{:S(2)}, u32[]{:S(2)}) collective-permute-start(bf16[2,2,80,1024]{3,2,1,0:T(8,128)(2,1)S(1)} %get-tuple-element.453), channel_id=1, source_target_pairs={{0,2},{1,3},{2,0},{3,1},{4,6},{5,7},{6,4},{7,5},{8,10},{9,11},{10,... | collective-permute-start | bytes 1966088 | tf_op jit(solution)/shard_map/ppermute | solution.py:35
  553.4 36.9 %collective-permute-start.71 = (bf16[2,4,32,1536]{3,2,1,0:T(8,128)(2,1)}, bf16[2,4,32,1536]{3,2,1,0:T(8,128)(2,1)S(1)}, u32[]{:S(2)}, u32[]{:S(2)}) collective-permute-start(bf16[2,4,32,1536]{3,2,1,0:T(8,128)(2,1)} %get-tuple-element.458), channel_id=1, source_target_pairs={{0,8},{8,0},{1,9},{9,1},{2,10},{10,2},{3,11},{11,3},{4,12},{12,4},... | collective-permute-start | bytes 2359304 | tf_op jit(solution)/shard_map/ppermute | solution.py:27
  599.5 64.5 %all-gather.24.cloned.1.call-start = ((), (), s32[]{:S(2)}) async-start(), calls=%async_computation.7 | async-start | bytes 2949120 | tf_op jit(solution)/shard_map/all_gather | solution.py:534
  635.2 58.7 %all-gather.26.cloned.1.call-start = ((), (), s32[]{:S(2)}) async-start(), calls=%async_computation.8 | async-start | bytes 2359296 | tf_op jit(solution)/shard_map/all_gather | solution.py:534
  (270 other events, 3351.0 us)
Sparse Core Ops, SparseCore 0:
  52.5 26.9 all-gather.9
  81.6 32.2 all-gather.11
  115.4 40.3 all-gather.13
  157.3 31.5 all-gather.15
  456.1 34.5 all-gather.17
  527.6 26.6 all-gather.19
  599.6 26.2 all-gather.21
  635.3 28.6 all-gather.23
  665.9 27.8 all-gather.25

commit v6 on v5

--- a/solution.py
+++ b/solution.py
@@ -531,7 +531,10 @@
         other = yield swap(half, "core")
         parts = by_core(place, half[:, None], other[:, None], 1)
     else:
-        parts = yield lax.all_gather(summed, ("ybit", "xbit", "core"))
+        moving = lax.all_gather(summed, ("ybit", "xbit", "core"))
+        yield ()
+        yield ()
+        parts = yield moving
     return parts.reshape(4, 2, 2 * eighth, columns)
 
 

time: 734 us -> 732 us (level)
  waiting for transfers between devices: 221 us -> 189 us
  local copies, waits for them, and re-layouts: 87.7 us -> 116 us
    all_gather x5, waiting for transfers between devices: 21.2 us -> 4.89 us  [reduce_weight(): moving = lax.all_gather(summed, ('ybit', 'xbit', 'core'))]
    unnamed x396 -> x448, local copies, waits for them, and re-layouts: 43.9 us -> 59.3 us
    ppermute x63, waiting for transfers between devices: 116 us -> 101 us  [swap(): return lax.ppermute(x, axis, [(0, 1), (1, 0)])]
    all_gather x4, waiting for transfers between devices: 10.2 us -> 0.02 us  [gather_weight(): moving = lax.all_gather(mine, 'shard')]
    convert_element_type x7, local copies, waits for them, and re-layouts: 0.19 us -> 8.91 us  [gather_small(): out.append(part.reshape(*v.shape[:-1], -1).astype(F32))]
  transfers between devices with their start and end apart: 105 -> 105, of which waited for: 32 -> 30; matrix products, arithmetic and copies ran while one was open for 24% -> 28% of each run, Pallas kernels for 20% -> 20%
where the time goes in v6:
time: 732 us; the launch traced here: 720 us
  waiting for transfers between devices  189 us (26%)
  Pallas kernels  158 us (22%)
  local copies, waits for them, and re-layouts  116 us (16%)
  starting transfers between devices  98 us (13%)
  other arithmetic  76.3 us (10%)
  matrix products  66.5 us (9%)
  between operations  16.3 us (2%)
    ppermute x63, waiting for transfers between devices, swap(): return lax.ppermute(x, axis, [(0, 1), (1, 0)])  101 us
    unnamed x448, local copies, waits for them, and re-layouts  59.3 us
    ppermute x12, waiting for transfers between devices, across(): return lax.ppermute(x, 'shard', [(j, j ^ step) for j in range(span)])  54.7 us
    ppermute x63, starting transfers between devices, swap(): return lax.ppermute(x, axis, [(0, 1), (1, 0)])  54.3 us
    dot_general x8, matrix products, dot_t(): lax.dot_general(a, b, (((1,), (1,)), ((), ())), preferred_element_type=F32)  33.3 us
    dot_general x8, matrix products, dot(): return jnp.dot(a, b, preferred_element_type=F32)  33.2 us
    pallas_call x6, Pallas kernels, weight_gradient(): pl.pallas_call(kernel, grid_spec=pltpu.PrefetchScalarGridSpec(num_scalar_...  31.5 us
    pallas_call x5, Pallas kernels, assemble(): pl.pallas_call(kernel, grid_spec=pltpu.PrefetchScalarGridSpec(num_scalar_...  28.8 us
  transfers between devices with their start and end apart: 105, of which 30 were waited for; matrix products, arithmetic and copies ran while one was open for 28% of the time, Pallas kernels for 20%

profile of v6, /device:TPU:0, one launch (start us, length us, event | category | flops | bytes accessed | tf_op | source)
XLA Modules:
  0.0 719.5 jit_solution(11678389955273795743)
XLA Ops:
  23.4 9.6 %collective-permute-done.1 = bf16[2,32,1536]{2,1,0:T(8,128)(2,1)S(1)} collective-permute-done((bf16[2,32,1536]{2,1,0:T(8,128)(2,1)S(1)}, bf16[2,32,1536]{2,1,0:T(8,128)(2,1)S(1)}, u32[]{:S(2)}, u32[]{:S(2)}) %collective-permute-start.1) | collective-permute-done | bytes 196640 | tf_op jit(solution)/shard_map/ppermute | solution.py:31
  147.7 18.2 %collective-permute-done.19.b_ref = bf16[3,32,2048]{2,1,0:T(8,128)(2,1)} collective-permute-done((bf16[3,32,2048]{2,1,0:T(8,128)(2,1)}, bf16[3,32,2048]{2,1,0:T(8,128)(2,1)}, u32[]{:S(2)}, u32[]{:S(2)}) %collective-permute-start.19) | collective-permute-done | bytes 393248 | tf_op jit(solution)/shard_map/ppermute | solution.py:27
  173.7 10.3 %shard_map.224 = (bf16[512,512]{1,0:T(8,128)(2,1)}, bf16[512,512]{1,0:T(8,128)(2,1)}, bf16[512,512]{1,0:T(8,128)(2,1)}, bf16[512,512]{1,0:T(8,128)(2,1)S(1)}, f32[8,512,1]{2,1,0:T(8,128)}) custom-call(f32[512,1536]{1,0:T(8,128)S(1)} %copy-done.135, f32[512,1536]{1,0:T(8,128)S(1)} %copy-done.135, f32[512,1536]{1,0:T(8,128)S(1)} %copy-done.135, ...), custom_call_target="tpu_custom_call" | custom-call | flops 8000000000 | bytes 1024 | tf_op jit(solution)/shard_map/pallas_call | solution.py:660
  195.3 6.8 multiply_convert_fusion.1
  202.1 10.9 %collective-permute-done.23.b_ref = bf16[3,80,1024]{2,1,0:T(8,128)(2,1)} collective-permute-done((bf16[3,80,1024]{2,1,0:T(8,128)(2,1)}, bf16[3,80,1024]{2,1,0:T(8,128)(2,1)}, u32[]{:S(2)}, u32[]{:S(2)}) %collective-permute-start.23) | collective-permute-done | bytes 491552 | tf_op jit(solution)/shard_map/ppermute | solution.py:27
  226.9 6.1 shard_map.232
  246.6 6.6 collective-permute-done.29.b_ref
  261.6 7.3 %shard_map.235 = (bf16[4,256,1536]{2,1,0:T(8,128)(2,1)}, bf16[4,256,2048]{2,1,0:T(8,128)(2,1)}) custom-call(s32[3]{0:T(128)S(1)} %pad_add_fusion.scalars, bf16[4,2,32,3584]{3,2,1,0:T(8,128)(2,1)} %bitcast.289, bf16[2,3,32,3584]{3,2,1,0:T(8,128)(2,1)} %shard_map.230.n_ref, bf16[2,3,32,3584]{3,2,1,0:T(8,128)(2,1)S(1)} %collective-permute-done.24.x_ref, ...), custom_call_target="tpu_custom_call" | custom-call | flops 1024 | bytes 1024 | tf_op jit(solution)/shard_map/pallas_call | solution.py:210
  277.0 10.3 %shard_map.236 = (bf16[512,512]{1,0:T(8,128)(2,1)}, bf16[512,512]{1,0:T(8,128)(2,1)}, bf16[512,512]{1,0:T(8,128)(2,1)}, bf16[512,512]{1,0:T(8,128)(2,1)S(1)}, f32[8,512,1]{2,1,0:T(8,128)}) custom-call(f32[512,1536]{1,0:T(8,128)S(1)} %convolution_add_fusion.refs_0_.refs_1_.refs_2_, f32[512,1536]{1,0:T(8,128)S(1)} %convolution_add_fusion.refs_0_.refs_1_.refs_2_, ...), custom_call_target="tpu_custom_call" | custom-call | flops 8000000000 | bytes 1024 | tf_op jit(solution)/shard_map/pallas_call | solution.py:660
  287.3 6.8 multiply_convert_fusion
  326.7 7.2 %collective-permute-done.38.ga_ref = bf16[2,4,80,1024]{3,2,1,0:T(8,128)(2,1)} collective-permute-done((bf16[2,4,80,1024]{3,2,1,0:T(8,128)(2,1)}, bf16[2,4,80,1024]{3,2,1,0:T(8,128)(2,1)}, u32[]{:S(2)}, u32[]{:S(2)}) %collective-permute-start.38) | collective-permute-done | bytes 1310752 | tf_op jit(solution)/shard_map/ppermute | solution.py:27
  340.0 11.6 %shard_map.241 = (bf16[512,512]{1,0:T(8,128)(2,1)S(1)}, bf16[512,512]{1,0:T(8,128)(2,1)S(1)}, bf16[512,512]{1,0:T(8,128)(2,1)S(1)}) custom-call(bf16[512,512]{1,0:T(8,128)(2,1)S(1)} %copy-done.88, bf16[512,512]{1,0:T(8,128)(2,1)S(1)} %copy-done.89, bf16[512,512]{1,0:T(8,128)(2,1)S(1)} %copy-done.90, bf16[512,512]{1,0:T(8,128)(2,1)S(1)} %convolution_convert_fusion.1.refs_3_, ...), custom_call_target="tpu_custom_call" | custom-call | flops 1024 | bytes 1024 | tf_op jit(solution)/shard_map/pallas_call | solution.py:691
  353.2 6.0 fusion.52
  368.7 7.1 collective-permute-done.42.ga_ref
  403.4 6.0 shard_map.244
  409.4 12.8 %collective-permute-done.44 = bf16[2,2,80,1024]{3,2,1,0:T(8,128)(2,1)} collective-permute-done((bf16[2,2,80,1024]{3,2,1,0:T(8,128)(2,1)S(1)}, bf16[2,2,80,1024]{3,2,1,0:T(8,128)(2,1)}, u32[]{:S(2)}, u32[]{:S(2)}) %collective-permute-start.44) | collective-permute-done | bytes 655392 | tf_op jit(solution)/shard_map/ppermute | solution.py:35
  439.5 7.3 %convert_reduce_fusion.1 = (f32[2048]{0:T(1024)}, bf16[512,2048]{1,0:T(8,128)(2,1)S(1)}) fusion(f32[512,2048]{1,0:T(8,128)} %get-tuple-element.632, f32[2048]{0:T(1024)S(1)} %bitcast.342, bf16[512,1024]{1,0:T(8,128)(2,1)S(1)} %get-tuple-element.403.refs_2_, bf16[2048,1024]{1,0:T(8,128)(2,1)} %bitcast.359), kind=kOutput, calls=%fused_computation.15 | convolution fusion | flops 2161113088 | bytes 11550720 | tf_op jit(solution)/shard_map/dot_general | solution.py:43
  453.8 11.7 %collective-permute-done.52.ma_ref = bf16[4,32,1536]{2,1,0:T(8,128)(2,1)S(1)} collective-permute-done((bf16[4,32,1536]{2,1,0:T(8,128)(2,1)S(1)}, bf16[4,32,1536]{2,1,0:T(8,128)(2,1)S(1)}, u32[]{:S(2)}, u32[]{:S(2)}) %collective-permute-start.52) | collective-permute-done | bytes 393248 | tf_op jit(solution)/shard_map/ppermute | solution.py:27
  486.3 11.6 %shard_map.248 = (bf16[512,512]{1,0:T(8,128)(2,1)S(1)}, bf16[512,512]{1,0:T(8,128)(2,1)S(1)}, bf16[512,512]{1,0:T(8,128)(2,1)S(1)}) custom-call(bf16[512,512]{1,0:T(8,128)(2,1)S(1)} %copy-done.84, bf16[512,512]{1,0:T(8,128)(2,1)S(1)} %copy-done.85, bf16[512,512]{1,0:T(8,128)(2,1)S(1)} %copy-done.86, bf16[512,512]{1,0:T(8,128)(2,1)S(1)} %copy-done.87, ...), custom_call_target="tpu_custom_call" | custom-call | flops 1024 | bytes 1024 | tf_op jit(solution)/shard_map/pallas_call | solution.py:691
  518.5 9.3 %collective-permute-done.57 = bf16[2,2,32,1536]{3,2,1,0:T(8,128)(2,1)S(1)} collective-permute-done((bf16[2,2,32,1536]{3,2,1,0:T(8,128)(2,1)S(1)}, bf16[2,2,32,1536]{3,2,1,0:T(8,128)(2,1)S(1)}, u32[]{:S(2)}, u32[]{:S(2)}) %collective-permute-start.57) | collective-permute-done | bytes 393248 | tf_op jit(solution)/shard_map/ppermute | solution.py:35
  563.8 26.2 %collective-permute-done.69.mb_ref = bf16[4,32,2048]{2,1,0:T(8,128)(2,1)S(1)} collective-permute-done((bf16[4,32,2048]{2,1,0:T(8,128)(2,1)S(1)}, bf16[4,32,2048]{2,1,0:T(8,128)(2,1)S(1)}, u32[]{:S(2)}, u32[]{:S(2)}) %collective-permute-start.69) | collective-permute-done | bytes 524320 | tf_op jit(solution)/shard_map/ppermute | solution.py:27
  597.3 7.6 %collective-permute-done.75.refs_2_ = bf16[128,512]{1,0:T(8,128)(2,1)S(1)} collective-permute-done((bf16[128,512]{1,0:T(8,128)(2,1)S(1)}, bf16[128,512]{1,0:T(8,128)(2,1)S(1)}, u32[]{:S(2)}, u32[]{:S(2)}) %collective-permute-start.75) | collective-permute-done | bytes 131104 | tf_op jit(solution)/shard_map/ppermute | solution.py:31
  622.6 13.7 %collective-permute-done.78 = bf16[1,2,80,1024]{3,2,1,0:T(8,128)(2,1)S(1)} collective-permute-done((bf16[1,2,80,1024]{3,2,1,0:T(8,128)(2,1)S(1)}, bf16[1,2,80,1024]{3,2,1,0:T(8,128)(2,1)S(1)}, u32[]{:S(2)}, u32[]{:S(2)}) %collective-permute-start.78) | collective-permute-done | bytes 327712 | tf_op jit(solution)/shard_map/ppermute | solution.py:35
  656.3 10.8 %collective-permute-done.84 = bf16[1,2,32,2048]{3,2,1,0:T(8,128)(2,1)} collective-permute-done((bf16[1,2,32,2048]{3,2,1,0:T(8,128)(2,1)}, bf16[1,2,32,2048]{3,2,1,0:T(8,128)(2,1)}, u32[]{:S(2)}, u32[]{:S(2)}) %collective-permute-start.84) | collective-permute-done | bytes 262176 | tf_op jit(solution)/shard_map/ppermute | solution.py:35
  (868 shorter events, 461.5 us)
Async XLA Ops:
  7.2 93.0 %all-gather.10.cloned.1.call-start = ((), (), s32[]{:S(2)}) async-start(), calls=%async_computation | async-start | bytes 1310720 | tf_op jit(solution)/shard_map/all_gather | solution.py:497
  55.6 73.6 %all-gather.12.cloned.1.call-start = ((), (), s32[]{:S(2)}) async-start(), calls=%async_computation.1 | async-start | bytes 1638400 | tf_op jit(solution)/shard_map/all_gather | solution.py:497
  85.9 80.0 %all-gather.14.cloned.1.call-start = ((), (), s32[]{:S(2)}) async-start(), calls=%async_computation.2 | async-start | bytes 2293760 | tf_op jit(solution)/shard_map/all_gather | solution.py:497
  105.5 96.6 %all-gather.16.cloned.1.call-start = ((), (), s32[]{:S(2)}) async-start(), calls=%async_computation.3 | async-start | bytes 1638400 | tf_op jit(solution)/shard_map/all_gather | solution.py:497
  147.2 494.1 %all-gather.18.cloned.1.call-start = ((), (), s32[]{:S(2)}) async-start(), calls=%async_computation.4 | async-start | bytes 2949120 | tf_op jit(solution)/shard_map/all_gather | solution.py:534
  171.0 42.0 %collective-permute-start.25 = (bf16[2,3,32,3584]{3,2,1,0:T(8,128)(2,1)}, bf16[2,3,32,3584]{3,2,1,0:T(8,128)(2,1)}, u32[]{:S(2)}, u32[]{:S(2)}) collective-permute-start(bf16[2,3,32,3584]{3,2,1,0:T(8,128)(2,1)} %shard_map.230.n_ref), channel_id=1, source_target_pairs={{0,16},{16,0},{1,17},{17,1},{2,18},{18,2},{3,19},{19,3},{4,20},{20... | collective-permute-start | bytes 4128776 | tf_op jit(solution)/shard_map/ppermute | solution.py:27
  172.2 40.8 %collective-permute-start.24 = (bf16[2,3,32,3584]{3,2,1,0:T(8,128)(2,1)}, bf16[2,3,32,3584]{3,2,1,0:T(8,128)(2,1)S(1)}, u32[]{:S(2)}, u32[]{:S(2)}) collective-permute-start(bf16[2,3,32,3584]{3,2,1,0:T(8,128)(2,1)} %shard_map.230.n_ref), channel_id=1, source_target_pairs={{0,8},{8,0},{1,9},{9,1},{2,10},{10,2},{3,11},{11,3},{4,12},{12,4},... | collective-permute-start | bytes 4128776 | tf_op jit(solution)/shard_map/ppermute | solution.py:27
  216.2 37.0 %collective-permute-start.31 = (bf16[2,3,80,1024]{3,2,1,0:T(8,128)(2,1)S(1)}, bf16[2,3,80,1024]{3,2,1,0:T(8,128)(2,1)}, u32[]{:S(2)}, u32[]{:S(2)}) collective-permute-start(bf16[2,3,80,1024]{3,2,1,0:T(8,128)(2,1)S(1)} %shard_map.234.n_ref), channel_id=1, source_target_pairs={{0,16},{16,0},{1,17},{17,1},{2,18},{18,2},{3,19},{19,3},{4,20},{20... | collective-permute-start | bytes 2949128 | tf_op jit(solution)/shard_map/ppermute | solution.py:27
  217.6 35.6 %collective-permute-start.30 = (bf16[2,3,80,1024]{3,2,1,0:T(8,128)(2,1)S(1)}, bf16[2,3,80,1024]{3,2,1,0:T(8,128)(2,1)}, u32[]{:S(2)}, u32[]{:S(2)}) collective-permute-start(bf16[2,3,80,1024]{3,2,1,0:T(8,128)(2,1)S(1)} %shard_map.234.n_ref), channel_id=1, source_target_pairs={{0,8},{8,0},{1,9},{9,1},{2,10},{10,2},{3,11},{11,3},{4,12},{12,4},... | collective-permute-start | bytes 2949128 | tf_op jit(solution)/shard_map/ppermute | solution.py:27
  254.3 39.7 %collective-permute-start.36 = (bf16[3,80,1024]{2,1,0:T(8,128)(2,1)S(1)}, bf16[3,80,1024]{2,1,0:T(8,128)(2,1)S(1)}, u32[]{:S(2)}, u32[]{:S(2)}) collective-permute-start(bf16[3,80,1024]{2,1,0:T(8,128)(2,1)S(1)} %slice_bitcast_fusion.2), channel_id=1, source_target_pairs={{0,8},{8,0},{1,9},{9,1},{2,10},{10,2},{3,11},{11,3},{4,12},{12,4},... | collective-permute-start | bytes 1474568 | tf_op jit(solution)/shard_map/ppermute | solution.py:27
  256.9 38.0 %collective-permute-start.35 = (bf16[3,80,1024]{2,1,0:T(8,128)(2,1)S(1)}, bf16[3,80,1024]{2,1,0:T(8,128)(2,1)S(1)}, u32[]{:S(2)}, u32[]{:S(2)}) collective-permute-start(bf16[3,80,1024]{2,1,0:T(8,128)(2,1)S(1)} %slice_bitcast_fusion.3), channel_id=1, source_target_pairs={{0,16},{16,0},{1,17},{17,1},{2,18},{18,2},{3,19},{19,3},{4,20},{20... | collective-permute-start | bytes 1474568 | tf_op jit(solution)/shard_map/ppermute | solution.py:27
  261.5 34.2 %collective-permute-start.37 = (bf16[512,512]{1,0:T(8,128)(2,1)S(1)}, bf16[512,512]{1,0:T(8,128)(2,1)S(1)}, u32[]{:S(2)}, u32[]{:S(2)}) collective-permute-start(bf16[512,512]{1,0:T(8,128)(2,1)S(1)} %bitcast.279), channel_id=1, source_target_pairs={{0,4},{4,0},{1,5},{5,1},{2,6},{6,2},{3,7},{7,3},{8,12},{12,8},{9,1... | collective-permute-start | bytes 1572872 | tf_op jit(solution)/shard_map/ppermute | solution.py:27
  409.3 59.8 %collective-permute-start.62 = (bf16[512,1024]{1,0:T(8,128)(2,1)}, bf16[512,1024]{1,0:T(8,128)(2,1)}, u32[]{:S(2)}, u32[]{:S(2)}) collective-permute-start(bf16[512,1024]{1,0:T(8,128)(2,1)} %add_convert_fusion.1), channel_id=1, source_target_pairs={{0,4},{4,0},{1,5},{5,1},{2,6},{6,2},{3,7},{7,3},{8,12},{12,8},{9,1... | collective-permute-start | bytes 3145736 | tf_op jit(solution)/shard_map/ppermute | solution.py:27
  425.9 41.2 %collective-permute-start.54 = (bf16[2,4,80,1024]{3,2,1,0:T(8,128)(2,1)}, bf16[2,4,80,1024]{3,2,1,0:T(8,128)(2,1)}, u32[]{:S(2)}, u32[]{:S(2)}) collective-permute-start(bf16[2,4,80,1024]{3,2,1,0:T(8,128)(2,1)} %get-tuple-element.401), channel_id=1, source_target_pairs={{0,8},{8,0},{1,9},{9,1},{2,10},{10,2},{3,11},{11,3},{4,12},{12,4},... | collective-permute-start | bytes 3932168 | tf_op jit(solution)/shard_map/ppermute | solution.py:27
  426.7 40.4 %collective-permute-start.55 = (bf16[2,4,80,1024]{3,2,1,0:T(8,128)(2,1)}, bf16[2,4,80,1024]{3,2,1,0:T(8,128)(2,1)}, u32[]{:S(2)}, u32[]{:S(2)}) collective-permute-start(bf16[2,4,80,1024]{3,2,1,0:T(8,128)(2,1)} %get-tuple-element.402), channel_id=1, source_target_pairs={{0,16},{16,0},{1,17},{17,1},{2,18},{18,2},{3,19},{19,3},{4,20},{20... | collective-permute-start | bytes 3932168 | tf_op jit(solution)/shard_map/ppermute | solution.py:27
  469.0 187.3 %all-gather.22.cloned.1.call-start = ((), (), s32[]{:S(2)}) async-start(), calls=%async_computation.6 | async-start | bytes 2359296 | tf_op jit(solution)/shard_map/all_gather | solution.py:534
  477.8 50.0 %collective-permute-start.60 = (bf16[2,4,32,2048]{3,2,1,0:T(8,128)(2,1)}, bf16[2,4,32,2048]{3,2,1,0:T(8,128)(2,1)}, u32[]{:S(2)}, u32[]{:S(2)}) collective-permute-start(bf16[2,4,32,2048]{3,2,1,0:T(8,128)(2,1)} %get-tuple-element.418), channel_id=1, source_target_pairs={{0,8},{8,0},{1,9},{9,1},{2,10},{10,2},{3,11},{11,3},{4,12},{12,4},... | collective-permute-start | bytes 3145736 | tf_op jit(solution)/shard_map/ppermute | solution.py:27
  479.0 48.7 %collective-permute-start.61 = (bf16[2,4,32,2048]{3,2,1,0:T(8,128)(2,1)}, bf16[2,4,32,2048]{3,2,1,0:T(8,128)(2,1)}, u32[]{:S(2)}, u32[]{:S(2)}) collective-permute-start(bf16[2,4,32,2048]{3,2,1,0:T(8,128)(2,1)} %get-tuple-element.419), channel_id=1, source_target_pairs={{0,16},{16,0},{1,17},{17,1},{2,18},{18,2},{3,19},{19,3},{4,20},{20... | collective-permute-start | bytes 3145736 | tf_op jit(solution)/shard_map/ppermute | solution.py:27
  536.5 144.9 %all-gather.20.cloned.1.call-start = ((), (), s32[]{:S(2)}) async-start(), calls=%async_computation.5 | async-start | bytes 1769472 | tf_op jit(solution)/shard_map/all_gather | solution.py:534
  551.9 42.2 %collective-permute-start.67 = (bf16[2,2,80,1024]{3,2,1,0:T(8,128)(2,1)S(1)}, bf16[2,2,80,1024]{3,2,1,0:T(8,128)(2,1)S(1)}, u32[]{:S(2)}, u32[]{:S(2)}) collective-permute-start(bf16[2,2,80,1024]{3,2,1,0:T(8,128)(2,1)S(1)} %get-tuple-element.443), channel_id=1, source_target_pairs={{0,2},{1,3},{2,0},{3,1},{4,6},{5,7},{6,4},{7,5},{8,10},{9,11},{10,... | collective-permute-start | bytes 1966088 | tf_op jit(solution)/shard_map/ppermute | solution.py:35
  557.1 38.2 %collective-permute-start.71 = (bf16[2,4,32,1536]{3,2,1,0:T(8,128)(2,1)S(1)}, bf16[2,4,32,1536]{3,2,1,0:T(8,128)(2,1)S(1)}, u32[]{:S(2)}, u32[]{:S(2)}) collective-permute-start(bf16[2,4,32,1536]{3,2,1,0:T(8,128)(2,1)S(1)} %copy-done.213), channel_id=1, source_target_pairs={{0,8},{8,0},{1,9},{9,1},{2,10},{10,2},{3,11},{11,3},{4,12},{12,4},... | collective-permute-start | bytes 2359304 | tf_op jit(solution)/shard_map/ppermute | solution.py:27
  558.4 36.9 %collective-permute-start.72 = (bf16[2,4,32,1536]{3,2,1,0:T(8,128)(2,1)S(1)}, bf16[2,4,32,1536]{3,2,1,0:T(8,128)(2,1)S(1)}, u32[]{:S(2)}, u32[]{:S(2)}) collective-permute-start(bf16[2,4,32,1536]{3,2,1,0:T(8,128)(2,1)S(1)} %copy-done.212), channel_id=1, source_target_pairs={{0,16},{16,0},{1,17},{17,1},{2,18},{18,2},{3,19},{19,3},{4,20},{20... | collective-permute-start | bytes 2359304 | tf_op jit(solution)/shard_map/ppermute | solution.py:27
  606.3 83.5 %all-gather.24.cloned.1.call-start = ((), (), s32[]{:S(2)}) async-start(), calls=%async_computation.7 | async-start | bytes 2949120 | tf_op jit(solution)/shard_map/all_gather | solution.py:534
  642.2 59.1 %all-gather.26.cloned.1.call-start = ((), (), s32[]{:S(2)}) async-start(), calls=%async_computation.8 | async-start | bytes 2359296 | tf_op jit(solution)/shard_map/all_gather | solution.py:534
  (296 other events, 3306.2 us)
Sparse Core Ops, SparseCore 0:
  55.7 26.9 all-gather.9
  86.0 30.4 all-gather.11
  118.1 40.3 all-gather.13
  159.9 31.5 all-gather.15
  469.1 37.7 all-gather.17
  536.6 28.8 all-gather.21
  606.5 27.4 all-gather.19
  642.3 26.9 all-gather.23
  671.2 30.1 all-gather.25
